TPU v7x, 256 devices: a whole 4x4x8 slice. The times are simulated.
256 devices in a mesh: group: 32 (over z, y_hi, core), member: 8 (over y_lo, x).
Axes of the slice: x: 4, y: 4 (y_hi: 2, y_lo: 2; y = y_hi * 2 + y_lo), z: 8, core: 2. Of those that a mesh axis runs over, the one named last changes fastest.
Arguments:
- hidden_states: bfloat16 [32768, 4096], P(('group', 'member')), may hold values from -24 to 24
- queries: bfloat16 [32768, 2048], P(('group', 'member')), may hold values from -5 to 5
- local_keys: bfloat16 [32768, 2048], P(('group', 'member')), may hold values from -5 to 5
- local_values: bfloat16 [32768, 2048], P(('group', 'member')), may hold values from -6 to 6
- memory_keys: bfloat16 [16384, 2048], P(('group', 'member')), may hold values from -5 to 5
- memory_values: bfloat16 [16384, 2048], P(('group', 'member')), may hold values from -6 to 6
- grad_output: bfloat16 [32768, 2048], P(('group', 'member')), may hold values from -192 to 192
Outputs:
- grad_queries: bfloat16 [32768, 2048], P(('group', 'member'))
- grad_local_keys: bfloat16 [32768, 2048], P(('group', 'member'))
- grad_local_values: bfloat16 [32768, 2048], P(('group', 'member'))
- grad_memory_keys: bfloat16 [16384, 2048], P(('group', 'member'))
- grad_memory_values: bfloat16 [16384, 2048], P(('group', 'member'))
- grad_weight: float32 [4096, 2048], P(('group', 'member'))
All inputs are finite; a program needn't handle non-finite values.
Results may differ from a plain program's by a relative error of at most 0.024.
Values may be sent and summed in bfloat16 or wider, within the bound.
No kernel may reach another device: no remote copies, remote signals or barrier semaphores. Data moves between devices by JAX's collectives and lax.ppermute only.
A program may use at most 128 MiB of HBM per device.

v0:
```python
import jax
import jax.numpy as jnp
from jax import lax
from jax.sharding import PartitionSpec as P

HEADS = 16
HEAD_DIM = 128


def split_heads(matrix):
    return matrix.reshape(matrix.shape[0], HEADS, HEAD_DIM)


def transposed_product(left_rows, right_rows):
    return lax.dot_general(
        left_rows, right_rows, (((0,), (0,)), ((), ())), preferred_element_type=jnp.float32
    )


def local(
    hidden_states, queries, local_keys, local_values, memory_keys, memory_values, grad_output
):
    score_scale = HEAD_DIM ** (-0.5)
    row_count = queries.shape[0]
    inner_width = queries.shape[1]
    query_heads = split_heads(queries)
    grad_heads = split_heads(grad_output)
    local_key_heads = split_heads(local_keys)
    local_value_heads = split_heads(local_values)
    stacked_memory = jnp.concatenate((memory_keys, memory_values), axis=1)
    segment = lax.all_gather(stacked_memory, "member", axis=0, tiled=True)
    key_heads = split_heads(segment[:, :inner_width])
    value_heads = split_heads(segment[:, inner_width:])
    scores = (
        jnp.einsum("khd,qhd->khq", key_heads, query_heads, preferred_element_type=jnp.float32)
        * score_scale
    )
    prob_grad = jnp.einsum(
        "khd,qhd->khq", value_heads, grad_heads, preferred_element_type=jnp.float32
    )
    positions = jnp.arange(row_count)
    visible = positions[:, None, None] <= positions[None, None, :]
    local_raw = (
        jnp.einsum("khd,qhd->khq", local_key_heads, query_heads, preferred_element_type=jnp.float32)
        * score_scale
    )
    local_scores = jnp.where(visible, local_raw, -jnp.inf)
    local_prob_grad = jnp.einsum(
        "khd,qhd->khq", local_value_heads, grad_heads, preferred_element_type=jnp.float32
    )
    row_max = jnp.maximum(jnp.max(local_scores, axis=0), jnp.max(scores, axis=0))
    local_exp = jnp.exp(local_scores - row_max)
    memory_exp = jnp.exp(scores - row_max)
    denominator = jnp.sum(local_exp, axis=0) + jnp.sum(memory_exp, axis=0)
    local_prob = local_exp / denominator
    memory_prob = memory_exp / denominator
    delta_row = jnp.sum(local_prob * local_prob_grad, axis=0) + jnp.sum(
        memory_prob * prob_grad, axis=0
    )
    local_dscore = (local_prob * (local_prob_grad - delta_row)).astype(jnp.bfloat16)
    memory_dscore = (memory_prob * (prob_grad - delta_row)).astype(jnp.bfloat16)
    local_prob_low = local_prob.astype(jnp.bfloat16)
    memory_prob_low = memory_prob.astype(jnp.bfloat16)
    grad_query = score_scale * (
        jnp.einsum(
            "khq,khd->qhd", local_dscore, local_key_heads, preferred_element_type=jnp.float32
        )
        + jnp.einsum("khq,khd->qhd", memory_dscore, key_heads, preferred_element_type=jnp.float32)
    )
    grad_queries = grad_query.reshape(row_count, inner_width).astype(jnp.bfloat16)
    grad_local_keys = (
        (
            score_scale
            * jnp.einsum(
                "khq,qhd->khd", local_dscore, query_heads, preferred_element_type=jnp.float32
            )
        )
        .reshape(row_count, inner_width)
        .astype(jnp.bfloat16)
    )
    grad_local_values = (
        jnp.einsum("khq,qhd->khd", local_prob_low, grad_heads, preferred_element_type=jnp.float32)
        .reshape(row_count, inner_width)
        .astype(jnp.bfloat16)
    )
    row_total = memory_keys.shape[0] * lax.axis_size("member")
    key_term = score_scale * jnp.einsum(
        "khq,qhd->khd", memory_dscore, query_heads, preferred_element_type=jnp.float32
    )
    value_term = jnp.einsum(
        "khq,qhd->khd", memory_prob_low, grad_heads, preferred_element_type=jnp.float32
    )
    summed_memory = lax.psum_scatter(
        jnp.concatenate(
            (key_term.reshape(row_total, inner_width), value_term.reshape(row_total, inner_width)),
            axis=1,
        ).astype(jnp.bfloat16),
        "member",
        scatter_dimension=0,
        tiled=True,
    ).astype(jnp.float32)
    grad_memory_keys = summed_memory[:, :inner_width].astype(jnp.bfloat16)
    grad_memory_values = summed_memory[:, inner_width:].astype(jnp.bfloat16)
    groups = lax.axis_size("group")
    members = lax.axis_size("member")
    group_summed = lax.psum_scatter(
        transposed_product(hidden_states, grad_queries).astype(jnp.bfloat16),
        "group",
        scatter_dimension=0,
        tiled=True,
    )
    weight_summed = lax.psum_scatter(
        group_summed, "member", scatter_dimension=0, tiled=True
    ).astype(jnp.float32)
    grad_weight = weight_summed / (groups * members)
    return (
        grad_queries,
        grad_local_keys,
        grad_local_values,
        grad_memory_keys,
        grad_memory_values,
        grad_weight,
    )


def solution(mesh):
    in_specs = (
        P(("group", "member"), None),
        P(("group", "member"), None),
        P(("group", "member"), None),
        P(("group", "member"), None),
        P(("group", "member"), None),
        P(("group", "member"), None),
        P(("group", "member"), None),
    )
    out_specs = (
        P(("group", "member"), None),
        P(("group", "member"), None),
        P(("group", "member"), None),
        P(("group", "member"), None),
        P(("group", "member"), None),
        P(("group", "member"), None),
    )
    return jax.shard_map(local, mesh=mesh, in_specs=in_specs, out_specs=out_specs, check_vma=False)
```

profile of v0, /device:TPU:1, one launch (start us, length us, event | category | flops | bytes accessed | tf_op | source)
XLA Modules:
  0.0 444.0 jit_solution(5089751133250265297)
XLA Ops:
  7.2 1.9 pad_maximum_fusion.1
  10.6 1.5 copy.90
  12.1 2.2 copy.92
  14.3 1.4 fusion.27
  15.7 53.6 %all-gather.2.cloned.1.call-done = bf16[512,4096]{1,0:T(8,128)(2,1)} async-done(((bf16[64,4096]{1,0:T(8,128)(2,1)}), bf16[512,4096]{1,0:T(8,128)(2,1)}) %all-gather.2.cloned.1.call-update) | async-done | bytes 4194320 | tf_op jit(solution)/shard_map/all_gather | solution.py:31
  69.3 4.8 %fusion.25 = (bf16[512,2048]{1,0:T(8,128)(2,1)}, bf16[512,2048]{1,0:T(8,128)(2,1)}) fusion(bf16[512,4096]{1,0:T(8,128)(2,1)} %all-gather.2.cloned.1.call-done), kind=kLoop, calls=%fused_computation.40 | loop fusion | bytes 8388608 | tf_op jit(solution)/shard_map/slice | solution.py:33
  74.1 3.9 copy.87
  78.0 2.9 copy.86
  80.9 2.0 bitcast_reduce_fusion
  86.4 1.5 fusion
  91.6 8.1 %convert_bitcast_fusion = bf16[4096,2048]{0,1:T(8,128)(2,1)} fusion(bf16[128,2048]{0,1:T(8,128)(2,1)S(1)} %bitcast.99, bf16[128,4096]{1,0:T(8,128)(2,1)S(1)} %copy-done), kind=kOutput, calls=%fused_computation | convolution fusion | flops 2155872256 | bytes 18350080 | tf_op jit(solution)/shard_map/dot_general | solution.py:15
  99.7 22.6 %copy.82 = bf16[4096,2048]{1,0:T(8,128)(2,1)} copy(bf16[4096,2048]{0,1:T(8,128)(2,1)} %convert_bitcast_fusion) | data formatting | bytes 33554432
  122.5 1.3 copy-done.4
  123.9 2.0 fusion.11
  126.0 2.9 copy.69
  128.8 3.4 fusion.8
  132.3 2.2 pad_maximum_fusion
  134.5 6.6 %copy.80 = bf16[512,4096]{1,0:T(8,128)(2,1)} copy(bf16[512,4096]{0,1:T(8,128)(2,1)} %pad_maximum_fusion) | data formatting | bytes 8388608
  141.2 196.7 %reduce-scatter.12.cloned.1.call-done = bf16[128,2048]{1,0:T(8,128)(2,1)} async-done(((bf16[4096,2048]{1,0:T(8,128)(2,1)}), bf16[128,2048]{1,0:T(8,128)(2,1)}) %reduce-scatter.12.cloned.1.call-update) | async-done | bytes 524304
  339.0 2.4 convolution_convert_fusion
  341.4 2.0 copy.73
  344.9 53.9 %reduce-scatter.10.cloned.1.call-done = bf16[64,4096]{1,0:T(8,128)(2,1)} async-done(((bf16[512,4096]{1,0:T(8,128)(2,1)}), bf16[64,4096]{1,0:T(8,128)(2,1)}) %reduce-scatter.10.cloned.1.call-update) | async-done | bytes 524304
  398.8 1.9 fusion.26
  400.7 34.7 %reduce-scatter.14.cloned.1.call-done = bf16[16,2048]{1,0:T(8,128)(2,1)} async-done(((bf16[128,2048]{1,0:T(8,128)(2,1)}), bf16[16,2048]{1,0:T(8,128)(2,1)}) %reduce-scatter.14.cloned.1.call-update) | async-done | bytes 65552
  (65 shorter events, 13.6 us)
Async XLA Ops:
  7.2 84.5 %copy-start = (bf16[128,4096]{1,0:T(8,128)(2,1)S(1)}, bf16[128,4096]{1,0:T(8,128)(2,1)}, u32[]{:S(2)}) copy-start(bf16[128,4096]{1,0:T(8,128)(2,1)} %param.7) | copy-start | bytes 3145732
  7.2 62.1 %all-gather.2.cloned.1.call-start = ((), (), s32[]{:S(2)}) async-start(), calls=%async_computation.3 | async-start | bytes 4718592 | tf_op jit(solution)/shard_map/all_gather | solution.py:31
  9.2 328.7 %reduce-scatter.12.cloned.1.call-start = ((), (), s32[]{:S(2)}) async-start(), calls=%async_computation.5 | async-start | bytes 17301504
  10.6 63.6 %copy-start.5 = (bf16[128,2048]{0,1:T(8,128)(2,1)}, bf16[128,2048]{0,1:T(8,128)(2,1)S(1)}, u32[]{:S(2)}) copy-start(bf16[128,2048]{0,1:T(8,128)(2,1)S(1)} %copy.91) | copy-start | bytes 1572868
  12.1 62.0 %copy-start.14 = (bf16[128,2048]{0,1:T(8,128)(2,1)}, bf16[128,2048]{0,1:T(8,128)(2,1)S(1)}, u32[]{:S(2)}) copy-start(bf16[128,2048]{0,1:T(8,128)(2,1)S(1)} %copy.90) | copy-start | bytes 1572868
  80.9 2.8 copy-start.8
  82.9 4.9 %copy-start.2 = (f32[16,512,128]{2,1,0:T(8,128)}, f32[16,512,128]{2,1,0:T(8,128)S(1)}, u32[]{:S(2)}) copy-start(f32[16,512,128]{2,1,0:T(8,128)S(1)} %get-tuple-element.31) | copy-start | bytes 12582916
  83.0 1.4 copy-start.17
  83.0 1.9 copy-start.19
  83.7 2.7 copy-start.16
  89.1 1.7 copy-start.3
  89.1 1.4 copy-start.15
  89.4 1.5 copy-start.12
  90.8 0.8 copy-start.10
  122.3 1.6 copy-start.4
  122.3 1.7 copy-start.6
  122.3 6.5 %copy-start.18 = (bf16[128,2048]{0,1:T(8,128)(2,1)S(1)}, bf16[128,2048]{0,1:T(8,128)(2,1)}, u32[]{:S(2)}) copy-start(bf16[128,2048]{0,1:T(8,128)(2,1)} %copy.92) | copy-start | bytes 1572868
  122.3 276.5 %reduce-scatter.10.cloned.1.call-start = ((), (), s32[]{:S(2)}) async-start(), calls=%async_computation.4 | async-start | bytes 4718592
  141.1 196.8 %copy-start.11 = (bf16[128,16,128]{0,2,1:T(8,128)(2,1)S(1)}, bf16[128,16,128]{0,2,1:T(8,128)(2,1)}, u32[]{:S(2)}) copy-start(bf16[128,16,128]{0,2,1:T(8,128)(2,1)} %copy-done.10) | copy-start | bytes 1572868
  141.1 197.9 %copy-start.9 = (f32[128,16,128]{2,0,1:T(8,128)S(1)}, f32[128,16,128]{2,0,1:T(8,128)}, u32[]{:S(2)}) copy-start(f32[128,16,128]{2,0,1:T(8,128)} %get-tuple-element.29) | copy-start | bytes 3145732
  141.1 202.3 %copy-start.7 = (bf16[128,2048]{0,1:T(8,128)(2,1)S(1)}, bf16[128,2048]{0,1:T(8,128)(2,1)}, u32[]{:S(2)}) copy-start(bf16[128,2048]{0,1:T(8,128)(2,1)} %copy-done.5) | copy-start | bytes 1572868
  141.1 202.3 %copy-start.13 = (bf16[128,16,128]{2,0,1:T(8,128)(2,1)S(1)}, bf16[128,16,128]{2,0,1:T(8,128)(2,1)}, u32[]{:S(2)}) copy-start(bf16[128,16,128]{2,0,1:T(8,128)(2,1)} %copy-done.12) | copy-start | bytes 1572868
  141.1 294.2 %reduce-scatter.14.cloned.1.call-start = ((), (), s32[]{:S(2)}) async-start(), calls=%async_computation.6 | async-start | bytes 589824
  339.0 98.6 %copy-start.1 = (bf16[128,4096]{1,0:T(8,128)(2,1)S(1)}, bf16[128,4096]{1,0:T(8,128)(2,1)}, u32[]{:S(2)}) copy-start(bf16[128,4096]{1,0:T(8,128)(2,1)} %param.7) | copy-start | bytes 3145732
Sparse Core Ops, SparseCore 0:
  10.4 58.9 all-gather.1
  122.4 215.4 reduce-scatter.11
  340.6 58.1 reduce-scatter.9
  401.3 33.9 reduce-scatter.13
where the time goes:
time: 449 us; the launch traced here: 444 us
  waiting for transfers between devices  339 us (76%)
  local copies, waits for them, and re-layouts  61.3 us (14%)
  matrix products  22.7 us (5%)
  between operations  14.1 us (3%)
  other arithmetic  6.63 us (1%)
    unnamed x7, waiting for transfers between devices  285 us
    all_gather x1, waiting for transfers between devices, local(): segment = lax.all_gather(stacked_memory, 'member', axis=0, tiled=True)  53.6 us
    unnamed x49, local copies, waits for them, and re-layouts  46.8 us
  transfers between devices with their start and end apart: 4, of which 4 were waited for; matrix products, arithmetic and copies ran while one was open for 7% of the time, Pallas kernels for 0%

commit v1 on v0

v1 whole, which is shorter than its diff:
```python
import jax
import jax.numpy as jnp
from jax import lax
from jax.experimental import pallas as pl
from jax.experimental.pallas import tpu as pltpu
from jax.sharding import PartitionSpec as P

HEAD_DIM = 128
DOCS = 8
ROWS = 128
MEM = 64
WIDTH = 4096
INNER = 2048
BATCHES = 2
SPAN = 2 * HEAD_DIM // BATCHES
AXES = ("group", "member")
LOW = jnp.bfloat16
FULL = jnp.float32


def coords(i):
    g, m = divmod(i, 8)
    return {"z": g // 4, "yh": (g // 2) % 2, "c": g % 2, "yl": m // 4, "x": m % 4}


def index_of(d):
    return (d["z"] * 4 + d["yh"] * 2 + d["c"]) * 8 + d["yl"] * 4 + d["x"]


def pairs(key, size, step):
    out = []
    for i in range(256):
        d = coords(i)
        d[key] = (d[key] + step) % size
        out.append((i, index_of(d)))
    return out


X_GROUPS = [[0, 1, 2, 3], [4, 5, 6, 7]]
Z_GROUPS = [[z * 4 + r for z in range(8)] for r in range(4)]
Y_GROUPS = [
    [index_of({"z": z, "yh": y // 2, "c": c, "yl": y % 2, "x": x}) for y in range(4)]
    for z in range(8)
    for c in range(2)
    for x in range(4)
]


def dot(left, right, left_dim, right_dim):
    return lax.dot_general(
        left, right, (((left_dim,), (right_dim,)), ((), ())), preferred_element_type=FULL
    )


def pack_kernel(q_ref, g_ref, k_ref, v_ref, mk_ref, mv_ref, *outs):
    for j, out in enumerate(outs):
        cols = slice(j * SPAN, (j + 1) * SPAN)
        for n, ref in enumerate((q_ref, g_ref, k_ref, v_ref)):
            out[0, n * ROWS : (n + 1) * ROWS, :] = ref[:, cols]
        out[0, 4 * ROWS : 4 * ROWS + MEM, :] = mk_ref[:, cols]
        out[0, 4 * ROWS + MEM :, :] = mv_ref[:, cols]


def pack(q, g, k, v, mk, mv):
    tall = pl.BlockSpec((ROWS, 256), lambda i: (0, i))
    short = pl.BlockSpec((MEM, 256), lambda i: (0, i))
    return pl.pallas_call(
        pack_kernel,
        grid=(DOCS,),
        in_specs=[tall] * 4 + [short] * 2,
        out_specs=[pl.BlockSpec((1, 640, SPAN), lambda i: (i, 0, 0))] * BATCHES,
        out_shape=[jax.ShapeDtypeStruct((DOCS, 640, SPAN), LOW)] * BATCHES,
        cost_estimate=pl.CostEstimate(flops=0, bytes_accessed=5 << 20, transcendentals=0),
        name="pack_heads",
    )(q, g, k, v, mk, mv)


def hidden_kernel(h_ref, out_ref, perm):
    @pl.when(pl.program_id(0) == 0)
    def _():
        src = lax.broadcasted_iota(jnp.int32, (1024, 1024), 0)
        dst = lax.broadcasted_iota(jnp.int32, (1024, 1024), 1)
        x, c, zl = dst >> 8, (dst >> 7) & 1, (dst >> 6) & 1
        yh, yl, i = (dst >> 5) & 1, (dst >> 4) & 1, dst & 15
        want = (zl << 9) | (yh << 8) | (c << 7) | (yl << 6) | (x << 4) | i
        perm[...] = jnp.where(src == want, 1.0, 0.0).astype(LOW)

    moved = jnp.dot(h_ref[...], perm[...], preferred_element_type=FULL).astype(LOW)
    for x in range(4):
        for c in range(2):
            lane = x * 256 + c * 128
            out_ref[x, c, :, :] = moved[:, lane : lane + 128]


def hidden_pieces(hidden):
    return pl.pallas_call(
        hidden_kernel,
        grid=(4,),
        in_specs=[pl.BlockSpec((ROWS, 1024), lambda t: (0, t))],
        out_specs=pl.BlockSpec((4, 2, ROWS, 128), lambda t: (0, 0, 0, t)),
        out_shape=jax.ShapeDtypeStruct((4, 2, ROWS, 512), LOW),
        scratch_shapes=[pltpu.VMEM((1024, 1024), LOW)],
        compiler_params=pltpu.CompilerParams(vmem_limit_bytes=32 << 20),
        cost_estimate=pl.CostEstimate(flops=1 << 30, bytes_accessed=2 << 20, transcendentals=0),
        name="pack_hidden",
    )(hidden)


def attention_kernel(doc_ref, mk_ref, mv_ref, out_ref, gq_ref, dk_acc, dv_acc):
    doc = pl.program_id(1)
    scale = HEAD_DIM**-0.5
    q = doc_ref[0, 0:ROWS, :]
    g = doc_ref[0, ROWS : 2 * ROWS, :]
    k = doc_ref[0, 2 * ROWS : 3 * ROWS, :]
    v = doc_ref[0, 3 * ROWS : 4 * ROWS, :]
    mk = mk_ref[...].reshape(DOCS * MEM, HEAD_DIM)
    mv = mv_ref[...].reshape(DOCS * MEM, HEAD_DIM)
    key_at = lax.broadcasted_iota(jnp.int32, (ROWS, ROWS), 0)
    query_at = lax.broadcasted_iota(jnp.int32, (ROWS, ROWS), 1)
    s_loc = jnp.where(key_at <= query_at, dot(k, q, 1, 1) * scale, -jnp.inf)
    s_mem = dot(mk, q, 1, 1) * scale
    dp_loc = dot(v, g, 1, 1)
    dp_mem = dot(mv, g, 1, 1)
    top = jnp.maximum(
        jnp.max(s_loc, axis=0, keepdims=True), jnp.max(s_mem, axis=0, keepdims=True)
    )
    e_loc = jnp.exp(s_loc - top)
    e_mem = jnp.exp(s_mem - top)
    total = jnp.sum(e_loc, axis=0, keepdims=True) + jnp.sum(e_mem, axis=0, keepdims=True)
    inverse = 1.0 / total
    p_loc = e_loc * inverse
    p_mem = e_mem * inverse
    delta = jnp.sum(p_loc * dp_loc, axis=0, keepdims=True) + jnp.sum(
        p_mem * dp_mem, axis=0, keepdims=True
    )
    ds_loc = (p_loc * (dp_loc - delta)).astype(LOW)
    ds_mem = (p_mem * (dp_mem - delta)).astype(LOW)
    gq = (scale * (dot(ds_loc, k, 0, 0) + dot(ds_mem, mk, 0, 0))).astype(LOW)
    gq_ref[doc] = gq
    out_ref[doc, 0:ROWS, :] = gq
    out_ref[doc, ROWS : 2 * ROWS, :] = (scale * dot(ds_loc, q, 1, 0)).astype(LOW)
    out_ref[doc, 2 * ROWS : 3 * ROWS, :] = dot(p_loc.astype(LOW), g, 1, 0).astype(LOW)
    dk = scale * dot(ds_mem, q, 1, 0)
    dv = dot(p_mem.astype(LOW), g, 1, 0)

    @pl.when(doc == 0)
    def _():
        dk_acc[...] = dk
        dv_acc[...] = dv

    @pl.when(doc > 0)
    def _():
        dk_acc[...] += dk
        dv_acc[...] += dv

    @pl.when(doc == DOCS - 1)
    def _():
        out_ref[:, 3 * ROWS : 3 * ROWS + MEM, :] = (
            dk_acc[...].reshape(DOCS, MEM, HEAD_DIM).astype(LOW)
        )
        out_ref[:, 3 * ROWS + MEM :, :] = dv_acc[...].reshape(DOCS, MEM, HEAD_DIM).astype(LOW)


def attention(received):
    return pl.pallas_call(
        attention_kernel,
        grid=(SPAN // HEAD_DIM, DOCS),
        in_specs=[
            pl.BlockSpec((1, 512, HEAD_DIM), lambda h, d: (d, 0, h)),
            pl.BlockSpec((DOCS, MEM, HEAD_DIM), lambda h, d: (0, 8, h)),
            pl.BlockSpec((DOCS, MEM, HEAD_DIM), lambda h, d: (0, 9, h)),
        ],
        out_specs=[
            pl.BlockSpec((DOCS, 512, HEAD_DIM), lambda h, d: (0, 0, h)),
            pl.BlockSpec((DOCS, ROWS, HEAD_DIM), lambda h, d: (0, 0, h)),
        ],
        out_shape=[
            jax.ShapeDtypeStruct((DOCS, 512, SPAN), LOW),
            jax.ShapeDtypeStruct((DOCS, ROWS, SPAN), LOW),
        ],
        scratch_shapes=[pltpu.VMEM((DOCS * MEM, HEAD_DIM), FULL)] * 2,
        compiler_params=pltpu.CompilerParams(vmem_limit_bytes=32 << 20),
        cost_estimate=pl.CostEstimate(
            flops=int(3.4e9) // BATCHES, bytes_accessed=(5 << 20) // BATCHES, transcendentals=1 << 20
        ),
        name="attention_backward",
    )(received, received, received)


def product_kernel(place, own_ref, other_ref, *refs):
    pieces, (send_ref, keep_ref) = refs[:-2], refs[-2:]
    yl = place[1]
    for n, piece in enumerate(pieces):
        cols = slice(n * SPAN, (n + 1) * SPAN)
        near = piece[pl.ds(pl.multiple_of(yl * 4, 4), 4)].reshape(512, SPAN)
        far = piece[pl.ds(pl.multiple_of(4 - yl * 4, 4), 4)].reshape(512, SPAN)
        part = dot(own_ref[...].reshape(512, 512), near, 0, 0)
        part = part + dot(other_ref[...].reshape(512, 512), far, 0, 0)

        @pl.when(pl.program_id(0) == 0)
        def _():
            send_ref[:, cols] = part.astype(LOW)

        @pl.when(pl.program_id(0) == 1)
        def _():
            keep_ref[:, cols] = part.astype(LOW)


def product(place, own, other, pieces):
    half = pl.BlockSpec((4, None, ROWS, 512), lambda i, s: (0, (1 - s[0]) * (1 - i) + s[0] * i, 0, 0))
    whole = pl.BlockSpec((DOCS, ROWS, SPAN), lambda i, s: (0, 0, 0))
    out = pl.BlockSpec((512, 4 * SPAN), lambda i, s: (0, 0))
    return pl.pallas_call(
        product_kernel,
        grid_spec=pltpu.PrefetchScalarGridSpec(
            num_scalar_prefetch=1,
            grid=(2,),
            in_specs=[half, half] + [whole] * 4,
            out_specs=[out, out],
        ),
        out_shape=[jax.ShapeDtypeStruct((512, 4 * SPAN), LOW)] * 2,
        compiler_params=pltpu.CompilerParams(vmem_limit_bytes=32 << 20),
        cost_estimate=pl.CostEstimate(
            flops=int(2.1e9) // BATCHES, bytes_accessed=6 << 20, transcendentals=0
        ),
        name="weight_product",
    )(place, own, other, *pieces)


def unpack_kernel(*refs):
    ins, outs = refs[:BATCHES], refs[BATCHES:]
    for j, ref in enumerate(ins):
        cols = slice(j * SPAN, (j + 1) * SPAN)
        for n in range(3):
            outs[n][:, cols] = ref[0, n * ROWS : (n + 1) * ROWS, :]
        outs[3][:, cols] = ref[0, 3 * ROWS : 3 * ROWS + MEM, :]
        outs[4][:, cols] = ref[0, 3 * ROWS + MEM :, :]


def unpack(returned):
    tall = pl.BlockSpec((ROWS, 256), lambda i: (0, i))
    short = pl.BlockSpec((MEM, 256), lambda i: (0, i))
    return pl.pallas_call(
        unpack_kernel,
        grid=(DOCS,),
        in_specs=[pl.BlockSpec((1, 512, SPAN), lambda i: (i, 0, 0))] * BATCHES,
        out_specs=[tall] * 3 + [short] * 2,
        out_shape=[jax.ShapeDtypeStruct((ROWS, INNER), LOW)] * 3
        + [jax.ShapeDtypeStruct((MEM, INNER), LOW)] * 2,
        cost_estimate=pl.CostEstimate(flops=0, bytes_accessed=4 << 20, transcendentals=0),
        name="unpack_heads",
    )(*returned)


def local(
    hidden_states, queries, local_keys, local_values, memory_keys, memory_values, grad_output
):
    core = lax.rem(lax.axis_index("group"), 2)
    member = lax.axis_index("member")
    yl, x = member // 4, lax.rem(member, 4)
    place = jnp.stack((core, yl)).astype(jnp.int32)

    sends = pack(queries, grad_output, local_keys, local_values, memory_keys, memory_values)
    hidden = hidden_pieces(hidden_states)
    arrived = [lax.all_to_all(s, "member", 0, 0, tiled=True) for s in sends]
    own = lax.all_to_all(hidden, "member", 0, 0, axis_index_groups=X_GROUPS, tiled=True)
    other = lax.ppermute(own, AXES, pairs("yl", 2, 1))

    returned = []
    summed = []
    for block in arrived:
        grads, gq = attention(block)
        returned.append(lax.all_to_all(grads, "member", 0, 0, tiled=True))
        pieces = [gq] + [lax.ppermute(gq, AXES, pairs("x", 4, k)) for k in (1, 2, 3)]
        send, keep = product(place, own, other, pieces)
        swapped = lax.ppermute(send, AXES, pairs("c", 2, 1))
        both = (keep.astype(FULL) + swapped.astype(FULL)).astype(LOW).reshape(8, 64, 4 * SPAN)
        along_z = lax.all_to_all(both, "group", 0, 0, axis_index_groups=Z_GROUPS, tiled=True)
        z_sum = jnp.sum(along_z.astype(FULL), axis=0).astype(LOW).reshape(4, 16, 4 * SPAN)
        along_y = lax.all_to_all(z_sum, AXES, 0, 0, axis_index_groups=Y_GROUPS, tiled=True)
        y_sum = along_y[:2].astype(FULL) + along_y[2:].astype(FULL)
        summed.append(y_sum.reshape(2, 16, 4, SPAN))
    weight = jnp.concatenate(summed, axis=3) * (1.0 / 256)
    order = lax.rem(x - jnp.arange(4) + 4, 4)
    weight = jnp.take(weight, order, axis=2)
    grad_weight = jnp.transpose(weight, (1, 0, 2, 3)).reshape(16, INNER)
    gq, glk, glv, gmk, gmv = unpack(returned)
    return gq, glk, glv, gmk, gmv, grad_weight


def solution(mesh):
    spec = P(("group", "member"), None)
    return jax.shard_map(
        local, mesh=mesh, in_specs=(spec,) * 7, out_specs=(spec,) * 6, check_vma=False
    )
```

time: 449 us -> 188 us (0.42)
  waiting for transfers between devices: 339 us -> 57.4 us
  local copies, waits for them, and re-layouts: 61.3 us -> 3.56 us
  starting transfers between devices: 0.34 us -> 56.9 us
  Pallas kernels: 0 us -> 44.5 us
  matrix products: 22.7 us -> 0 us
  blocking collectives: 0 us -> 20.3 us
  between operations: 14.1 us -> 0.77 us
    unnamed x7 -> x0, waiting for transfers between devices: 285 us -> none
    all_to_all x0 -> x8, waiting for transfers between devices: none -> 55.7 us  [the longest x2 21.3 us: local(): lax.all_to_all(both, 'group', 0, 0, axis_index_groups=Z_GROUPS, tiled=True)]
    all_gather x1 -> x0, waiting for transfers between devices: 53.6 us -> none  [local(): segment = lax.all_gather(stacked_memory, 'member', axis=0, tiled=True)]
    unnamed x49 -> x8, local copies, waits for them, and re-layouts: 46.8 us -> 2.19 us
    pallas_call x0 -> x7, Pallas kernels: none -> 44.5 us  [the longest x2 15 us: product(): pl.pallas_call(product_kernel, grid_spec=pltpu.PrefetchScalarGridSpec(num...]
    all_to_all x0 -> x8, starting transfers between devices: none -> 42.2 us  [the longest x2 15 us: local(): lax.all_to_all(both, 'group', 0, 0, axis_index_groups=Z_GROUPS, tiled=True)]
    dot_general x11 -> x0, matrix products: 22.7 us -> none  [the longest x1 8.06 us: transposed_product(): lax.dot_general(left_rows, right_rows, (((0,), (0,)), ((), ())), preferre...]
    all_to_all x0 -> x1, blocking collectives: none -> 20.3 us  [local(): arrived = [lax.all_to_all(s, 'member', 0, 0, tiled=True) for s in sends]]
  transfers between devices with their start and end apart: 4 -> 17, of which waited for: 4 -> 9; matrix products, arithmetic and copies ran while one was open for 7% -> 2% of each run, Pallas kernels for 0% -> 22%
where the time goes in v1:
time: 188 us; the launch traced here: 187 us
  waiting for transfers between devices  57.4 us (31%)
  starting transfers between devices  56.9 us (30%)
  Pallas kernels  44.5 us (24%)
  blocking collectives  20.3 us (11%)
  local copies, waits for them, and re-layouts  3.56 us (2%)
  other arithmetic  3.47 us (2%)
    all_to_all x2, waiting for transfers between devices, local(): lax.all_to_all(both, 'group', 0, 0, axis_index_groups=Z_GROUPS, tiled=True)  21.3 us
    all_to_all x1, blocking collectives, local(): arrived = [lax.all_to_all(s, 'member', 0, 0, tiled=True) for s in sends]  20.3 us
    pallas_call x2, Pallas kernels, product(): pl.pallas_call(product_kernel, grid_spec=pltpu.PrefetchScalarGridSpec(num...  15 us
    all_to_all x2, starting transfers between devices, local(): lax.all_to_all(both, 'group', 0, 0, axis_index_groups=Z_GROUPS, tiled=True)  15 us
    pallas_call x2, Pallas kernels, attention(): pl.pallas_call(attention_kernel, grid=(SPAN // HEAD_DIM, DOCS), in_specs=...  14.5 us
    all_to_all x2, waiting for transfers between devices, local(): returned.append(lax.all_to_all(grads, 'member', 0, 0, tiled=True))  13.1 us
    all_to_all x2, starting transfers between devices, local(): returned.append(lax.all_to_all(grads, 'member', 0, 0, tiled=True))  10.4 us
    ppermute x6, starting transfers between devices, local(): lax.ppermute(gq, AXES, pairs('x', 4, k))  10.2 us
  transfers between devices with their start and end apart: 17, of which 9 were waited for; matrix products, arithmetic and copies ran while one was open for 2% of the time, Pallas kernels for 22%

profile of v1, /device:TPU:1, one launch (start us, length us, event | category | flops | bytes accessed | tf_op | source)
XLA Modules:
  0.0 187.0 jit_solution(7803166468951219003)
XLA Ops:
  1.9 3.3 %pack_hidden.1 = bf16[4,2,128,512]{3,2,1,0:T(8,128)(2,1)} custom-call(bf16[128,4096]{1,0:T(8,128)(2,1)S(1)} %copy-done.3), custom_call_target="tpu_custom_call" | custom-call | flops 1073741824 | bytes 2097152 | tf_op jit(solution)/shard_map/pack_hidden/pallas_call | solution.py:96
  5.2 4.8 %all-to-all-start.4 = ((bf16[4,2,128,512]{3,2,1,0:T(8,128)(2,1)}), bf16[4,2,128,512]{3,2,1,0:T(8,128)(2,1)S(1)}, u32[]{:S(2)}, u32[]{:S(2)}) async-start(bf16[4,2,128,512]{3,2,1,0:T(8,128)(2,1)} %pack_hidden.1), calls=%async_computation.4 | async-start | bytes 2097152 | tf_op jit(solution)/shard_map/all_to_all | solution.py:266
  10.0 6.0 %pack_heads.1 = (bf16[8,640,128]{2,1,0:T(8,128)(2,1)}, bf16[8,640,128]{2,1,0:T(8,128)(2,1)}) custom-call(bf16[128,2048]{1,0:T(8,128)(2,1)} %q_ref.1, bf16[128,2048]{1,0:T(8,128)(2,1)} %g_ref.1, bf16[128,2048]{1,0:T(8,128)(2,1)} %k_ref.1, bf16[128,2048]{1,0:T(8,128)(2,1)} %v_ref.1, bf16[64,2048]{1,0:T(8,128)(2,1)} %mk_ref.1, bf16[64,2048]{1,0:T(8,128)(2,1)} %mv_ref.1), custom_call_target="tpu_custom_call" | custom-call | bytes 5242880 | tf_op jit(solution)/shard_map/pack_heads/pallas_call | solution.py:67
  16.0 7.3 %all-to-all-done.4.own_ref = bf16[4,2,128,512]{3,2,1,0:T(8,128)(2,1)S(1)} async-done(((bf16[4,2,128,512]{3,2,1,0:T(8,128)(2,1)}), bf16[4,2,128,512]{3,2,1,0:T(8,128)(2,1)S(1)}, u32[]{:S(2)}, u32[]{:S(2)}) %all-to-all-start.4) | async-done | bytes 1048608 | tf_op jit(solution)/shard_map/all_to_all | solution.py:266
  23.3 20.3 %all_to_all.45.doc_ref.mk_ref.mv_ref = bf16[8,640,128]{2,1,0:T(8,128)(2,1)S(1)} all-to-all(bf16[8,640,128]{2,1,0:T(8,128)(2,1)} %get-tuple-element.21), channel_id=1, replica_groups=mesh['group'=32,'member'=8] {'member'}, dimensions={0} | all-to-all | bytes 2621440 | tf_op jit(solution)/shard_map/all_to_all | solution.py:265
  43.6 3.6 %all-to-all-start.2 = ((bf16[8,640,128]{2,1,0:T(8,128)(2,1)}), bf16[8,640,128]{2,1,0:T(8,128)(2,1)S(1)}, u32[]{:S(2)}, u32[]{:S(2)}) async-start(bf16[8,640,128]{2,1,0:T(8,128)(2,1)} %get-tuple-element.23), calls=%async_computation.2 | async-start | bytes 2621440 | tf_op jit(solution)/shard_map/all_to_all | solution.py:265
  48.6 6.7 %attention_backward.2 = (bf16[8,512,128]{2,1,0:T(8,128)(2,1)S(1)}, bf16[8,128,128]{2,1,0:T(8,128)(2,1)S(1)}) custom-call(bf16[8,640,128]{2,1,0:T(8,128)(2,1)S(1)} %all_to_all.45.doc_ref.mk_ref.mv_ref, bf16[8,640,128]{2,1,0:T(8,128)(2,1)S(1)} %all_to_all.45.doc_ref.mk_ref.mv_ref, bf16[8,640,128]{2,1,0:T(8,128)(2,1)S(1)} %all_to_all.45.doc_ref.mk_ref.mv_ref), custom_call_target="tpu_custom_call" | custom-call | flops 1700000000 | bytes 2621440 | tf_op jit(solution)/shard_map/attention_backward/pallas_call | solution.py:165
  56.3 9.5 %all-to-all-done.2.doc_ref.mk_ref.mv_ref = bf16[8,640,128]{2,1,0:T(8,128)(2,1)S(1)} async-done(((bf16[8,640,128]{2,1,0:T(8,128)(2,1)}), bf16[8,640,128]{2,1,0:T(8,128)(2,1)S(1)}, u32[]{:S(2)}, u32[]{:S(2)}) %all-to-all-start.2) | async-done | bytes 1310752 | tf_op jit(solution)/shard_map/all_to_all | solution.py:265
  65.8 4.2 %all-to-all-start.1 = ((bf16[8,512,128]{2,1,0:T(8,128)(2,1)}), bf16[8,512,128]{2,1,0:T(8,128)(2,1)}, u32[]{:S(2)}, u32[]{:S(2)}) async-start(bf16[8,512,128]{2,1,0:T(8,128)(2,1)} %copy-done.2), calls=%async_computation.1 | async-start | bytes 2097152 | tf_op jit(solution)/shard_map/all_to_all | solution.py:273
  70.0 7.7 %attention_backward.3 = (bf16[8,512,128]{2,1,0:T(8,128)(2,1)}, bf16[8,128,128]{2,1,0:T(8,128)(2,1)S(1)}) custom-call(bf16[8,640,128]{2,1,0:T(8,128)(2,1)S(1)} %all-to-all-done.2.doc_ref.mk_ref.mv_ref, bf16[8,640,128]{2,1,0:T(8,128)(2,1)S(1)} %all-to-all-done.2.doc_ref.mk_ref.mv_ref, bf16[8,640,128]{2,1,0:T(8,128)(2,1)S(1)} %all-to-all-done.2.doc_ref.mk_ref.mv_ref), custom_call_target="tpu_custom_call" | custom-call | flops 1700000000 | bytes 2621440 | tf_op jit(solution)/shard_map/attention_backward/pallas_call | solution.py:165
  79.0 2.4 %collective-permute-start.6 = (bf16[8,128,128]{2,1,0:T(8,128)(2,1)S(1)}, bf16[8,128,128]{2,1,0:T(8,128)(2,1)S(1)}, u32[]{:S(2)}, u32[]{:S(2)}) collective-permute-start(bf16[8,128,128]{2,1,0:T(8,128)(2,1)S(1)} %get-tuple-element.33.refs_0_), channel_id=1, source_target_pairs={{0,2},{1,3},{2,0},{3,1},{4,6},{5,7},{6,4},{7,5},{8,10},{9,11},{10,... | collective-permute-start | bytes 786440 | tf_op jit(solution)/shard_map/ppermute | solution.py:274
  82.6 12.4 %all-to-all-done.1.refs_0_ = bf16[8,512,128]{2,1,0:T(8,128)(2,1)} async-done(((bf16[8,512,128]{2,1,0:T(8,128)(2,1)}), bf16[8,512,128]{2,1,0:T(8,128)(2,1)}, u32[]{:S(2)}, u32[]{:S(2)}) %all-to-all-start.1) | async-done | bytes 1048608 | tf_op jit(solution)/shard_map/all_to_all | solution.py:273
  95.1 6.2 %all-to-all-start.3 = ((bf16[8,512,128]{2,1,0:T(8,128)(2,1)}), bf16[8,512,128]{2,1,0:T(8,128)(2,1)}, u32[]{:S(2)}, u32[]{:S(2)}) async-start(bf16[8,512,128]{2,1,0:T(8,128)(2,1)} %get-tuple-element.24), calls=%async_computation.3 | async-start | bytes 2097152 | tf_op jit(solution)/shard_map/all_to_all | solution.py:273
  101.3 7.5 %weight_product.3 = (bf16[512,512]{1,0:T(8,128)(2,1)S(1)}, bf16[512,512]{1,0:T(8,128)(2,1)S(1)}) custom-call(s32[2]{0:T(128)S(1)} %pad_add_fusion.place, bf16[4,2,128,512]{3,2,1,0:T(8,128)(2,1)S(1)} %copy-done.1, bf16[4,2,128,512]{3,2,1,0:T(8,128)(2,1)} %collective-permute-done.other_ref, bf16[8,128,128]{2,1,0:T(8,128)(2,1)S(1)} %get-tuple-element.33.refs_0_, ...), custom_call_target="tpu_custom_call" | custom-call | flops 1050000000 | bytes 6291456 | tf_op jit(solution)/shard_map/weight_product/pallas_call | solution.py:213
  112.0 2.4 %collective-permute-start.2 = (bf16[8,128,128]{2,1,0:T(8,128)(2,1)S(1)}, bf16[8,128,128]{2,1,0:T(8,128)(2,1)S(1)}, u32[]{:S(2)}, u32[]{:S(2)}) collective-permute-start(bf16[8,128,128]{2,1,0:T(8,128)(2,1)S(1)} %get-tuple-element.30.refs_0_), channel_id=1, source_target_pairs={{0,2},{1,3},{2,0},{3,1},{4,6},{5,7},{6,4},{7,5},{8,10},{9,11},{10,... | collective-permute-start | bytes 786440 | tf_op jit(solution)/shard_map/ppermute | solution.py:274
  117.1 9.5 %all-to-all-start.7 = ((bf16[8,64,512]{2,1,0:T(8,128)(2,1)}), bf16[8,64,512]{2,1,0:T(8,128)(2,1)S(1)}, u32[]{:S(2)}, u32[]{:S(2)}) async-start(bf16[8,64,512]{2,1,0:T(8,128)(2,1)} %bitcast.4), calls=%async_computation.7 | async-start | bytes 1048576 | tf_op jit(solution)/shard_map/all_to_all | solution.py:278
  126.9 7.5 %weight_product.2 = (bf16[512,512]{1,0:T(8,128)(2,1)S(1)}, bf16[512,512]{1,0:T(8,128)(2,1)S(1)}) custom-call(s32[2]{0:T(128)S(1)} %pad_add_fusion.place, bf16[4,2,128,512]{3,2,1,0:T(8,128)(2,1)S(1)} %copy-done.1, bf16[4,2,128,512]{3,2,1,0:T(8,128)(2,1)} %collective-permute-done.other_ref, bf16[8,128,128]{2,1,0:T(8,128)(2,1)S(1)} %get-tuple-element.30.refs_0_, ...), custom_call_target="tpu_custom_call" | custom-call | flops 1050000000 | bytes 6291456 | tf_op jit(solution)/shard_map/weight_product/pallas_call | solution.py:213
  138.6 4.1 %all-to-all-done.7 = bf16[8,64,512]{2,1,0:T(8,128)(2,1)S(1)} async-done(((bf16[8,64,512]{2,1,0:T(8,128)(2,1)}), bf16[8,64,512]{2,1,0:T(8,128)(2,1)S(1)}, u32[]{:S(2)}, u32[]{:S(2)}) %all-to-all-start.7) | async-done | bytes 524320 | tf_op jit(solution)/shard_map/all_to_all | solution.py:278
  142.7 5.4 %all-to-all-start.5 = ((bf16[8,64,512]{2,1,0:T(8,128)(2,1)}), bf16[8,64,512]{2,1,0:T(8,128)(2,1)S(1)}, u32[]{:S(2)}, u32[]{:S(2)}) async-start(bf16[8,64,512]{2,1,0:T(8,128)(2,1)} %bitcast.2), calls=%async_computation.5 | async-start | bytes 1048576 | tf_op jit(solution)/shard_map/all_to_all | solution.py:278
  148.9 17.2 %all-to-all-done.5 = bf16[8,64,512]{2,1,0:T(8,128)(2,1)S(1)} async-done(((bf16[8,64,512]{2,1,0:T(8,128)(2,1)}), bf16[8,64,512]{2,1,0:T(8,128)(2,1)S(1)}, u32[]{:S(2)}, u32[]{:S(2)}) %all-to-all-start.5) | async-done | bytes 524320 | tf_op jit(solution)/shard_map/all_to_all | solution.py:278
  166.1 4.2 %all-to-all-start.8 = ((bf16[4,16,512]{2,1,0:T(8,128)(2,1)}), bf16[4,16,512]{2,1,0:T(8,128)(2,1)S(1)}, u32[]{:S(2)}, u32[]{:S(2)}) async-start(bf16[4,16,512]{2,1,0:T(8,128)(2,1)} %bitcast.5), calls=%async_computation.8 | async-start | bytes 131072 | tf_op jit(solution)/shard_map/all_to_all | solution.py:280
  170.3 5.8 %unpack_heads.1 = (bf16[128,2048]{1,0:T(8,128)(2,1)}, bf16[128,2048]{1,0:T(8,128)(2,1)}, bf16[128,2048]{1,0:T(8,128)(2,1)}, bf16[64,2048]{1,0:T(8,128)(2,1)}, bf16[64,2048]{1,0:T(8,128)(2,1)}) custom-call(bf16[8,512,128]{2,1,0:T(8,128)(2,1)} %all-to-all-done.1.refs_0_, bf16[8,512,128]{2,1,0:T(8,128)(2,1)} %all-to-all-done.3.refs_1_), custom_call_target="tpu_custom_call" | custom-call | bytes 4194304 | tf_op jit(solution)/shard_map/unpack_heads/pallas_call | solution.py:243
  176.8 4.2 %all-to-all-start.6 = ((bf16[4,16,512]{2,1,0:T(8,128)(2,1)}), bf16[4,16,512]{2,1,0:T(8,128)(2,1)S(1)}, u32[]{:S(2)}, u32[]{:S(2)}) async-start(bf16[4,16,512]{2,1,0:T(8,128)(2,1)} %bitcast.3), calls=%async_computation.6 | async-start | bytes 131072 | tf_op jit(solution)/shard_map/all_to_all | solution.py:280
  181.1 4.5 %all-to-all-done.6 = bf16[4,16,512]{2,1,0:T(8,128)(2,1)S(1)} async-done(((bf16[4,16,512]{2,1,0:T(8,128)(2,1)}), bf16[4,16,512]{2,1,0:T(8,128)(2,1)S(1)}, u32[]{:S(2)}, u32[]{:S(2)}) %all-to-all-start.6) | async-done | bytes 65568 | tf_op jit(solution)/shard_map/all_to_all | solution.py:280
  (41 shorter events, 19.4 us)
Async XLA Ops:
  0.6 1.2 copy-start.3
  5.2 18.1 %all-to-all-start.4 = ((bf16[4,2,128,512]{3,2,1,0:T(8,128)(2,1)}), bf16[4,2,128,512]{3,2,1,0:T(8,128)(2,1)S(1)}, u32[]{:S(2)}, u32[]{:S(2)}) async-start(bf16[4,2,128,512]{3,2,1,0:T(8,128)(2,1)} %pack_hidden.1), calls=%async_computation.4 | async-start | bytes 2097152 | tf_op jit(solution)/shard_map/all_to_all | solution.py:266
  23.3 20.3 %copy-start = (bf16[4,2,128,512]{3,2,1,0:T(8,128)(2,1)}, bf16[4,2,128,512]{3,2,1,0:T(8,128)(2,1)S(1)}, u32[]{:S(2)}) copy-start(bf16[4,2,128,512]{3,2,1,0:T(8,128)(2,1)S(1)} %all-to-all-done.4.own_ref) | copy-start | bytes 3145732
  43.6 22.1 %all-to-all-start.2 = ((bf16[8,640,128]{2,1,0:T(8,128)(2,1)}), bf16[8,640,128]{2,1,0:T(8,128)(2,1)S(1)}, u32[]{:S(2)}, u32[]{:S(2)}) async-start(bf16[8,640,128]{2,1,0:T(8,128)(2,1)} %get-tuple-element.23), calls=%async_computation.2 | async-start | bytes 2621440 | tf_op jit(solution)/shard_map/all_to_all | solution.py:265
  47.2 54.1 %collective-permute-start = (bf16[4,2,128,512]{3,2,1,0:T(8,128)(2,1)}, bf16[4,2,128,512]{3,2,1,0:T(8,128)(2,1)}, u32[]{:S(2)}, u32[]{:S(2)}) collective-permute-start(bf16[4,2,128,512]{3,2,1,0:T(8,128)(2,1)} %copy-done), channel_id=1, source_target_pairs={{0,4},{1,5},{2,6},{3,7},{4,0},{5,1},{6,2},{7,3},{8,12},{9,13},{10,... | collective-permute-start | bytes 3145736 | tf_op jit(solution)/shard_map/ppermute | solution.py:267
  55.3 1.0 copy-start.2
  65.8 29.3 %all-to-all-start.1 = ((bf16[8,512,128]{2,1,0:T(8,128)(2,1)}), bf16[8,512,128]{2,1,0:T(8,128)(2,1)}, u32[]{:S(2)}, u32[]{:S(2)}) async-start(bf16[8,512,128]{2,1,0:T(8,128)(2,1)} %copy-done.2), calls=%async_computation.1 | async-start | bytes 2097152 | tf_op jit(solution)/shard_map/all_to_all | solution.py:273
  77.7 23.6 %copy-start.1 = (bf16[4,2,128,512]{3,2,1,0:T(8,128)(2,1)S(1)}, bf16[4,2,128,512]{3,2,1,0:T(8,128)(2,1)}, u32[]{:S(2)}) copy-start(bf16[4,2,128,512]{3,2,1,0:T(8,128)(2,1)} %copy-done) | copy-start | bytes 3145732
  77.7 23.6 %collective-permute-start.5 = (bf16[8,128,128]{2,1,0:T(8,128)(2,1)S(1)}, bf16[8,128,128]{2,1,0:T(8,128)(2,1)S(1)}, u32[]{:S(2)}, u32[]{:S(2)}) collective-permute-start(bf16[8,128,128]{2,1,0:T(8,128)(2,1)S(1)} %get-tuple-element.33.refs_0_), channel_id=1, source_target_pairs={{0,1},{1,2},{2,3},{3,0},{4,5},{5,6},{6,7},{7,4},{8,9},{9,10},{10,1... | collective-permute-start | bytes 786440 | tf_op jit(solution)/shard_map/ppermute | solution.py:274
  79.0 22.3 %collective-permute-start.6 = (bf16[8,128,128]{2,1,0:T(8,128)(2,1)S(1)}, bf16[8,128,128]{2,1,0:T(8,128)(2,1)S(1)}, u32[]{:S(2)}, u32[]{:S(2)}) collective-permute-start(bf16[8,128,128]{2,1,0:T(8,128)(2,1)S(1)} %get-tuple-element.33.refs_0_), channel_id=1, source_target_pairs={{0,2},{1,3},{2,0},{3,1},{4,6},{5,7},{6,4},{7,5},{8,10},{9,11},{10,... | collective-permute-start | bytes 786440 | tf_op jit(solution)/shard_map/ppermute | solution.py:274
  81.5 19.9 %collective-permute-start.7 = (bf16[8,128,128]{2,1,0:T(8,128)(2,1)S(1)}, bf16[8,128,128]{2,1,0:T(8,128)(2,1)S(1)}, u32[]{:S(2)}, u32[]{:S(2)}) collective-permute-start(bf16[8,128,128]{2,1,0:T(8,128)(2,1)S(1)} %get-tuple-element.33.refs_0_), channel_id=1, source_target_pairs={{0,3},{1,0},{2,1},{3,2},{4,7},{5,4},{6,5},{7,6},{8,11},{9,8},{10,9... | collective-permute-start | bytes 786440 | tf_op jit(solution)/shard_map/ppermute | solution.py:274
  95.1 22.1 %all-to-all-start.3 = ((bf16[8,512,128]{2,1,0:T(8,128)(2,1)}), bf16[8,512,128]{2,1,0:T(8,128)(2,1)}, u32[]{:S(2)}, u32[]{:S(2)}) async-start(bf16[8,512,128]{2,1,0:T(8,128)(2,1)} %get-tuple-element.24), calls=%async_computation.3 | async-start | bytes 2097152 | tf_op jit(solution)/shard_map/all_to_all | solution.py:273
  108.8 6.7 %collective-permute-start.8 = (bf16[512,512]{1,0:T(8,128)(2,1)S(1)}, bf16[512,512]{1,0:T(8,128)(2,1)S(1)}, u32[]{:S(2)}, u32[]{:S(2)}) collective-permute-start(bf16[512,512]{1,0:T(8,128)(2,1)S(1)} %get-tuple-element.35), channel_id=1, source_target_pairs={{0,8},{1,9},{2,10},{3,11},{4,12},{5,13},{6,14},{7,15},{8,0},{9,1},... | collective-permute-start | bytes 1572872 | tf_op jit(solution)/shard_map/ppermute | solution.py:276
  110.2 16.5 %collective-permute-start.1 = (bf16[8,128,128]{2,1,0:T(8,128)(2,1)S(1)}, bf16[8,128,128]{2,1,0:T(8,128)(2,1)S(1)}, u32[]{:S(2)}, u32[]{:S(2)}) collective-permute-start(bf16[8,128,128]{2,1,0:T(8,128)(2,1)S(1)} %get-tuple-element.30.refs_0_), channel_id=1, source_target_pairs={{0,1},{1,2},{2,3},{3,0},{4,5},{5,6},{6,7},{7,4},{8,9},{9,10},{10,1... | collective-permute-start | bytes 786440 | tf_op jit(solution)/shard_map/ppermute | solution.py:274
  112.0 14.9 %collective-permute-start.2 = (bf16[8,128,128]{2,1,0:T(8,128)(2,1)S(1)}, bf16[8,128,128]{2,1,0:T(8,128)(2,1)S(1)}, u32[]{:S(2)}, u32[]{:S(2)}) collective-permute-start(bf16[8,128,128]{2,1,0:T(8,128)(2,1)S(1)} %get-tuple-element.30.refs_0_), channel_id=1, source_target_pairs={{0,2},{1,3},{2,0},{3,1},{4,6},{5,7},{6,4},{7,5},{8,10},{9,11},{10,... | collective-permute-start | bytes 786440 | tf_op jit(solution)/shard_map/ppermute | solution.py:274
  114.4 12.5 %collective-permute-start.3 = (bf16[8,128,128]{2,1,0:T(8,128)(2,1)S(1)}, bf16[8,128,128]{2,1,0:T(8,128)(2,1)S(1)}, u32[]{:S(2)}, u32[]{:S(2)}) collective-permute-start(bf16[8,128,128]{2,1,0:T(8,128)(2,1)S(1)} %get-tuple-element.30.refs_0_), channel_id=1, source_target_pairs={{0,3},{1,0},{2,1},{3,2},{4,7},{5,4},{6,5},{7,6},{8,11},{9,8},{10,9... | collective-permute-start | bytes 786440 | tf_op jit(solution)/shard_map/ppermute | solution.py:274
  117.1 25.6 %all-to-all-start.7 = ((bf16[8,64,512]{2,1,0:T(8,128)(2,1)}), bf16[8,64,512]{2,1,0:T(8,128)(2,1)S(1)}, u32[]{:S(2)}, u32[]{:S(2)}) async-start(bf16[8,64,512]{2,1,0:T(8,128)(2,1)} %bitcast.4), calls=%async_computation.7 | async-start | bytes 1048576 | tf_op jit(solution)/shard_map/all_to_all | solution.py:278
  134.4 3.3 %collective-permute-start.4 = (bf16[512,512]{1,0:T(8,128)(2,1)S(1)}, bf16[512,512]{1,0:T(8,128)(2,1)S(1)}, u32[]{:S(2)}, u32[]{:S(2)}) collective-permute-start(bf16[512,512]{1,0:T(8,128)(2,1)S(1)} %get-tuple-element.32), channel_id=1, source_target_pairs={{0,8},{1,9},{2,10},{3,11},{4,12},{5,13},{6,14},{7,15},{8,0},{9,1},... | collective-permute-start | bytes 1572872 | tf_op jit(solution)/shard_map/ppermute | solution.py:276
  142.7 23.4 %all-to-all-start.5 = ((bf16[8,64,512]{2,1,0:T(8,128)(2,1)}), bf16[8,64,512]{2,1,0:T(8,128)(2,1)S(1)}, u32[]{:S(2)}, u32[]{:S(2)}) async-start(bf16[8,64,512]{2,1,0:T(8,128)(2,1)} %bitcast.2), calls=%async_computation.5 | async-start | bytes 1048576 | tf_op jit(solution)/shard_map/all_to_all | solution.py:278
  166.1 10.7 %all-to-all-start.8 = ((bf16[4,16,512]{2,1,0:T(8,128)(2,1)}), bf16[4,16,512]{2,1,0:T(8,128)(2,1)S(1)}, u32[]{:S(2)}, u32[]{:S(2)}) async-start(bf16[4,16,512]{2,1,0:T(8,128)(2,1)} %bitcast.5), calls=%async_computation.8 | async-start | bytes 131072 | tf_op jit(solution)/shard_map/all_to_all | solution.py:280
  176.8 8.7 %all-to-all-start.6 = ((bf16[4,16,512]{2,1,0:T(8,128)(2,1)}), bf16[4,16,512]{2,1,0:T(8,128)(2,1)S(1)}, u32[]{:S(2)}, u32[]{:S(2)}) async-start(bf16[4,16,512]{2,1,0:T(8,128)(2,1)} %bitcast.3), calls=%async_computation.6 | async-start | bytes 131072 | tf_op jit(solution)/shard_map/all_to_all | solution.py:280

commit v2 on v1

v2 whole, which is shorter than its diff:
```python
import jax
import jax.numpy as jnp
from jax import lax
from jax.experimental import pallas as pl
from jax.experimental.pallas import tpu as pltpu
from jax.sharding import PartitionSpec as P

HEAD_DIM = 128
DOCS = 8
ROWS = 128
MEM = 64
WIDTH = 4096
INNER = 2048
SPAN = 2 * HEAD_DIM
AXES = ("group", "member")
LOW = jnp.bfloat16
FULL = jnp.float32


def coords(i):
    g, m = divmod(i, 8)
    return {"z": g // 4, "yh": (g // 2) % 2, "c": g % 2, "yl": m // 4, "x": m % 4}


def index_of(d):
    return (d["z"] * 4 + d["yh"] * 2 + d["c"]) * 8 + d["yl"] * 4 + d["x"]


def pairs(key, size, step):
    out = []
    for i in range(256):
        d = coords(i)
        d[key] = (d[key] + step) % size
        out.append((i, index_of(d)))
    return out


ZY_GROUPS = [
    [
        index_of({"z": z, "yh": yh, "c": c, "yl": yl, "x": x})
        for z in range(8)
        for yh in range(2)
        for yl in range(2)
    ]
    for c in range(2)
    for x in range(4)
]
ANY = pl.BlockSpec(memory_space=pl.ANY)
VMEM = pl.BlockSpec(memory_space=pltpu.VMEM)
SMEM = pl.BlockSpec(memory_space=pltpu.SMEM)


def shift(array, key, size, step):
    return lax.ppermute(array, AXES, pairs(key, size, step))


def dot(left, right, left_dim, right_dim):
    return lax.dot_general(
        left, right, (((left_dim,), (right_dim,)), ((), ())), preferred_element_type=FULL
    )


def pack_kernel(q_ref, g_ref, k_ref, v_ref, mk_ref, mv_ref, out):
    for m in range(4):
        cols = slice(m * SPAN, (m + 1) * SPAN)
        for n, ref in enumerate((q_ref, g_ref, k_ref, v_ref)):
            out[m, n * ROWS : (n + 1) * ROWS, :] = ref[:, cols]
        out[m, 4 * ROWS : 4 * ROWS + MEM, :] = mk_ref[:, cols]
        out[m, 4 * ROWS + MEM :, :] = mv_ref[:, cols]


def pack(q, g, k, v, mk, mv):
    tall = pl.BlockSpec((ROWS, 4 * SPAN), lambda i: (0, i))
    short = pl.BlockSpec((MEM, 4 * SPAN), lambda i: (0, i))
    return pl.pallas_call(
        pack_kernel,
        grid=(2,),
        in_specs=[tall] * 4 + [short] * 2,
        out_specs=pl.BlockSpec((4, 640, SPAN), lambda i: (i, 0, 0)),
        out_shape=jax.ShapeDtypeStruct((DOCS, 640, SPAN), LOW),
        cost_estimate=pl.CostEstimate(flops=0, bytes_accessed=5 << 20, transcendentals=0),
        name="pack_heads",
    )(q, g, k, v, mk, mv)


def hidden_kernel(place, h_ref, _, *refs):
    outs, perm = refs[:4], refs[4]
    dst = lax.broadcasted_iota(jnp.int32, (1024, 1), 0)
    src = lax.broadcasted_iota(jnp.int32, (1024, 1024), 1)
    x, c, zl = ((dst >> 8) + place[3]) & 3, (dst >> 7) & 1, (dst >> 6) & 1
    yh, yl, i = (dst >> 5) & 1, (dst >> 4) & 1, dst & 15
    want = (zl << 9) | (yh << 8) | (c << 7) | (yl << 6) | (x << 4) | i
    perm[...] = jnp.where(src == want, 1.0, 0.0).astype(LOW)
    for t in range(4):
        moved = dot(perm[...], h_ref[:, t * 1024 : (t + 1) * 1024], 1, 1).astype(LOW)
        for k, out in enumerate(outs):
            for c in range(2):
                row = k * 256 + c * 128
                out[c, t * 128 : (t + 1) * 128, :] = moved[row : row + 128, :]


def hidden_pieces(place, hidden, after):
    return pl.pallas_call(
        hidden_kernel,
        in_specs=[SMEM, VMEM, ANY],
        out_specs=[VMEM] * 4,
        out_shape=[jax.ShapeDtypeStruct((2, 512, ROWS), LOW)] * 4,
        scratch_shapes=[pltpu.VMEM((1024, 1024), LOW)],
        compiler_params=pltpu.CompilerParams(vmem_limit_bytes=24 << 20),
        cost_estimate=pl.CostEstimate(flops=1 << 30, bytes_accessed=2 << 20, transcendentals=0),
        name="pack_hidden",
    )(place, hidden, after)


def gate_kernel(*refs):
    pass


def gate(arrays, after):
    count = len(arrays)
    return pl.pallas_call(
        gate_kernel,
        in_specs=[ANY] * (count + 1),
        out_specs=[ANY] * count,
        out_shape=[jax.ShapeDtypeStruct(a.shape, a.dtype) for a in arrays],
        input_output_aliases={n: n for n in range(count)},
        compiler_params=pltpu.CompilerParams(vmem_limit_bytes=1 << 20),
        name="gate",
    )(*arrays, after)


def attention_kernel(place, doc_ref, mk_ref, mv_ref, *refs):
    outs = list(refs[:4]) + [refs[4].at[n] for n in range(4)]
    gq_ref, dk_acc, dv_acc = refs[5:]
    me = place[2]
    scale = HEAD_DIM**-0.5
    mk = mk_ref[...].reshape(DOCS * MEM, HEAD_DIM)
    mv = mv_ref[...].reshape(DOCS * MEM, HEAD_DIM)
    key_at = lax.broadcasted_iota(jnp.int32, (ROWS, ROWS), 0)
    query_at = lax.broadcasted_iota(jnp.int32, (ROWS, ROWS), 1)
    visible = key_at <= query_at
    for step in range(DOCS // 2):
        docs = [me ^ (2 * step), me ^ (2 * step + 1)]
        q = [doc_ref[d, 0:ROWS, :] for d in docs]
        g = [doc_ref[d, ROWS : 2 * ROWS, :] for d in docs]
        k = [doc_ref[d, 2 * ROWS : 3 * ROWS, :] for d in docs]
        v = [doc_ref[d, 3 * ROWS : 4 * ROWS, :] for d in docs]
        both_q = jnp.concatenate(q, axis=0)
        both_g = jnp.concatenate(g, axis=0)
        s_loc = jnp.concatenate(
            [jnp.where(visible, dot(k[n], q[n], 1, 1) * scale, -jnp.inf) for n in range(2)],
            axis=1,
        )
        dp_loc = jnp.concatenate([dot(v[n], g[n], 1, 1) for n in range(2)], axis=1)
        s_mem = dot(mk, both_q, 1, 1) * scale
        dp_mem = dot(mv, both_g, 1, 1)
        top = jnp.maximum(
            jnp.max(s_loc, axis=0, keepdims=True), jnp.max(s_mem, axis=0, keepdims=True)
        )
        e_loc = jnp.exp(s_loc - top)
        e_mem = jnp.exp(s_mem - top)
        total = jnp.sum(e_loc, axis=0, keepdims=True) + jnp.sum(e_mem, axis=0, keepdims=True)
        inverse = 1.0 / total
        p_loc = e_loc * inverse
        p_mem = e_mem * inverse
        delta = jnp.sum(p_loc * dp_loc, axis=0, keepdims=True) + jnp.sum(
            p_mem * dp_mem, axis=0, keepdims=True
        )
        ds_loc = (p_loc * (dp_loc - delta)).astype(LOW)
        ds_mem = (p_mem * (dp_mem - delta)).astype(LOW)
        low_loc = p_loc.astype(LOW)
        gq_mem = dot(ds_mem, mk, 0, 0)
        for n in range(2):
            rows = slice(n * ROWS, (n + 1) * ROWS)
            mine = ds_loc[:, rows]
            gq = (scale * (dot(mine, k[n], 0, 0) + gq_mem[rows, :])).astype(LOW)
            gq_ref[docs[n]] = gq
            out = outs[2 * step + n]
            out[0:ROWS, :] = gq
            out[ROWS : 2 * ROWS, :] = (scale * dot(mine, q[n], 1, 0)).astype(LOW)
            out[2 * ROWS : 3 * ROWS, :] = dot(low_loc[:, rows], g[n], 1, 0).astype(LOW)
        dk = scale * dot(ds_mem, both_q, 1, 0)
        dv = dot(p_mem.astype(LOW), both_g, 1, 0)
        if step == 0:
            dk_acc[...] = dk.reshape(DOCS, MEM, HEAD_DIM)
            dv_acc[...] = dv.reshape(DOCS, MEM, HEAD_DIM)
        else:
            dk_acc[...] += dk.reshape(DOCS, MEM, HEAD_DIM)
            dv_acc[...] += dv.reshape(DOCS, MEM, HEAD_DIM)
    for n, out in enumerate(outs):
        out[3 * ROWS : 3 * ROWS + MEM, :] = dk_acc[me ^ n].astype(LOW)
        out[3 * ROWS + MEM :, :] = dv_acc[me ^ n].astype(LOW)


def attention(place, received):
    return pl.pallas_call(
        attention_kernel,
        grid_spec=pltpu.PrefetchScalarGridSpec(
            num_scalar_prefetch=1,
            grid=(2,),
            in_specs=[
                pl.BlockSpec((DOCS, 512, HEAD_DIM), lambda h, s: (0, 0, h)),
                pl.BlockSpec((DOCS, MEM, HEAD_DIM), lambda h, s: (0, 8, h)),
                pl.BlockSpec((DOCS, MEM, HEAD_DIM), lambda h, s: (0, 9, h)),
            ],
            out_specs=[pl.BlockSpec((512, HEAD_DIM), lambda h, s: (0, h))] * 4
            + [
                pl.BlockSpec((4, 512, HEAD_DIM), lambda h, s: (0, 0, h)),
                pl.BlockSpec((DOCS, ROWS, HEAD_DIM), lambda h, s: (0, 0, h)),
            ],
            scratch_shapes=[pltpu.VMEM((DOCS, MEM, HEAD_DIM), FULL)] * 2,
        ),
        out_shape=[jax.ShapeDtypeStruct((512, SPAN), LOW)] * 4
        + [
            jax.ShapeDtypeStruct((4, 512, SPAN), LOW),
            jax.ShapeDtypeStruct((DOCS, ROWS, SPAN), LOW),
        ],
        compiler_params=pltpu.CompilerParams(vmem_limit_bytes=24 << 20),
        cost_estimate=pl.CostEstimate(
            flops=int(8e9), bytes_accessed=5 << 20, transcendentals=2 << 20
        ),
        name="attention_backward",
    )(place, received, received, received)


def product_kernel(place, *refs):
    near, far, pieces, (give_ref, keep_ref) = refs[:4], refs[4:8], refs[8:12], refs[12:]
    yl, x = place[1], place[3]
    mine = [yl * 4 + ((x + 4 - k) & 3) for k in range(4)]
    docs = mine + [d ^ 4 for d in mine]
    for out, half in ((give_ref, 1 - place[0]), (keep_ref, place[0])):
        left = jnp.concatenate([ref[half] for ref in near + far], axis=1)
        for n, piece in enumerate(pieces):
            right = jnp.concatenate([piece[d] for d in docs], axis=0)
            out[:, n * SPAN : (n + 1) * SPAN] = dot(left, right, 1, 0).astype(LOW)


def product(place, near, far, pieces):
    return pl.pallas_call(
        product_kernel,
        in_specs=[SMEM] + [VMEM] * 12,
        out_specs=[VMEM] * 2,
        out_shape=[jax.ShapeDtypeStruct((512, 4 * SPAN), LOW)] * 2,
        compiler_params=pltpu.CompilerParams(vmem_limit_bytes=24 << 20),
        cost_estimate=pl.CostEstimate(flops=int(2.1e9), bytes_accessed=6 << 20, transcendentals=0),
        name="weight_product",
    )(place, *near, *far, *pieces)


def merge(keep, swapped, carried):
    count = len(carried)

    def kernel(a_ref, b_ref, *refs):
        refs[count][...] = (a_ref[...].astype(FULL) + b_ref[...].astype(FULL)).astype(LOW)

    return pl.pallas_call(
        kernel,
        in_specs=[VMEM] * 2 + [ANY] * count,
        out_specs=[VMEM] + [ANY] * count,
        out_shape=[jax.ShapeDtypeStruct(a.shape, LOW) for a in (keep, *carried)],
        input_output_aliases={2 + n: 1 + n for n in range(count)},
        compiler_params=pltpu.CompilerParams(vmem_limit_bytes=16 << 20),
        cost_estimate=pl.CostEstimate(flops=1 << 20, bytes_accessed=3 << 20, transcendentals=0),
        name="core_sum",
    )(keep, swapped, *carried)


def unpack_kernel(place, *refs):
    ins, outs = refs[:DOCS], refs[DOCS:]
    for n, ref in enumerate(ins):
        lane = pl.multiple_of((place[2] ^ n) * SPAN, SPAN)
        row = 0
        for out in outs:
            height = out.shape[0]
            out[:, pl.ds(lane, SPAN)] = ref[row : row + height, :]
            row += height


def unpack(place, returned):
    return pl.pallas_call(
        unpack_kernel,
        in_specs=[SMEM] + [VMEM] * DOCS,
        out_specs=[VMEM] * 5,
        out_shape=[jax.ShapeDtypeStruct((ROWS, INNER), LOW)] * 3
        + [jax.ShapeDtypeStruct((MEM, INNER), LOW)] * 2,
        compiler_params=pltpu.CompilerParams(vmem_limit_bytes=16 << 20),
        cost_estimate=pl.CostEstimate(flops=0, bytes_accessed=4 << 20, transcendentals=0),
        name="unpack_heads",
    )(place, *returned)


def finish_kernel(place, in_ref, out_ref):
    for y in range(2):
        total = in_ref[y].astype(FULL)
        for n in range(1, 16):
            total = total + in_ref[2 * n + y].astype(FULL)
        total = total * (1.0 / 256)
        for k in range(4):
            slot = (place[3] + 4 - k) & 3
            lane = pl.multiple_of(y * 1024 + slot * SPAN, SPAN)
            out_ref[:, pl.ds(lane, SPAN)] = total[:, k * SPAN : (k + 1) * SPAN]


def finish(place, along):
    return pl.pallas_call(
        finish_kernel,
        in_specs=[SMEM, VMEM],
        out_specs=VMEM,
        out_shape=jax.ShapeDtypeStruct((16, INNER), FULL),
        compiler_params=pltpu.CompilerParams(vmem_limit_bytes=16 << 20),
        cost_estimate=pl.CostEstimate(flops=1 << 20, bytes_accessed=1 << 20, transcendentals=0),
        name="weight_sum",
    )(place, along)


def local(
    hidden_states, queries, local_keys, local_values, memory_keys, memory_values, grad_output
):
    core = lax.rem(lax.axis_index("group"), 2)
    member = lax.axis_index("member")
    place = jnp.stack((core, member // 4, member, lax.rem(member, 4))).astype(jnp.int32)

    send = pack(queries, grad_output, local_keys, local_values, memory_keys, memory_values)
    arrived = lax.all_to_all(send, "member", 0, 0, tiled=True)
    hidden = gate(hidden_pieces(place, hidden_states, send), arrived)
    near = [hidden[0]] + [shift(hidden[k], "x", 4, k) for k in (1, 2, 3)]
    far = [shift(piece, "yl", 2, 1) for piece in near]
    *grads, grads_far, gq = attention(place, arrived)
    pieces = [gq] + [shift(gq, "x", 4, k) for k in (1, 2, 3)]
    grads_far = shift(grads_far, "yl", 2, 1)
    give, keep = product(place, near, far, pieces)
    swapped = shift(give, "c", 2, 1)
    both, *grads, grads_far = merge(keep, swapped, [*grads, grads_far])
    along = lax.all_to_all(
        both.reshape(32, 16, 4 * SPAN), AXES, 0, 0, axis_index_groups=ZY_GROUPS, tiled=True
    )
    returned = grads + [grads_far[k] for k in range(4)]
    returned = [
        lax.ppermute(piece, "member", [(i, i ^ (n & 3)) for i in range(DOCS)]) if n & 3 else piece
        for n, piece in enumerate(returned)
    ]
    gq_out, glk, glv, gmk, gmv = unpack(place, returned)
    grad_weight = finish(place, along)
    return gq_out, glk, glv, gmk, gmv, grad_weight


def solution(mesh):
    spec = P(("group", "member"), None)
    return jax.shard_map(
        local, mesh=mesh, in_specs=(spec,) * 7, out_specs=(spec,) * 6, check_vma=False
    )
```

time: 188 us -> 144 us (0.77)
  Pallas kernels: 44.5 us -> 23.5 us
  blocking collectives: 20.3 us -> 0 us
  starting transfers between devices: 56.9 us -> 36.9 us
  waiting for transfers between devices: 57.4 us -> 76.7 us
  other arithmetic: 3.47 us -> 0.08 us
    ppermute x9 -> x18, waiting for transfers between devices: 1.78 us -> 50.9 us  [the longest x12 31.4 us: shift(): return lax.ppermute(array, AXES, pairs(key, size, step))]
    all_to_all x8 -> x2, waiting for transfers between devices: 55.7 us -> 25.8 us  [the longest x1 25.8 us: local(): arrived = lax.all_to_all(send, 'member', 0, 0, tiled=True)]
    all_to_all x8 -> x2, starting transfers between devices: 42.2 us -> 16.8 us  [the longest x1 10.9 us: local(): lax.all_to_all(both.reshape(32, 16, 4 * SPAN), AXES, 0, 0, axis_index_gro...]
    pallas_call x7 -> x8, Pallas kernels: 44.5 us -> 23.5 us  [the longest x1 9.18 us: attention(): pl.pallas_call(attention_kernel, grid_spec=pltpu.PrefetchScalarGridSpec(n...]
    all_to_all x1 -> x0, blocking collectives: 20.3 us -> none  [local(): arrived = [lax.all_to_all(s, 'member', 0, 0, tiled=True) for s in sends]]
    ppermute x9 -> x18, starting transfers between devices: 14.7 us -> 20.1 us  [the longest x12 13.5 us: shift(): return lax.ppermute(array, AXES, pairs(key, size, step))]
    unnamed x8 -> x10, local copies, waits for them, and re-layouts: 2.19 us -> 5.07 us
  transfers between devices with their start and end apart: 17 -> 20, of which waited for: 9 -> 10; matrix products, arithmetic and copies ran while one was open for 2% -> 0% of each run, Pallas kernels for 22% -> 13%
where the time goes in v2:
time: 144 us; the launch traced here: 143 us
  waiting for transfers between devices  76.7 us (53%)
  starting transfers between devices  36.9 us (26%)
  Pallas kernels  23.5 us (16%)
  local copies, waits for them, and re-layouts  5.14 us (4%)
    ppermute x12, waiting for transfers between devices, shift(): return lax.ppermute(array, AXES, pairs(key, size, step))  31.4 us
    all_to_all x1, waiting for transfers between devices, local(): arrived = lax.all_to_all(send, 'member', 0, 0, tiled=True)  25.8 us
    ppermute x6, waiting for transfers between devices, local(): lax.ppermute(piece, 'member', [(i, i ^ n & 3) for i in range(DOCS)])  19.6 us
    ppermute x12, starting transfers between devices, shift(): return lax.ppermute(array, AXES, pairs(key, size, step))  13.5 us
    all_to_all x1, starting transfers between devices, local(): lax.all_to_all(both.reshape(32, 16, 4 * SPAN), AXES, 0, 0, axis_index_gro...  10.9 us
    pallas_call x1, Pallas kernels, attention(): pl.pallas_call(attention_kernel, grid_spec=pltpu.PrefetchScalarGridSpec(n...  9.18 us
    ppermute x6, starting transfers between devices, local(): lax.ppermute(piece, 'member', [(i, i ^ n & 3) for i in range(DOCS)])  6.54 us
    all_to_all x1, starting transfers between devices, local(): arrived = lax.all_to_all(send, 'member', 0, 0, tiled=True)  5.86 us
  transfers between devices with their start and end apart: 20, of which 10 were waited for; matrix products, arithmetic and copies ran while one was open for 0% of the time, Pallas kernels for 13%

profile of v2, /device:TPU:1, one launch (start us, length us, event | category | flops | bytes accessed | tf_op | source)
XLA Modules:
  0.0 143.0 jit_solution(610132218581180690)
XLA Ops:
  0.6 2.9 %pack_heads.1._ = bf16[8,640,256]{2,1,0:T(8,128)(2,1)} custom-call(bf16[128,2048]{1,0:T(8,128)(2,1)} %q_ref.1, bf16[128,2048]{1,0:T(8,128)(2,1)} %g_ref.1, bf16[128,2048]{1,0:T(8,128)(2,1)} %k_ref.1, bf16[128,2048]{1,0:T(8,128)(2,1)} %v_ref.1, bf16[64,2048]{1,0:T(8,128)(2,1)} %mk_ref.1, bf16[64,2048]{1,0:T(8,128)(2,1)} %mv_ref.1), custom_call_target="tpu_custom_call" | custom-call | bytes 5242880 | tf_op jit(solution)/shard_map/pack_heads/pallas_call | solution.py:75
  3.5 5.9 %all-to-all-start = ((bf16[8,640,256]{2,1,0:T(8,128)(2,1)}), bf16[8,640,256]{2,1,0:T(8,128)(2,1)S(1)}, u32[]{:S(2)}, u32[]{:S(2)}) async-start(bf16[8,640,256]{2,1,0:T(8,128)(2,1)} %pack_heads.1._), calls=%async_computation | async-start | bytes 5242880 | tf_op jit(solution)/shard_map/all_to_all | solution.py:324
  9.4 1.7 %copy-done = bf16[8,640,256]{2,1,0:T(8,128)(2,1)S(1)} copy-done((bf16[8,640,256]{2,1,0:T(8,128)(2,1)S(1)}, bf16[8,640,256]{2,1,0:T(8,128)(2,1)}, u32[]{:S(2)}) %copy-start) | copy-done | bytes 2621464
  11.2 1.2 copy-done.4
  12.4 3.8 %pack_hidden.1 = (bf16[2,512,128]{2,1,0:T(8,128)(2,1)S(1)}, bf16[2,512,128]{2,1,0:T(8,128)(2,1)S(1)}, bf16[2,512,128]{2,1,0:T(8,128)(2,1)}, bf16[2,512,128]{2,1,0:T(8,128)(2,1)}) custom-call(s32[4]{0:T(128)S(1)} %pad_add_fusion.place, bf16[128,4096]{1,0:T(8,128)(2,1)S(1)} %copy-done.4, bf16[8,640,256]{2,1,0:T(8,128)(2,1)S(1)} %copy-done), custom_call_target="tpu_custom_call" | custom-call | flops 1073741824 | bytes 2097152 | tf_op jit(solution)/shard_map/pack_hidden/pallas_call | solution.py:103
  16.3 25.8 %all-to-all-done.refs_4_.doc_ref.mk_ref.mv_ref = bf16[8,640,256]{2,1,0:T(8,128)(2,1)S(1)} async-done(((bf16[8,640,256]{2,1,0:T(8,128)(2,1)}), bf16[8,640,256]{2,1,0:T(8,128)(2,1)S(1)}, u32[]{:S(2)}, u32[]{:S(2)}) %all-to-all-start) | async-done | bytes 2621472 | tf_op jit(solution)/shard_map/all_to_all | solution.py:324
  42.0 2.4 %collective-permute-start = (bf16[2,512,128]{2,1,0:T(8,128)(2,1)S(1)}, bf16[2,512,128]{2,1,0:T(8,128)(2,1)S(1)}, u32[]{:S(2)}, u32[]{:S(2)}) collective-permute-start(bf16[2,512,128]{2,1,0:T(8,128)(2,1)S(1)} %get-tuple-element.38), channel_id=1, source_target_pairs={{0,1},{1,2},{2,3},{3,0},{4,5},{5,6},{6,7},{7,4},{8,9},{9,10},{10,1... | collective-permute-start | bytes 786440 | tf_op jit(solution)/shard_map/ppermute | solution.py:54
  44.4 4.2 %collective-permute-start.1 = (bf16[2,512,128]{2,1,0:T(8,128)(2,1)}, bf16[2,512,128]{2,1,0:T(8,128)(2,1)S(1)}, u32[]{:S(2)}, u32[]{:S(2)}) collective-permute-start(bf16[2,512,128]{2,1,0:T(8,128)(2,1)} %get-tuple-element.39), channel_id=1, source_target_pairs={{0,2},{1,3},{2,0},{3,1},{4,6},{5,7},{6,4},{7,5},{8,10},{9,11},{10,... | collective-permute-start | bytes 786440 | tf_op jit(solution)/shard_map/ppermute | solution.py:54
  49.8 9.2 %attention_backward.1 = (bf16[512,256]{1,0:T(8,128)(2,1)S(1)}, bf16[512,256]{1,0:T(8,128)(2,1)S(1)}, bf16[512,256]{1,0:T(8,128)(2,1)S(1)}, bf16[512,256]{1,0:T(8...) custom-call(s32[4]{0:T(128)S(1)} %pad_add_fusion.place, ...), custom_call_target="tpu_custom_call" | custom-call | flops 8000000000 | bytes 5242880 | tf_op jit(solution)/shard_map/attention_backward/pallas_call | solution.py:196
  59.7 3.0 %collective-permute-start.8 = (bf16[8,128,256]{2,1,0:T(8,128)(2,1)S(1)}, bf16[8,128,256]{2,1,0:T(8,128)(2,1)S(1)}, u32[]{:S(2)}, u32[]{:S(2)}) collective-permute-start(bf16[8,128,256]{2,1,0:T(8,128)(2,1)S(1)} %get-tuple-element.41.refs_8_), channel_id=1, source_target_pairs={{0,2},{1,3},{2,0},{3,1},{4,6},{5,7},{6,4},{7,5},{8,10},{9,11},{10,... | collective-permute-start | bytes 1572872 | tf_op jit(solution)/shard_map/ppermute | solution.py:54
  62.6 1.3 collective-permute-start.5
  64.6 6.4 %collective-permute-done.5.refs_6_ = bf16[2,512,128]{2,1,0:T(8,128)(2,1)S(1)} collective-permute-done((bf16[2,512,128]{2,1,0:T(8,128)(2,1)S(1)}, bf16[2,512,128]{2,1,0:T(8,128)(2,1)S(1)}, u32[]{:S(2)}, u32[]{:S(2)}) %collective-permute-start.5) | collective-permute-done | bytes 262176 | tf_op jit(solution)/shard_map/ppermute | solution.py:54
  71.0 5.6 %collective-permute-done.6.refs_7_ = bf16[2,512,128]{2,1,0:T(8,128)(2,1)S(1)} collective-permute-done((bf16[2,512,128]{2,1,0:T(8,128)(2,1)S(1)}, bf16[2,512,128]{2,1,0:T(8,128)(2,1)S(1)}, u32[]{:S(2)}, u32[]{:S(2)}) %collective-permute-start.6) | collective-permute-done | bytes 262176 | tf_op jit(solution)/shard_map/ppermute | solution.py:54
  76.6 9.7 %collective-permute-done.7.refs_9_ = bf16[8,128,256]{2,1,0:T(8,128)(2,1)S(1)} collective-permute-done((bf16[8,128,256]{2,1,0:T(8,128)(2,1)S(1)}, bf16[8,128,256]{2,1,0:T(8,128)(2,1)S(1)}, u32[]{:S(2)}, u32[]{:S(2)}) %collective-permute-start.7) | collective-permute-done | bytes 524320 | tf_op jit(solution)/shard_map/ppermute | solution.py:54
  86.2 2.9 %weight_product.1 = (bf16[512,1024]{1,0:T(8,128)(2,1)S(1)}, bf16[512,1024]{1,0:T(8,128)(2,1)S(1)}) custom-call(s32[4]{0:T(128)S(1)} %pad_add_fusion.place, bf16[2,512,128]{2,1,0:T(8,128)(2,1)S(1)} %get-tuple-element.37.refs_0_, bf16[2,512,128]{2,1,0:T(8,128)(2,1)S(1)} %collective-permute-done.refs_1_, ...), custom_call_target="tpu_custom_call" | custom-call | flops 2100000000 | bytes 6291456 | tf_op jit(solution)/shard_map/weight_product/pallas_call | solution.py:239
  89.7 9.3 %collective-permute-done.11.refs_4_ = bf16[4,512,256]{2,1,0:T(8,128)(2,1)S(1)} collective-permute-done((bf16[4,512,256]{2,1,0:T(8,128)(2,1)S(1)}, bf16[4,512,256]{2,1,0:T(8,128)(2,1)S(1)}, u32[]{:S(2)}, u32[]{:S(2)}) %collective-permute-start.11) | collective-permute-done | bytes 1048608 | tf_op jit(solution)/shard_map/ppermute | solution.py:54
  102.4 10.9 %all-to-all-start.1 = ((bf16[32,16,1024]{2,1,0:T(8,128)(2,1)}), bf16[32,16,1024]{2,1,0:T(8,128)(2,1)S(1)}, u32[]{:S(2)}, u32[]{:S(2)}) async-start(bf16[32,16,1024]{2,1,0:T(8,128)(2,1)} %bitcast.8), calls=%async_computation.1 | async-start | bytes 2097152 | tf_op jit(solution)/shard_map/all_to_all | solution.py:334
  114.6 2.6 %collective-permute-start.14 = (bf16[512,256]{1,0:T(8,128)(2,1)}, bf16[512,256]{1,0:T(8,128)(2,1)S(1)}, u32[]{:S(2)}, u32[]{:S(2)}) collective-permute-start(bf16[512,256]{1,0:T(8,128)(2,1)} %copy-done.3), channel_id=1, source_target_pairs={{0,3},{1,2},{2,1},{3,0},{4,7},{5,6},{6,5},{7,4},{8,11},{9,10},{10,... | collective-permute-start | bytes 786440 | tf_op jit(solution)/shard_map/ppermute | solution.py:339
  118.8 1.8 %collective-permute-start.15 = (bf16[512,256]{1,0:T(8,128)(2,1)S(1)}, bf16[512,256]{1,0:T(8,128)(2,1)S(1)}, u32[]{:S(2)}, u32[]{:S(2)}) collective-permute-start(bf16[512,256]{1,0:T(8,128)(2,1)S(1)} %get-tuple-element.62), channel_id=1, source_target_pairs={{0,1},{1,0},{2,3},{3,2},{4,5},{5,4},{6,7},{7,6},{8,9},{9,8},{10,11... | collective-permute-start | bytes 786440 | tf_op jit(solution)/shard_map/ppermute | solution.py:339
  120.7 2.3 %collective-permute-done.13.refs_2_ = bf16[512,256]{1,0:T(8,128)(2,1)S(1)} collective-permute-done((bf16[512,256]{1,0:T(8,128)(2,1)}, bf16[512,256]{1,0:T(8,128)(2,1)S(1)}, u32[]{:S(2)}, u32[]{:S(2)}) %collective-permute-start.13) | collective-permute-done | bytes 262176 | tf_op jit(solution)/shard_map/ppermute | solution.py:339
  123.0 7.9 %collective-permute-done.14.refs_3_ = bf16[512,256]{1,0:T(8,128)(2,1)S(1)} collective-permute-done((bf16[512,256]{1,0:T(8,128)(2,1)}, bf16[512,256]{1,0:T(8,128)(2,1)S(1)}, u32[]{:S(2)}, u32[]{:S(2)}) %collective-permute-start.14) | collective-permute-done | bytes 262176 | tf_op jit(solution)/shard_map/ppermute | solution.py:339
  130.9 8.6 %collective-permute-done.17.refs_7_ = bf16[512,256]{1,0:T(8,128)(2,1)S(1)} collective-permute-done((bf16[512,256]{1,0:T(8,128)(2,1)S(1)}, bf16[512,256]{1,0:T(8,128)(2,1)S(1)}, u32[]{:S(2)}, u32[]{:S(2)}) %collective-permute-start.17) | collective-permute-done | bytes 262176 | tf_op jit(solution)/shard_map/ppermute | solution.py:339
  139.5 2.1 %unpack_heads.1 = (bf16[128,2048]{1,0:T(8,128)(2,1)}, bf16[128,2048]{1,0:T(8,128)(2,1)}, bf16[128,2048]{1,0:T(8,128)(2,1)}, bf16[64,2048]{1,0:T(8,128)(2,1)}, bf16[64,2048]{1,0:T(8,128)(2,1)}) custom-call(s32[4]{0:T(128)S(1)} %pad_add_fusion.place, bf16[512,256]{1,0:T(8,128)(2,1)S(1)} %get-tuple-element.49.refs_0_, ...), custom_call_target="tpu_custom_call" | custom-call | bytes 4194304 | tf_op jit(solution)/shard_map/unpack_heads/pallas_call | solution.py:280
  141.6 1.3 weight_sum.1
  (36 shorter events, 9.4 us)
Async XLA Ops:
  3.5 38.5 %all-to-all-start = ((bf16[8,640,256]{2,1,0:T(8,128)(2,1)}), bf16[8,640,256]{2,1,0:T(8,128)(2,1)S(1)}, u32[]{:S(2)}, u32[]{:S(2)}) async-start(bf16[8,640,256]{2,1,0:T(8,128)(2,1)} %pack_heads.1._), calls=%async_computation | async-start | bytes 5242880 | tf_op jit(solution)/shard_map/all_to_all | solution.py:324
  9.4 1.7 %copy-start = (bf16[8,640,256]{2,1,0:T(8,128)(2,1)S(1)}, bf16[8,640,256]{2,1,0:T(8,128)(2,1)}, u32[]{:S(2)}) copy-start(bf16[8,640,256]{2,1,0:T(8,128)(2,1)} %pack_heads.1._) | copy-start | bytes 7864324
  11.2 1.2 copy-start.4
  42.0 17.0 %collective-permute-start = (bf16[2,512,128]{2,1,0:T(8,128)(2,1)S(1)}, bf16[2,512,128]{2,1,0:T(8,128)(2,1)S(1)}, u32[]{:S(2)}, u32[]{:S(2)}) collective-permute-start(bf16[2,512,128]{2,1,0:T(8,128)(2,1)S(1)} %get-tuple-element.38), channel_id=1, source_target_pairs={{0,1},{1,2},{2,3},{3,0},{4,5},{5,6},{6,7},{7,4},{8,9},{9,10},{10,1... | collective-permute-start | bytes 786440 | tf_op jit(solution)/shard_map/ppermute | solution.py:54
  44.4 15.2 %collective-permute-start.1 = (bf16[2,512,128]{2,1,0:T(8,128)(2,1)}, bf16[2,512,128]{2,1,0:T(8,128)(2,1)S(1)}, u32[]{:S(2)}, u32[]{:S(2)}) collective-permute-start(bf16[2,512,128]{2,1,0:T(8,128)(2,1)} %get-tuple-element.39), channel_id=1, source_target_pairs={{0,2},{1,3},{2,0},{3,1},{4,6},{5,7},{6,4},{7,5},{8,10},{9,11},{10,... | collective-permute-start | bytes 786440 | tf_op jit(solution)/shard_map/ppermute | solution.py:54
  48.6 14.0 %collective-permute-start.2 = (bf16[2,512,128]{2,1,0:T(8,128)(2,1)}, bf16[2,512,128]{2,1,0:T(8,128)(2,1)S(1)}, u32[]{:S(2)}, u32[]{:S(2)}) collective-permute-start(bf16[2,512,128]{2,1,0:T(8,128)(2,1)} %get-tuple-element.40), channel_id=1, source_target_pairs={{0,3},{1,0},{2,1},{3,2},{4,7},{5,4},{6,5},{7,6},{8,11},{9,8},{10,9... | collective-permute-start | bytes 786440 | tf_op jit(solution)/shard_map/ppermute | solution.py:54
  48.6 14.0 %collective-permute-start.3 = (bf16[2,512,128]{2,1,0:T(8,128)(2,1)S(1)}, bf16[2,512,128]{2,1,0:T(8,128)(2,1)S(1)}, u32[]{:S(2)}, u32[]{:S(2)}) collective-permute-start(bf16[2,512,128]{2,1,0:T(8,128)(2,1)S(1)} %get-tuple-element.37.refs_0_), channel_id=1, source_target_pairs={{0,4},{1,5},{2,6},{3,7},{4,0},{5,1},{6,2},{7,3},{8,12},{9,13},{10,... | collective-permute-start | bytes 786440 | tf_op jit(solution)/shard_map/ppermute | solution.py:54
  59.0 5.3 %collective-permute-start.4 = (bf16[2,512,128]{2,1,0:T(8,128)(2,1)S(1)}, bf16[2,512,128]{2,1,0:T(8,128)(2,1)S(1)}, u32[]{:S(2)}, u32[]{:S(2)}) collective-permute-start(bf16[2,512,128]{2,1,0:T(8,128)(2,1)S(1)} %collective-permute-done.refs_1_), channel_id=1, source_target_pairs={{0,4},{1,5},{2,6},{3,7},{4,0},{5,1},{6,2},{7,3},{8,12},{9,13},{10,... | collective-permute-start | bytes 786440 | tf_op jit(solution)/shard_map/ppermute | solution.py:54
  59.4 17.2 %collective-permute-start.9 = (bf16[8,128,256]{2,1,0:T(8,128)(2,1)S(1)}, bf16[8,128,256]{2,1,0:T(8,128)(2,1)S(1)}, u32[]{:S(2)}, u32[]{:S(2)}) collective-permute-start(bf16[8,128,256]{2,1,0:T(8,128)(2,1)S(1)} %get-tuple-element.41.refs_8_), channel_id=1, source_target_pairs={{0,3},{1,0},{2,1},{3,2},{4,7},{5,4},{6,5},{7,6},{8,11},{9,8},{10,9... | collective-permute-start | bytes 1572872 | tf_op jit(solution)/shard_map/ppermute | solution.py:54
  59.7 16.9 %collective-permute-start.8 = (bf16[8,128,256]{2,1,0:T(8,128)(2,1)S(1)}, bf16[8,128,256]{2,1,0:T(8,128)(2,1)S(1)}, u32[]{:S(2)}, u32[]{:S(2)}) collective-permute-start(bf16[8,128,256]{2,1,0:T(8,128)(2,1)S(1)} %get-tuple-element.41.refs_8_), channel_id=1, source_target_pairs={{0,2},{1,3},{2,0},{3,1},{4,6},{5,7},{6,4},{7,5},{8,10},{9,11},{10,... | collective-permute-start | bytes 1572872 | tf_op jit(solution)/shard_map/ppermute | solution.py:54
  62.6 23.6 %collective-permute-start.7 = (bf16[8,128,256]{2,1,0:T(8,128)(2,1)S(1)}, bf16[8,128,256]{2,1,0:T(8,128)(2,1)S(1)}, u32[]{:S(2)}, u32[]{:S(2)}) collective-permute-start(bf16[8,128,256]{2,1,0:T(8,128)(2,1)S(1)} %get-tuple-element.41.refs_8_), channel_id=1, source_target_pairs={{0,1},{1,2},{2,3},{3,0},{4,5},{5,6},{6,7},{7,4},{8,9},{9,10},{10,1... | collective-permute-start | bytes 1572872 | tf_op jit(solution)/shard_map/ppermute | solution.py:54
  62.6 8.3 %collective-permute-start.5 = (bf16[2,512,128]{2,1,0:T(8,128)(2,1)S(1)}, bf16[2,512,128]{2,1,0:T(8,128)(2,1)S(1)}, u32[]{:S(2)}, u32[]{:S(2)}) collective-permute-start(bf16[2,512,128]{2,1,0:T(8,128)(2,1)S(1)} %collective-permute-done.1.refs_2_), channel_id=1, source_target_pairs={{0,4},{1,5},{2,6},{3,7},{4,0},{5,1},{6,2},{7,3},{8,12},{9,13},{10,... | collective-permute-start | bytes 786440 | tf_op jit(solution)/shard_map/ppermute | solution.py:54
  64.3 12.3 %collective-permute-start.6 = (bf16[2,512,128]{2,1,0:T(8,128)(2,1)S(1)}, bf16[2,512,128]{2,1,0:T(8,128)(2,1)S(1)}, u32[]{:S(2)}, u32[]{:S(2)}) collective-permute-start(bf16[2,512,128]{2,1,0:T(8,128)(2,1)S(1)} %collective-permute-done.2.refs_3_), channel_id=1, source_target_pairs={{0,4},{1,5},{2,6},{3,7},{4,0},{5,1},{6,2},{7,3},{8,12},{9,13},{10,... | collective-permute-start | bytes 786440 | tf_op jit(solution)/shard_map/ppermute | solution.py:54
  71.0 28.1 %collective-permute-start.11 = (bf16[4,512,256]{2,1,0:T(8,128)(2,1)S(1)}, bf16[4,512,256]{2,1,0:T(8,128)(2,1)S(1)}, u32[]{:S(2)}, u32[]{:S(2)}) collective-permute-start(bf16[4,512,256]{2,1,0:T(8,128)(2,1)S(1)} %get-tuple-element.48), channel_id=1, source_target_pairs={{0,4},{1,5},{2,6},{3,7},{4,0},{5,1},{6,2},{7,3},{8,12},{9,13},{10,... | collective-permute-start | bytes 3145736 | tf_op jit(solution)/shard_map/ppermute | solution.py:54
  89.1 9.9 %collective-permute-start.10 = (bf16[512,1024]{1,0:T(8,128)(2,1)S(1)}, bf16[512,1024]{1,0:T(8,128)(2,1)S(1)}, u32[]{:S(2)}, u32[]{:S(2)}) collective-permute-start(bf16[512,1024]{1,0:T(8,128)(2,1)S(1)} %get-tuple-element.43), channel_id=1, source_target_pairs={{0,8},{1,9},{2,10},{3,11},{4,12},{5,13},{6,14},{7,15},{8,0},{9,1},... | collective-permute-start | bytes 3145736 | tf_op jit(solution)/shard_map/ppermute | solution.py:54
  100.3 0.7 copy-start.1
  101.0 0.7 copy-start.2
  102.4 39.2 %all-to-all-start.1 = ((bf16[32,16,1024]{2,1,0:T(8,128)(2,1)}), bf16[32,16,1024]{2,1,0:T(8,128)(2,1)S(1)}, u32[]{:S(2)}, u32[]{:S(2)}) async-start(bf16[32,16,1024]{2,1,0:T(8,128)(2,1)} %bitcast.8), calls=%async_computation.1 | async-start | bytes 2097152 | tf_op jit(solution)/shard_map/all_to_all | solution.py:334
  113.3 5.5 %collective-permute-start.12 = (bf16[512,256]{1,0:T(8,128)(2,1)}, bf16[512,256]{1,0:T(8,128)(2,1)S(1)}, u32[]{:S(2)}, u32[]{:S(2)}) collective-permute-start(bf16[512,256]{1,0:T(8,128)(2,1)} %copy-done.1), channel_id=1, source_target_pairs={{0,1},{1,0},{2,3},{3,2},{4,5},{5,4},{6,7},{7,6},{8,9},{9,8},{10,11... | collective-permute-start | bytes 786440 | tf_op jit(solution)/shard_map/ppermute | solution.py:339
  113.4 9.6 %collective-permute-start.13 = (bf16[512,256]{1,0:T(8,128)(2,1)}, bf16[512,256]{1,0:T(8,128)(2,1)S(1)}, u32[]{:S(2)}, u32[]{:S(2)}) collective-permute-start(bf16[512,256]{1,0:T(8,128)(2,1)} %copy-done.2), channel_id=1, source_target_pairs={{0,2},{1,3},{2,0},{3,1},{4,6},{5,7},{6,4},{7,5},{8,10},{9,11},{10,... | collective-permute-start | bytes 786440 | tf_op jit(solution)/shard_map/ppermute | solution.py:339
  114.6 16.3 %collective-permute-start.14 = (bf16[512,256]{1,0:T(8,128)(2,1)}, bf16[512,256]{1,0:T(8,128)(2,1)S(1)}, u32[]{:S(2)}, u32[]{:S(2)}) collective-permute-start(bf16[512,256]{1,0:T(8,128)(2,1)} %copy-done.3), channel_id=1, source_target_pairs={{0,3},{1,2},{2,1},{3,0},{4,7},{5,6},{6,5},{7,4},{8,11},{9,10},{10,... | collective-permute-start | bytes 786440 | tf_op jit(solution)/shard_map/ppermute | solution.py:339
  117.3 22.2 %collective-permute-start.17 = (bf16[512,256]{1,0:T(8,128)(2,1)S(1)}, bf16[512,256]{1,0:T(8,128)(2,1)S(1)}, u32[]{:S(2)}, u32[]{:S(2)}) collective-permute-start(bf16[512,256]{1,0:T(8,128)(2,1)S(1)} %get-tuple-element.60), channel_id=1, source_target_pairs={{0,3},{1,2},{2,1},{3,0},{4,7},{5,6},{6,5},{7,4},{8,11},{9,10},{10,... | collective-permute-start | bytes 786440 | tf_op jit(solution)/shard_map/ppermute | solution.py:339
  117.4 22.0 %collective-permute-start.16 = (bf16[512,256]{1,0:T(8,128)(2,1)S(1)}, bf16[512,256]{1,0:T(8,128)(2,1)S(1)}, u32[]{:S(2)}, u32[]{:S(2)}) collective-permute-start(bf16[512,256]{1,0:T(8,128)(2,1)S(1)} %get-tuple-element.61), channel_id=1, source_target_pairs={{0,2},{1,3},{2,0},{3,1},{4,6},{5,7},{6,4},{7,5},{8,10},{9,11},{10,... | collective-permute-start | bytes 786440 | tf_op jit(solution)/shard_map/ppermute | solution.py:339
  118.8 20.7 %collective-permute-start.15 = (bf16[512,256]{1,0:T(8,128)(2,1)S(1)}, bf16[512,256]{1,0:T(8,128)(2,1)S(1)}, u32[]{:S(2)}, u32[]{:S(2)}) collective-permute-start(bf16[512,256]{1,0:T(8,128)(2,1)S(1)} %get-tuple-element.62), channel_id=1, source_target_pairs={{0,1},{1,0},{2,3},{3,2},{4,5},{5,4},{6,7},{7,6},{8,9},{9,8},{10,11... | collective-permute-start | bytes 786440 | tf_op jit(solution)/shard_map/ppermute | solution.py:339
  (1 other events, 0.7 us)

commit v3 on v2

v3 whole, which is shorter than its diff:
```python
import jax
import jax.numpy as jnp
from jax import lax
from jax.experimental import pallas as pl
from jax.experimental.pallas import tpu as pltpu
from jax.sharding import PartitionSpec as P

HEAD_DIM = 128
DOCS = 8
ROWS = 128
MEM = 64
WIDTH = 4096
INNER = 2048
HALF = INNER // 2
PAIR = 2 * HEAD_DIM
AXES = ("group", "member")
LOW = jnp.bfloat16
FULL = jnp.float32


def coords(i):
    g, m = divmod(i, 8)
    return {"z": g // 4, "yh": (g // 2) % 2, "c": g % 2, "yl": m // 4, "x": m % 4}


def index_of(d):
    return (d["z"] * 4 + d["yh"] * 2 + d["c"]) * 8 + d["yl"] * 4 + d["x"]


def pairs(key, size, step):
    out = []
    for i in range(256):
        d = coords(i)
        d[key] = (d[key] + step) % size
        out.append((i, index_of(d)))
    return out


ZY_GROUPS = [
    [
        index_of({"z": z, "yh": yh, "c": c, "yl": yl, "x": x})
        for z in range(8)
        for yh in range(2)
        for yl in range(2)
    ]
    for c in range(2)
    for x in range(4)
]
ANY = pl.BlockSpec(memory_space=pl.ANY)
VMEM = pl.BlockSpec(memory_space=pltpu.VMEM)
SMEM = pl.BlockSpec(memory_space=pltpu.SMEM)


def shift(array, key, size, step):
    return lax.ppermute(array, AXES, pairs(key, size, step))


def dot(left, right, left_dim, right_dim):
    return lax.dot_general(
        left, right, (((left_dim,), (right_dim,)), ((), ())), preferred_element_type=FULL
    )


def pack_memory_kernel(place, mk_ref, mv_ref, near_ref, far_ref):
    for out, half in ((near_ref, place[1]), (far_ref, 1 - place[1])):
        cols = pl.ds(pl.multiple_of(half * HALF, HALF), HALF)
        out[0:MEM, :] = mk_ref[:, cols]
        out[MEM:, :] = mv_ref[:, cols]


def pack_memory(place, mk, mv):
    return pl.pallas_call(
        pack_memory_kernel,
        in_specs=[SMEM, VMEM, VMEM],
        out_specs=[VMEM] * 2,
        out_shape=[jax.ShapeDtypeStruct((2 * MEM, HALF), LOW)] * 2,
        cost_estimate=pl.CostEstimate(flops=0, bytes_accessed=1 << 20, transcendentals=0),
        name="pack_memory",
    )(place, mk, mv)


def pack_queries_kernel(place, q_ref, g_ref, k_ref, v_ref, *rest):
    out = rest[-1]
    for n, ref in enumerate((q_ref, g_ref, k_ref, v_ref)):
        out[n * ROWS : (n + 1) * ROWS, :] = ref[...]


def pack_queries(place, q, g, k, v, after):
    tall = pl.BlockSpec((ROWS, HALF), lambda i, s: (0, 1 - s[1]))
    return pl.pallas_call(
        pack_queries_kernel,
        grid_spec=pltpu.PrefetchScalarGridSpec(
            num_scalar_prefetch=1,
            grid=(1,),
            in_specs=[tall] * 4 + [ANY] * len(after),
            out_specs=pl.BlockSpec((4 * ROWS, HALF), lambda i, s: (0, 0)),
        ),
        out_shape=jax.ShapeDtypeStruct((4 * ROWS, HALF), LOW),
        cost_estimate=pl.CostEstimate(flops=0, bytes_accessed=2 << 20, transcendentals=0),
        name="pack_queries",
    )(place, q, g, k, v, *after)


def hidden_kernel(place, h_ref, *refs):
    outs, perm = refs[-5:-1], refs[-1]
    dst = lax.broadcasted_iota(jnp.int32, (1024, 1), 0)
    src = lax.broadcasted_iota(jnp.int32, (1024, 1024), 1)
    x, c, zl = ((dst >> 8) + place[3]) & 3, (dst >> 7) & 1, (dst >> 6) & 1
    yh, yl, i = (dst >> 5) & 1, (dst >> 4) & 1, dst & 15
    want = (zl << 9) | (yh << 8) | (c << 7) | (yl << 6) | (x << 4) | i
    perm[...] = jnp.where(src == want, 1.0, 0.0).astype(LOW)
    for t in range(4):
        moved = dot(perm[...], h_ref[:, t * 1024 : (t + 1) * 1024], 1, 1).astype(LOW)
        for k, out in enumerate(outs):
            for c in range(2):
                row = k * 256 + c * 128
                out[c, t * 128 : (t + 1) * 128, :] = moved[row : row + 128, :]


def hidden_pieces(place, hidden, after):
    return pl.pallas_call(
        hidden_kernel,
        in_specs=[SMEM, VMEM] + [ANY] * len(after),
        out_specs=[VMEM] * 4,
        out_shape=[jax.ShapeDtypeStruct((2, 512, ROWS), LOW)] * 4,
        scratch_shapes=[pltpu.VMEM((1024, 1024), LOW)],
        compiler_params=pltpu.CompilerParams(vmem_limit_bytes=24 << 20),
        cost_estimate=pl.CostEstimate(flops=1 << 30, bytes_accessed=2 << 20, transcendentals=0),
        name="pack_hidden",
    )(place, hidden, *after)


def gate_kernel(*refs):
    pass


def gate(arrays, after):
    count = len(arrays)
    return pl.pallas_call(
        gate_kernel,
        in_specs=[ANY] * (count + len(after)),
        out_specs=[ANY] * count,
        out_shape=[jax.ShapeDtypeStruct(a.shape, a.dtype) for a in arrays],
        input_output_aliases={n: n for n in range(count)},
        compiler_params=pltpu.CompilerParams(vmem_limit_bytes=1 << 20),
        name="gate",
    )(*arrays, *after)


def attention_kernel(place, q_ref, g_ref, k_ref, v_ref, far_ref, *refs):
    memory = refs[:4]
    gq_ref, local_ref, first_ref, back_ref = refs[4:8]
    term_refs = refs[8:]
    scale = HEAD_DIM**-0.5
    key_at = lax.broadcasted_iota(jnp.int32, (ROWS, ROWS), 0)
    query_at = lax.broadcasted_iota(jnp.int32, (ROWS, ROWS), 1)
    visible = key_at <= query_at
    for head in range(2):
        cols = slice(head * HEAD_DIM, (head + 1) * HEAD_DIM)
        q, g, k, v = [
            [ref[:, cols], far_ref[n * ROWS : (n + 1) * ROWS, cols]]
            for n, ref in enumerate((q_ref, g_ref, k_ref, v_ref))
        ]
        mk = jnp.concatenate([ref[n, 0:MEM, cols] for n in range(2) for ref in memory], axis=0)
        mv = jnp.concatenate([ref[n, MEM:, cols] for n in range(2) for ref in memory], axis=0)
        both_q = jnp.concatenate(q, axis=0)
        both_g = jnp.concatenate(g, axis=0)
        s_loc = jnp.concatenate(
            [jnp.where(visible, dot(k[n], q[n], 1, 1) * scale, -jnp.inf) for n in range(2)],
            axis=1,
        )
        dp_loc = jnp.concatenate([dot(v[n], g[n], 1, 1) for n in range(2)], axis=1)
        s_mem = dot(mk, both_q, 1, 1) * scale
        dp_mem = dot(mv, both_g, 1, 1)
        top = jnp.maximum(
            jnp.max(s_loc, axis=0, keepdims=True), jnp.max(s_mem, axis=0, keepdims=True)
        )
        e_loc = jnp.exp(s_loc - top)
        e_mem = jnp.exp(s_mem - top)
        total = jnp.sum(e_loc, axis=0, keepdims=True) + jnp.sum(e_mem, axis=0, keepdims=True)
        inverse = 1.0 / total
        p_loc = e_loc * inverse
        p_mem = e_mem * inverse
        delta = jnp.sum(p_loc * dp_loc, axis=0, keepdims=True) + jnp.sum(
            p_mem * dp_mem, axis=0, keepdims=True
        )
        ds_loc = (p_loc * (dp_loc - delta)).astype(LOW)
        ds_mem = (p_mem * (dp_mem - delta)).astype(LOW)
        low_loc = p_loc.astype(LOW)
        gq_mem = dot(ds_mem, mk, 0, 0)
        gq, glk, glv = [], [], []
        for n in range(2):
            rows = slice(n * ROWS, (n + 1) * ROWS)
            mine = ds_loc[:, rows]
            gq.append((scale * (dot(mine, k[n], 0, 0) + gq_mem[rows, :])).astype(LOW))
            glk.append((scale * dot(mine, q[n], 1, 0)).astype(LOW))
            glv.append(dot(low_loc[:, rows], g[n], 1, 0).astype(LOW))
        gq_ref[0:ROWS, cols] = gq[0]
        gq_ref[ROWS:, cols] = gq[1]
        local_ref[0:ROWS, cols] = glk[0]
        local_ref[ROWS:, cols] = glv[0]
        first_ref[:, cols] = gq[1]
        back_ref[0:ROWS, cols] = glk[1]
        back_ref[ROWS:, cols] = glv[1]
        dk = (scale * dot(ds_mem, both_q, 1, 0)).astype(LOW)
        dv = dot(p_mem.astype(LOW), both_g, 1, 0).astype(LOW)
        for n in range(8):
            rows = slice(n * MEM, (n + 1) * MEM)
            term_refs[n][0:MEM, cols] = dk[rows, :]
            term_refs[n][MEM:, cols] = dv[rows, :]


def attention(place, q, g, k, v, far, memory):
    def rows(count):
        return pl.BlockSpec((count, PAIR), lambda h, s: (0, h))

    mine = pl.BlockSpec((ROWS, PAIR), lambda h, s: (0, 4 * s[1] + h))
    whole = pl.BlockSpec((2, 2 * MEM, PAIR), lambda h, s: (0, 0, h))
    shapes = [(2 * ROWS, HALF), (2 * ROWS, HALF), (ROWS, HALF), (2 * ROWS, HALF)]
    shapes += [(2 * MEM, HALF)] * 8
    return pl.pallas_call(
        attention_kernel,
        grid_spec=pltpu.PrefetchScalarGridSpec(
            num_scalar_prefetch=1,
            grid=(4,),
            in_specs=[mine] * 4 + [rows(4 * ROWS)] + [whole] * 4,
            out_specs=[rows(shape[0]) for shape in shapes],
        ),
        out_shape=[jax.ShapeDtypeStruct(shape, LOW) for shape in shapes],
        compiler_params=pltpu.CompilerParams(vmem_limit_bytes=24 << 20),
        cost_estimate=pl.CostEstimate(
            flops=int(8e9), bytes_accessed=5 << 20, transcendentals=2 << 20
        ),
        name="attention_backward",
    )(place, q, g, k, v, far, *memory)


def product_half(place, half, out, refs):
    first, rest, pieces = refs[:4], refs[4:6], refs[6:10]
    left = jnp.concatenate(
        [ref[half] for ref in first] + [rest[0][half]] + [rest[1][k, half] for k in range(3)],
        axis=1,
    )
    for n in range(4):
        cols = slice(n * PAIR, (n + 1) * PAIR)
        right = jnp.concatenate(
            [p[0:ROWS, cols] for p in pieces] + [p[ROWS:, cols] for p in pieces], axis=0
        )
        out[:, cols] = dot(left, right, 1, 0).astype(LOW)


def give_kernel(place, *refs):
    product_half(place, 1 - place[0], refs[17], refs)


def keep_kernel(place, *refs):
    product_half(place, place[0], refs[11], refs)


def product_give(place, sources, carried, after):
    return pl.pallas_call(
        give_kernel,
        in_specs=[SMEM] + [VMEM] * 10 + [ANY] * 7,
        out_specs=[VMEM] + [ANY] * 6,
        out_shape=[jax.ShapeDtypeStruct((512, HALF), LOW)]
        + [jax.ShapeDtypeStruct(a.shape, LOW) for a in carried],
        input_output_aliases={11 + n: 1 + n for n in range(6)},
        compiler_params=pltpu.CompilerParams(vmem_limit_bytes=24 << 20),
        cost_estimate=pl.CostEstimate(flops=int(1e9), bytes_accessed=4 << 20, transcendentals=0),
        name="product_give",
    )(place, *sources, *carried, after)


def product_keep(place, sources, after):
    return pl.pallas_call(
        keep_kernel,
        in_specs=[SMEM] + [VMEM] * 10 + [ANY],
        out_specs=VMEM,
        out_shape=jax.ShapeDtypeStruct((512, HALF), LOW),
        compiler_params=pltpu.CompilerParams(vmem_limit_bytes=24 << 20),
        cost_estimate=pl.CostEstimate(flops=int(2e9), bytes_accessed=4 << 20, transcendentals=0),
        name="product_keep",
    )(place, *sources, after)


def merge_kernel(a_ref, b_ref, out_ref):
    out_ref[...] = (a_ref[...].astype(FULL) + b_ref[...].astype(FULL)).astype(LOW)


def merge(keep, swapped):
    return pl.pallas_call(
        merge_kernel,
        in_specs=[VMEM] * 2,
        out_specs=VMEM,
        out_shape=jax.ShapeDtypeStruct(keep.shape, LOW),
        compiler_params=pltpu.CompilerParams(vmem_limit_bytes=16 << 20),
        cost_estimate=pl.CostEstimate(flops=1 << 20, bytes_accessed=3 << 20, transcendentals=0),
        name="core_sum",
    )(keep, swapped)


def join_kernel(a_ref, b_ref, out_ref):
    out_ref[0] = a_ref[...]
    out_ref[1] = b_ref[...]


def join(a, b):
    return pl.pallas_call(
        join_kernel,
        in_specs=[VMEM] * 2,
        out_specs=VMEM,
        out_shape=jax.ShapeDtypeStruct((2, *a.shape), LOW),
        compiler_params=pltpu.CompilerParams(vmem_limit_bytes=8 << 20),
        cost_estimate=pl.CostEstimate(flops=0, bytes_accessed=1 << 20, transcendentals=0),
        name="join_memory",
    )(a, b)


def stack_kernel(*refs):
    for n in range(3):
        refs[-1][n] = refs[n][...]


def stack(arrays, after):
    return pl.pallas_call(
        stack_kernel,
        in_specs=[VMEM] * 3 + [ANY] * len(after),
        out_specs=VMEM,
        out_shape=jax.ShapeDtypeStruct((3, *arrays[0].shape), LOW),
        compiler_params=pltpu.CompilerParams(vmem_limit_bytes=16 << 20),
        cost_estimate=pl.CostEstimate(flops=0, bytes_accessed=2 << 20, transcendentals=0),
        name="stack_hidden",
    )(*arrays, *after)


def total_of(refs):
    total = refs[0][...].astype(FULL)
    for ref in refs[1:]:
        total = total + ref[...].astype(FULL)
    return total.astype(LOW)


def terms_kernel(*refs):
    refs[4][...] = total_of(refs[:4])


def sum_terms(terms):
    return pl.pallas_call(
        terms_kernel,
        in_specs=[VMEM] * 4,
        out_specs=VMEM,
        out_shape=jax.ShapeDtypeStruct((2 * MEM, HALF), LOW),
        compiler_params=pltpu.CompilerParams(vmem_limit_bytes=16 << 20),
        cost_estimate=pl.CostEstimate(flops=1 << 20, bytes_accessed=2 << 20, transcendentals=0),
        name="memory_sum",
    )(*terms)


def unpack_kernel(place, gq_ref, local_ref, first_ref, back_ref, got_ref, *refs):
    terms, outs = refs[:4], refs[4:]
    mine = pl.ds(pl.multiple_of(place[1] * HALF, HALF), HALF)
    theirs = pl.ds(pl.multiple_of((1 - place[1]) * HALF, HALF), HALF)
    outs[0][:, mine] = gq_ref[0:ROWS, :]
    outs[1][:, mine] = local_ref[0:ROWS, :]
    outs[2][:, mine] = local_ref[ROWS:, :]
    outs[0][:, theirs] = first_ref[...]
    outs[1][:, theirs] = back_ref[0:ROWS, :]
    outs[2][:, theirs] = back_ref[ROWS:, :]
    for value, cols in ((total_of(terms), mine), (got_ref[...], theirs)):
        outs[3][:, cols] = value[0:MEM, :]
        outs[4][:, cols] = value[MEM:, :]


def unpack(place, gq, local_grads, first, back, got, terms):
    return pl.pallas_call(
        unpack_kernel,
        in_specs=[SMEM] + [VMEM] * 9,
        out_specs=[VMEM] * 5,
        out_shape=[jax.ShapeDtypeStruct((ROWS, INNER), LOW)] * 3
        + [jax.ShapeDtypeStruct((MEM, INNER), LOW)] * 2,
        compiler_params=pltpu.CompilerParams(vmem_limit_bytes=16 << 20),
        cost_estimate=pl.CostEstimate(flops=0, bytes_accessed=4 << 20, transcendentals=0),
        name="unpack_heads",
    )(place, gq, local_grads, first, back, got, *terms)


def finish_kernel(in_ref, out_ref):
    for y in range(2):
        total = in_ref[y].astype(FULL)
        for n in range(1, 16):
            total = total + in_ref[2 * n + y].astype(FULL)
        out_ref[:, y * HALF : (y + 1) * HALF] = total * (1.0 / 256)


def finish(along):
    return pl.pallas_call(
        finish_kernel,
        in_specs=[VMEM],
        out_specs=VMEM,
        out_shape=jax.ShapeDtypeStruct((16, INNER), FULL),
        compiler_params=pltpu.CompilerParams(vmem_limit_bytes=16 << 20),
        cost_estimate=pl.CostEstimate(flops=1 << 20, bytes_accessed=1 << 20, transcendentals=0),
        name="weight_sum",
    )(along)


def local(
    hidden_states, queries, local_keys, local_values, memory_keys, memory_values, grad_output
):
    core = lax.rem(lax.axis_index("group"), 2)
    member = lax.axis_index("member")
    place = jnp.stack((core, member // 4, member, lax.rem(member, 4))).astype(jnp.int32)

    own_memory, give_memory = pack_memory(place, memory_keys, memory_values)
    other_memory = shift(give_memory, "yl", 2, 1)
    give_queries = pack_queries(
        place, queries, grad_output, local_keys, local_values, [own_memory]
    )
    joined = join(own_memory, other_memory)
    memory = [joined] + [shift(joined, "x", 4, k) for k in (1, 2, 3)]
    (give_queries,) = gate([give_queries], [joined])
    far_queries = shift(give_queries, "yl", 2, 1)

    hidden = hidden_pieces(place, hidden_states, [give_queries, joined])
    hidden = gate(hidden, memory[2:])
    near = [hidden[0]] + [shift(hidden[k], "x", 4, k) for k in (1, 2, 3)]

    gq, local_grads, first, back, *terms = attention(
        place, queries, grad_output, local_keys, local_values, far_queries, memory
    )
    pieces = [gq] + [shift(gq, "x", 4, k) for k in (1, 2, 3)]
    far = [shift(near[0], "yl", 2, 1)]
    far.append(shift(stack(near[1:], [gq, far[0]]), "yl", 2, 1))
    back = shift(back, "yl", 2, 1)
    first = shift(first, "yl", 2, 1)
    sources = near + far + pieces
    give, *moving = product_give(place, sources, terms[1:4] + terms[5:], first)
    keep = product_keep(place, sources, give)
    swapped = shift(give, "c", 2, 1)
    both = merge(keep, swapped)
    along = lax.all_to_all(
        both.reshape(32, 16, HALF), AXES, 0, 0, axis_index_groups=ZY_GROUPS, tiled=True
    )
    others = [terms[4]] + [shift(moving[2 + k], "x", 4, 4 - k) for k in (1, 2, 3)]
    got_sum = shift(sum_terms(others), "yl", 2, 1)
    nears = [terms[0]] + [shift(moving[k - 1], "x", 4, 4 - k) for k in (1, 2, 3)]
    gq_out, glk, glv, gmk, gmv = unpack(
        place, gq, local_grads, first, back, got_sum, nears
    )
    grad_weight = finish(along)
    return gq_out, glk, glv, gmk, gmv, grad_weight


def solution(mesh):
    spec = P(("group", "member"), None)
    return jax.shard_map(
        local, mesh=mesh, in_specs=(spec,) * 7, out_specs=(spec,) * 6, check_vma=False
    )
```

time: 144 us -> 131 us (0.910)
  waiting for transfers between devices: 76.7 us -> 56.5 us
  starting transfers between devices: 36.9 us -> 46 us
  local copies, waits for them, and re-layouts: 5.14 us -> 0.82 us
  Pallas kernels: 23.5 us -> 25.9 us
    all_to_all x2 -> x1, waiting for transfers between devices: 25.8 us -> 0.01 us  [local(): lax.all_to_all(both.reshape(32, 16, HALF), AXES, 0, 0, axis_index_groups=...]
    ppermute x12 -> x23, waiting for transfers between devices: 31.4 us -> 56.5 us  [shift(): return lax.ppermute(array, AXES, pairs(key, size, step))]
    ppermute x12 -> x23, starting transfers between devices: 13.5 us -> 35.1 us  [shift(): return lax.ppermute(array, AXES, pairs(key, size, step))]
    ppermute x6 -> x0, waiting for transfers between devices: 19.6 us -> none  [local(): lax.ppermute(piece, 'member', [(i, i ^ n & 3) for i in range(DOCS)])]
    ppermute x6 -> x0, starting transfers between devices: 6.54 us -> none  [local(): lax.ppermute(piece, 'member', [(i, i ^ n & 3) for i in range(DOCS)])]
    all_to_all x2 -> x1, starting transfers between devices: 16.8 us -> 10.9 us  [local(): lax.all_to_all(both.reshape(32, 16, HALF), AXES, 0, 0, axis_index_groups=...]
    unnamed x10 -> x28, local copies, waits for them, and re-layouts: 5.07 us -> 0.82 us
    pallas_call x7 -> x13, Pallas kernels: 14.3 us -> 15.9 us  [the longest x1 3.12 us: hidden_pieces(): pl.pallas_call(hidden_kernel, in_specs=[SMEM, VMEM] + [ANY] * len(after),...]
  transfers between devices with their start and end apart: 20 -> 24, of which waited for: 10 -> 13; matrix products, arithmetic and copies ran while one was open for 0% -> 0% of each run, Pallas kernels for 13% -> 15%
where the time goes in v3:
time: 131 us
  waiting for transfers between devices  56.5 us (43%)
  starting transfers between devices  46 us (35%)
  Pallas kernels  25.9 us (20%)
    ppermute x23, waiting for transfers between devices, shift(): return lax.ppermute(array, AXES, pairs(key, size, step))  56.5 us
    ppermute x23, starting transfers between devices, shift(): return lax.ppermute(array, AXES, pairs(key, size, step))  35.1 us
    all_to_all x1, starting transfers between devices, local(): lax.all_to_all(both.reshape(32, 16, HALF), AXES, 0, 0, axis_index_groups=...  10.9 us
    pallas_call x1, Pallas kernels, attention(): pl.pallas_call(attention_kernel, grid_spec=pltpu.PrefetchScalarGridSpec(n...  10 us
    pallas_call x1, Pallas kernels, hidden_pieces(): pl.pallas_call(hidden_kernel, in_specs=[SMEM, VMEM] + [ANY] * len(after),...  3.12 us
    pallas_call x1, Pallas kernels, pack_queries(): pl.pallas_call(pack_queries_kernel, grid_spec=pltpu.PrefetchScalarGridSpe...  3.04 us
  transfers between devices with their start and end apart: 24, of which 13 were waited for; matrix products, arithmetic and copies ran while one was open for 0% of the time, Pallas kernels for 15%

profile of v3, /device:TPU:1, one launch (start us, length us, event | category | flops | bytes accessed | tf_op | source)
XLA Modules:
  0.0 130.7 jit_solution(17729383631554317297)
XLA Ops:
  1.2 1.9 %pack_memory.1 = (bf16[128,1024]{1,0:T(8,128)(2,1)}, bf16[128,1024]{1,0:T(8,128)(2,1)}) custom-call(s32[4]{0:T(128)} %pad_add_fusion.place, bf16[64,2048]{1,0:T(8,128)(2,1)} %mk_ref.1, bf16[64,2048]{1,0:T(8,128)(2,1)} %mv_ref.1), custom_call_target="tpu_custom_call" | custom-call | bytes 1048576 | tf_op jit(solution)/shard_map/pack_memory/pallas_call | solution.py:72
  3.1 2.1 %collective-permute-start = (bf16[128,1024]{1,0:T(8,128)(2,1)}, bf16[128,1024]{1,0:T(8,128)(2,1)S(1)}, u32[]{:S(2)}, u32[]{:S(2)}) collective-permute-start(bf16[128,1024]{1,0:T(8,128)(2,1)} %get-tuple-element.41), channel_id=1, source_target_pairs={{0,4},{1,5},{2,6},{3,7},{4,0},{5,1},{6,2},{7,3},{8,12},{9,13},{10,... | collective-permute-start | bytes 786440 | tf_op jit(solution)/shard_map/ppermute | solution.py:55
  5.2 3.0 %pack_queries.1.refs_0_ = bf16[512,1024]{1,0:T(8,128)(2,1)} custom-call(s32[4]{0:T(128)} %pad_add_fusion.place, bf16[128,2048]{1,0:T(8,128)(2,1)} %q_ref.3, bf16[128,2048]{1,0:T(8,128)(2,1)} %g_ref.3, bf16[128,2048]{1,0:T(8,128)(2,1)} %k_ref.3, bf16[128,2048]{1,0:T(8,128)(2,1)} %v_ref.3, bf16[128,1024]{1,0:T(8,128)(2,1)} %get-tuple-element.40.rest_0_.a_ref), custom_call_target="tpu_custom_call" | custom-call | bytes 2097152 | tf_op jit(solution)/shard_map/pack_queries/pallas_call | solution.py:90
  8.3 2.1 %collective-permute-done.b_ref = bf16[128,1024]{1,0:T(8,128)(2,1)S(1)} collective-permute-done((bf16[128,1024]{1,0:T(8,128)(2,1)}, bf16[128,1024]{1,0:T(8,128)(2,1)S(1)}, u32[]{:S(2)}, u32[]{:S(2)}) %collective-permute-start) | collective-permute-done | bytes 262176 | tf_op jit(solution)/shard_map/ppermute | solution.py:55
  10.4 2.2 %collective-permute-start.1 = (bf16[512,1024]{1,0:T(8,128)(2,1)S(1)}, bf16[512,1024]{1,0:T(8,128)(2,1)S(1)}, u32[]{:S(2)}, u32[]{:S(2)}) collective-permute-start(bf16[512,1024]{1,0:T(8,128)(2,1)S(1)} %gate.2.refs_0_), channel_id=1, source_target_pairs={{0,4},{1,5},{2,6},{3,7},{4,0},{5,1},{6,2},{7,3},{8,12},{9,13},{10,... | collective-permute-start | bytes 3145736 | tf_op jit(solution)/shard_map/ppermute | solution.py:55
  12.6 2.7 %collective-permute-start.4 = (bf16[2,128,1024]{2,1,0:T(8,128)(2,1)S(1)}, bf16[2,128,1024]{2,1,0:T(8,128)(2,1)S(1)}, u32[]{:S(2)}, u32[]{:S(2)}) collective-permute-start(bf16[2,128,1024]{2,1,0:T(8,128)(2,1)S(1)} %join_memory.1.refs_1_.refs_0_), channel_id=1, source_target_pairs={{0,3},{1,0},{2,1},{3,2},{4,7},{5,4},{6,5},{7,6},{8,11},{9,8},{10,9... | collective-permute-start | bytes 1572872 | tf_op jit(solution)/shard_map/ppermute | solution.py:55
  16.4 3.1 %pack_hidden.1 = (bf16[2,512,128]{2,1,0:T(8,128)(2,1)S(1)}, bf16[2,512,128]{2,1,0:T(8,128)(2,1)S(1)}, bf16[2,512,128]{2,1,0:T(8,128)(2,1)S(1)}, bf16[2,512,128]{2,1,0:T(8,128)(2,1)S(1)}) custom-call(s32[4]{0:T(128)S(1)} %copy-done.11, bf16[128,4096]{1,0:T(8,128)(2,1)S(1)} %copy-done.12, bf16[512,1024]{1,0:T(8,128)(2,1)S(1)} %gate.2.refs_0_, ...), custom_call_target="tpu_custom_call" | custom-call | flops 1073741824 | bytes 2097152 | tf_op jit(solution)/shard_map/pack_hidden/pallas_call | solution.py:121
  19.5 6.3 %collective-permute-done.4.refs_3_.refs_5_ = bf16[2,128,1024]{2,1,0:T(8,128)(2,1)S(1)} collective-permute-done((bf16[2,128,1024]{2,1,0:T(8,128)(2,1)S(1)}, bf16[2,128,1024]{2,1,0:T(8,128)(2,1)S(1)}, u32[]{:S(2)}, u32[]{:S(2)}) %collective-permute-start.4) | collective-permute-done | bytes 524320 | tf_op jit(solution)/shard_map/ppermute | solution.py:55
  25.8 2.3 %collective-permute-done.3.refs_2_.refs_4_ = bf16[2,128,1024]{2,1,0:T(8,128)(2,1)S(1)} collective-permute-done((bf16[2,128,1024]{2,1,0:T(8,128)(2,1)S(1)}, bf16[2,128,1024]{2,1,0:T(8,128)(2,1)S(1)}, u32[]{:S(2)}, u32[]{:S(2)}) %collective-permute-start.3) | collective-permute-done | bytes 524320 | tf_op jit(solution)/shard_map/ppermute | solution.py:55
  28.2 9.7 %collective-permute-start.7 = (bf16[2,512,128]{2,1,0:T(8,128)(2,1)S(1)}, bf16[2,512,128]{2,1,0:T(8,128)(2,1)S(1)}, u32[]{:S(2)}, u32[]{:S(2)}) collective-permute-start(bf16[2,512,128]{2,1,0:T(8,128)(2,1)S(1)} %get-tuple-element.52), channel_id=1, source_target_pairs={{0,1},{1,2},{2,3},{3,0},{4,5},{5,6},{6,7},{7,4},{8,9},{9,10},{10,1... | collective-permute-start | bytes 786440 | tf_op jit(solution)/shard_map/ppermute | solution.py:55
  42.1 10.0 %attention_backward.1 = (bf16[256,1024]{1,0:T(8,128)(2,1)S(1)}, bf16[256,1024]{1,0:T(8,128)(2,1)S(1)}, bf16[128,1024]{1,0:T(8,128)(2,1)S(1)}, bf16[256,1024]{1,0...) custom-call(s32[4]{0:T(128)S(1)} %copy-done.11, ...), custom_call_target="tpu_custom_call" | custom-call | flops 8000000000 | bytes 5242880 | tf_op jit(solution)/shard_map/attention_backward/pallas_call | solution.py:221
  55.9 19.4 %collective-permute-done.5.refs_16_.first_ref = bf16[128,1024]{1,0:T(8,128)(2,1)S(1)} collective-permute-done((bf16[128,1024]{1,0:T(8,128)(2,1)S(1)}, bf16[128,1024]{1,0:T(8,128)(2,1)S(1)}, u32[]{:S(2)}, u32[]{:S(2)}) %collective-permute-start.5) | collective-permute-done | bytes 262176 | tf_op jit(solution)/shard_map/ppermute | solution.py:55
  75.2 5.6 %collective-permute-done.12.refs_7_ = bf16[256,1024]{1,0:T(8,128)(2,1)S(1)} collective-permute-done((bf16[256,1024]{1,0:T(8,128)(2,1)S(1)}, bf16[256,1024]{1,0:T(8,128)(2,1)S(1)}, u32[]{:S(2)}, u32[]{:S(2)}) %collective-permute-start.12) | collective-permute-done | bytes 524320 | tf_op jit(solution)/shard_map/ppermute | solution.py:55
  80.8 1.8 %product_give.1 = (bf16[512,1024]{1,0:T(8,128)(2,1)S(1)}, bf16[128,1024]{1,0:T(8,128)(2,1)S(1)}, bf16[128,1024]{1,0:T(8,128)(2,1)S(1)}, bf16[128,1024]{1,0:T(8,1...) custom-call(s32[4]{0:T(128)S(1)} %copy-done.11, ...), custom_call_target="tpu_custom_call", output_to_operand_aliasing={{1}: (11, {}), {2}: (12, {}), {3}: (13, {}), {4}: (14, {}),... | custom-call | flops 1000000000 | bytes 4194304 | tf_op jit(solution)/shard_map/product_give/pallas_call | solution.py:261
  83.3 1.8 %product_keep.1.a_ref = bf16[512,1024]{1,0:T(8,128)(2,1)S(1)} custom-call(s32[4]{0:T(128)S(1)} %copy-done.11, bf16[2,512,128]{2,1,0:T(8,128)(2,1)S(1)} %get-tuple-element.51.refs_0_, bf16[2,512,128]{2,1,0:T(8,128)(2,1)S(1)} %collective-permute-done.7.refs_0_.refs_1_, bf16[2,512,128]{2,1,0:T(8,128)(2,1)S(1)} %collective-permute-done.8.refs_1_.refs_2_, ...), custom_call_target="tpu_custom_call" | custom-call | flops 2000000000 | bytes 4194304 | tf_op jit(solution)/shard_map/product_keep/pallas_call | solution.py:275
  86.8 10.9 %all-to-all-start = ((bf16[32,16,1024]{2,1,0:T(8,128)(2,1)}), bf16[32,16,1024]{2,1,0:T(8,128)(2,1)S(1)}, u32[]{:S(2)}, u32[]{:S(2)}) async-start(bf16[32,16,1024]{2,1,0:T(8,128)(2,1)} %bitcast.4), calls=%async_computation | async-start | bytes 2097152 | tf_op jit(solution)/shard_map/all_to_all | solution.py:441
  100.6 2.3 %collective-permute-start.19 = (bf16[128,1024]{1,0:T(8,128)(2,1)S(1)}, bf16[128,1024]{1,0:T(8,128)(2,1)S(1)}, u32[]{:S(2)}, u32[]{:S(2)}) collective-permute-start(bf16[128,1024]{1,0:T(8,128)(2,1)S(1)} %get-tuple-element.65), channel_id=1, source_target_pairs={{0,3},{1,0},{2,1},{3,2},{4,7},{5,4},{6,5},{7,6},{8,11},{9,8},{10,9... | collective-permute-start | bytes 786440 | tf_op jit(solution)/shard_map/ppermute | solution.py:55
  102.9 2.3 %collective-permute-done.15.refs_1_ = bf16[128,1024]{1,0:T(8,128)(2,1)S(1)} collective-permute-done((bf16[128,1024]{1,0:T(8,128)(2,1)}, bf16[128,1024]{1,0:T(8,128)(2,1)S(1)}, u32[]{:S(2)}, u32[]{:S(2)}) %collective-permute-start.15) | collective-permute-done | bytes 262176 | tf_op jit(solution)/shard_map/ppermute | solution.py:55
  107.3 3.7 %collective-permute-start.21 = (bf16[128,1024]{1,0:T(8,128)(2,1)S(1)}, bf16[128,1024]{1,0:T(8,128)(2,1)S(1)}, u32[]{:S(2)}, u32[]{:S(2)}) collective-permute-start(bf16[128,1024]{1,0:T(8,128)(2,1)S(1)} %get-tuple-element.67), channel_id=1, source_target_pairs={{0,1},{1,2},{2,3},{3,0},{4,5},{5,6},{6,7},{7,4},{8,9},{9,10},{10,1... | collective-permute-start | bytes 786440 | tf_op jit(solution)/shard_map/ppermute | solution.py:55
  111.0 4.6 %collective-permute-done.17.refs_3_ = bf16[128,1024]{1,0:T(8,128)(2,1)S(1)} collective-permute-done((bf16[128,1024]{1,0:T(8,128)(2,1)}, bf16[128,1024]{1,0:T(8,128)(2,1)S(1)}, u32[]{:S(2)}, u32[]{:S(2)}) %collective-permute-start.17) | collective-permute-done | bytes 262176 | tf_op jit(solution)/shard_map/ppermute | solution.py:55
  117.3 4.1 %collective-permute-done.6.back_ref = bf16[256,1024]{1,0:T(8,128)(2,1)S(1)} collective-permute-done((bf16[256,1024]{1,0:T(8,128)(2,1)}, bf16[256,1024]{1,0:T(8,128)(2,1)S(1)}, u32[]{:S(2)}, u32[]{:S(2)}) %collective-permute-start.6) | collective-permute-done | bytes 524320 | tf_op jit(solution)/shard_map/ppermute | solution.py:55
  121.4 4.0 %collective-permute-done.21.refs_3_ = bf16[128,1024]{1,0:T(8,128)(2,1)S(1)} collective-permute-done((bf16[128,1024]{1,0:T(8,128)(2,1)S(1)}, bf16[128,1024]{1,0:T(8,128)(2,1)S(1)}, u32[]{:S(2)}, u32[]{:S(2)}) %collective-permute-start.21) | collective-permute-done | bytes 262176 | tf_op jit(solution)/shard_map/ppermute | solution.py:55
  125.4 2.5 %collective-permute-done.18.got_ref = bf16[128,1024]{1,0:T(8,128)(2,1)S(1)} collective-permute-done((bf16[128,1024]{1,0:T(8,128)(2,1)S(1)}, bf16[128,1024]{1,0:T(8,128)(2,1)S(1)}, u32[]{:S(2)}, u32[]{:S(2)}) %collective-permute-start.18) | collective-permute-done | bytes 262176 | tf_op jit(solution)/shard_map/ppermute | solution.py:55
  127.9 2.0 %unpack_heads.1 = (bf16[128,2048]{1,0:T(8,128)(2,1)}, bf16[128,2048]{1,0:T(8,128)(2,1)}, bf16[128,2048]{1,0:T(8,128)(2,1)}, bf16[64,2048]{1,0:T(8,128)(2,1)}, bf16[64,2048]{1,0:T(8,128)(2,1)}) custom-call(s32[4]{0:T(128)S(1)} %copy-done.11, bf16[256,1024]{1,0:T(8,128)(2,1)S(1)} %get-tuple-element.42.refs_3_.refs_6_.gq_ref, ...), custom_call_target="tpu_custom_call" | custom-call | bytes 4194304 | tf_op jit(solution)/shard_map/unpack_heads/pallas_call | solution.py:375
  (67 shorter events, 19.5 us)
Async XLA Ops:
  3.1 7.2 %collective-permute-start = (bf16[128,1024]{1,0:T(8,128)(2,1)}, bf16[128,1024]{1,0:T(8,128)(2,1)S(1)}, u32[]{:S(2)}, u32[]{:S(2)}) collective-permute-start(bf16[128,1024]{1,0:T(8,128)(2,1)} %get-tuple-element.41), channel_id=1, source_target_pairs={{0,4},{1,5},{2,6},{3,7},{4,0},{5,1},{6,2},{7,3},{8,12},{9,13},{10,... | collective-permute-start | bytes 786440 | tf_op jit(solution)/shard_map/ppermute | solution.py:55
  10.4 31.6 %collective-permute-start.1 = (bf16[512,1024]{1,0:T(8,128)(2,1)S(1)}, bf16[512,1024]{1,0:T(8,128)(2,1)S(1)}, u32[]{:S(2)}, u32[]{:S(2)}) collective-permute-start(bf16[512,1024]{1,0:T(8,128)(2,1)S(1)} %gate.2.refs_0_), channel_id=1, source_target_pairs={{0,4},{1,5},{2,6},{3,7},{4,0},{5,1},{6,2},{7,3},{8,12},{9,13},{10,... | collective-permute-start | bytes 3145736 | tf_op jit(solution)/shard_map/ppermute | solution.py:55
  12.6 13.2 %collective-permute-start.4 = (bf16[2,128,1024]{2,1,0:T(8,128)(2,1)S(1)}, bf16[2,128,1024]{2,1,0:T(8,128)(2,1)S(1)}, u32[]{:S(2)}, u32[]{:S(2)}) collective-permute-start(bf16[2,128,1024]{2,1,0:T(8,128)(2,1)S(1)} %join_memory.1.refs_1_.refs_0_), channel_id=1, source_target_pairs={{0,3},{1,0},{2,1},{3,2},{4,7},{5,4},{6,5},{7,6},{8,11},{9,8},{10,9... | collective-permute-start | bytes 1572872 | tf_op jit(solution)/shard_map/ppermute | solution.py:55
  15.3 12.9 %collective-permute-start.3 = (bf16[2,128,1024]{2,1,0:T(8,128)(2,1)S(1)}, bf16[2,128,1024]{2,1,0:T(8,128)(2,1)S(1)}, u32[]{:S(2)}, u32[]{:S(2)}) collective-permute-start(bf16[2,128,1024]{2,1,0:T(8,128)(2,1)S(1)} %join_memory.1.refs_1_.refs_0_), channel_id=1, source_target_pairs={{0,2},{1,3},{2,0},{3,1},{4,6},{5,7},{6,4},{7,5},{8,10},{9,11},{10,... | collective-permute-start | bytes 1572872 | tf_op jit(solution)/shard_map/ppermute | solution.py:55
  15.8 26.1 %collective-permute-start.2 = (bf16[2,128,1024]{2,1,0:T(8,128)(2,1)S(1)}, bf16[2,128,1024]{2,1,0:T(8,128)(2,1)S(1)}, u32[]{:S(2)}, u32[]{:S(2)}) collective-permute-start(bf16[2,128,1024]{2,1,0:T(8,128)(2,1)S(1)} %join_memory.1.refs_1_.refs_0_), channel_id=1, source_target_pairs={{0,1},{1,2},{2,3},{3,0},{4,5},{5,6},{6,7},{7,4},{8,9},{9,10},{10,1... | collective-permute-start | bytes 1572872 | tf_op jit(solution)/shard_map/ppermute | solution.py:55
  28.2 23.9 %collective-permute-start.7 = (bf16[2,512,128]{2,1,0:T(8,128)(2,1)S(1)}, bf16[2,512,128]{2,1,0:T(8,128)(2,1)S(1)}, u32[]{:S(2)}, u32[]{:S(2)}) collective-permute-start(bf16[2,512,128]{2,1,0:T(8,128)(2,1)S(1)} %get-tuple-element.52), channel_id=1, source_target_pairs={{0,1},{1,2},{2,3},{3,0},{4,5},{5,6},{6,7},{7,4},{8,9},{9,10},{10,1... | collective-permute-start | bytes 786440 | tf_op jit(solution)/shard_map/ppermute | solution.py:55
  37.9 14.3 %collective-permute-start.8 = (bf16[2,512,128]{2,1,0:T(8,128)(2,1)S(1)}, bf16[2,512,128]{2,1,0:T(8,128)(2,1)S(1)}, u32[]{:S(2)}, u32[]{:S(2)}) collective-permute-start(bf16[2,512,128]{2,1,0:T(8,128)(2,1)S(1)} %get-tuple-element.53), channel_id=1, source_target_pairs={{0,2},{1,3},{2,0},{3,1},{4,6},{5,7},{6,4},{7,5},{8,10},{9,11},{10,... | collective-permute-start | bytes 786440 | tf_op jit(solution)/shard_map/ppermute | solution.py:55
  39.0 13.2 %collective-permute-start.9 = (bf16[2,512,128]{2,1,0:T(8,128)(2,1)S(1)}, bf16[2,512,128]{2,1,0:T(8,128)(2,1)S(1)}, u32[]{:S(2)}, u32[]{:S(2)}) collective-permute-start(bf16[2,512,128]{2,1,0:T(8,128)(2,1)S(1)} %get-tuple-element.54), channel_id=1, source_target_pairs={{0,3},{1,0},{2,1},{3,2},{4,7},{5,4},{6,5},{7,6},{8,11},{9,8},{10,9... | collective-permute-start | bytes 786440 | tf_op jit(solution)/shard_map/ppermute | solution.py:55
  41.9 10.3 %collective-permute-start.10 = (bf16[2,512,128]{2,1,0:T(8,128)(2,1)S(1)}, bf16[2,512,128]{2,1,0:T(8,128)(2,1)S(1)}, u32[]{:S(2)}, u32[]{:S(2)}) collective-permute-start(bf16[2,512,128]{2,1,0:T(8,128)(2,1)S(1)} %get-tuple-element.51.refs_0_), channel_id=1, source_target_pairs={{0,4},{1,5},{2,6},{3,7},{4,0},{5,1},{6,2},{7,3},{8,12},{9,13},{10,... | collective-permute-start | bytes 786440 | tf_op jit(solution)/shard_map/ppermute | solution.py:55
  52.9 27.9 %collective-permute-start.11 = (bf16[3,2,512,128]{3,2,1,0:T(8,128)(2,1)S(1)}, bf16[3,2,512,128]{3,2,1,0:T(8,128)(2,1)S(1)}, u32[]{:S(2)}, u32[]{:S(2)}) collective-permute-start(bf16[3,2,512,128]{3,2,1,0:T(8,128)(2,1)S(1)} %stack_hidden.1), channel_id=1, source_target_pairs={{0,4},{1,5},{2,6},{3,7},{4,0},{5,1},{6,2},{7,3},{8,12},{9,13},{10,... | collective-permute-start | bytes 2359304 | tf_op jit(solution)/shard_map/ppermute | solution.py:55
  54.2 21.0 %collective-permute-start.14 = (bf16[256,1024]{1,0:T(8,128)(2,1)S(1)}, bf16[256,1024]{1,0:T(8,128)(2,1)S(1)}, u32[]{:S(2)}, u32[]{:S(2)}) collective-permute-start(bf16[256,1024]{1,0:T(8,128)(2,1)S(1)} %get-tuple-element.42.refs_3_.refs_6_.gq_ref), channel_id=1, source_target_pairs={{0,3},{1,0},{2,1},{3,2},{4,7},{5,4},{6,5},{7,6},{8,11},{9,8},{10,9... | collective-permute-start | bytes 1572872 | tf_op jit(solution)/shard_map/ppermute | solution.py:55
  54.2 21.0 %collective-permute-start.13 = (bf16[256,1024]{1,0:T(8,128)(2,1)S(1)}, bf16[256,1024]{1,0:T(8,128)(2,1)S(1)}, u32[]{:S(2)}, u32[]{:S(2)}) collective-permute-start(bf16[256,1024]{1,0:T(8,128)(2,1)S(1)} %get-tuple-element.42.refs_3_.refs_6_.gq_ref), channel_id=1, source_target_pairs={{0,2},{1,3},{2,0},{3,1},{4,6},{5,7},{6,4},{7,5},{8,10},{9,11},{10,... | collective-permute-start | bytes 1572872 | tf_op jit(solution)/shard_map/ppermute | solution.py:55
  54.8 26.1 %collective-permute-start.12 = (bf16[256,1024]{1,0:T(8,128)(2,1)S(1)}, bf16[256,1024]{1,0:T(8,128)(2,1)S(1)}, u32[]{:S(2)}, u32[]{:S(2)}) collective-permute-start(bf16[256,1024]{1,0:T(8,128)(2,1)S(1)} %get-tuple-element.42.refs_3_.refs_6_.gq_ref), channel_id=1, source_target_pairs={{0,1},{1,2},{2,3},{3,0},{4,5},{5,6},{6,7},{7,4},{8,9},{9,10},{10,1... | collective-permute-start | bytes 1572872 | tf_op jit(solution)/shard_map/ppermute | solution.py:55
  55.7 19.5 %collective-permute-start.5 = (bf16[128,1024]{1,0:T(8,128)(2,1)S(1)}, bf16[128,1024]{1,0:T(8,128)(2,1)S(1)}, u32[]{:S(2)}, u32[]{:S(2)}) collective-permute-start(bf16[128,1024]{1,0:T(8,128)(2,1)S(1)} %get-tuple-element.44), channel_id=1, source_target_pairs={{0,4},{1,5},{2,6},{3,7},{4,0},{5,1},{6,2},{7,3},{8,12},{9,13},{10,... | collective-permute-start | bytes 786440 | tf_op jit(solution)/shard_map/ppermute | solution.py:55
  82.7 2.9 %collective-permute-start.22 = (bf16[512,1024]{1,0:T(8,128)(2,1)S(1)}, bf16[512,1024]{1,0:T(8,128)(2,1)S(1)}, u32[]{:S(2)}, u32[]{:S(2)}) collective-permute-start(bf16[512,1024]{1,0:T(8,128)(2,1)S(1)} %get-tuple-element.73.refs_10_), channel_id=1, source_target_pairs={{0,8},{1,9},{2,10},{3,11},{4,12},{5,13},{6,14},{7,15},{8,0},{9,1},... | collective-permute-start | bytes 3145736 | tf_op jit(solution)/shard_map/ppermute | solution.py:55
  86.8 43.1 %all-to-all-start = ((bf16[32,16,1024]{2,1,0:T(8,128)(2,1)}), bf16[32,16,1024]{2,1,0:T(8,128)(2,1)S(1)}, u32[]{:S(2)}, u32[]{:S(2)}) async-start(bf16[32,16,1024]{2,1,0:T(8,128)(2,1)} %bitcast.4), calls=%async_computation | async-start | bytes 2097152 | tf_op jit(solution)/shard_map/all_to_all | solution.py:441
  97.7 7.5 %collective-permute-start.15 = (bf16[128,1024]{1,0:T(8,128)(2,1)}, bf16[128,1024]{1,0:T(8,128)(2,1)S(1)}, u32[]{:S(2)}, u32[]{:S(2)}) collective-permute-start(bf16[128,1024]{1,0:T(8,128)(2,1)} %copy-done.6), channel_id=1, source_target_pairs={{0,3},{1,0},{2,1},{3,2},{4,7},{5,4},{6,5},{7,6},{8,11},{9,8},{10,9... | collective-permute-start | bytes 786440 | tf_op jit(solution)/shard_map/ppermute | solution.py:55
  98.7 8.6 %collective-permute-start.16 = (bf16[128,1024]{1,0:T(8,128)(2,1)}, bf16[128,1024]{1,0:T(8,128)(2,1)S(1)}, u32[]{:S(2)}, u32[]{:S(2)}) collective-permute-start(bf16[128,1024]{1,0:T(8,128)(2,1)} %copy-done.7), channel_id=1, source_target_pairs={{0,2},{1,3},{2,0},{3,1},{4,6},{5,7},{6,4},{7,5},{8,10},{9,11},{10,... | collective-permute-start | bytes 786440 | tf_op jit(solution)/shard_map/ppermute | solution.py:55
  98.8 16.7 %collective-permute-start.17 = (bf16[128,1024]{1,0:T(8,128)(2,1)}, bf16[128,1024]{1,0:T(8,128)(2,1)S(1)}, u32[]{:S(2)}, u32[]{:S(2)}) collective-permute-start(bf16[128,1024]{1,0:T(8,128)(2,1)} %copy-done.8), channel_id=1, source_target_pairs={{0,1},{1,2},{2,3},{3,0},{4,5},{5,6},{6,7},{7,4},{8,9},{9,10},{10,1... | collective-permute-start | bytes 786440 | tf_op jit(solution)/shard_map/ppermute | solution.py:55
  99.4 22.0 %collective-permute-start.6 = (bf16[256,1024]{1,0:T(8,128)(2,1)}, bf16[256,1024]{1,0:T(8,128)(2,1)S(1)}, u32[]{:S(2)}, u32[]{:S(2)}) collective-permute-start(bf16[256,1024]{1,0:T(8,128)(2,1)} %copy-done.13), channel_id=1, source_target_pairs={{0,4},{1,5},{2,6},{3,7},{4,0},{5,1},{6,2},{7,3},{8,12},{9,13},{10,... | collective-permute-start | bytes 1572872 | tf_op jit(solution)/shard_map/ppermute | solution.py:55
  100.6 20.8 %collective-permute-start.19 = (bf16[128,1024]{1,0:T(8,128)(2,1)S(1)}, bf16[128,1024]{1,0:T(8,128)(2,1)S(1)}, u32[]{:S(2)}, u32[]{:S(2)}) collective-permute-start(bf16[128,1024]{1,0:T(8,128)(2,1)S(1)} %get-tuple-element.65), channel_id=1, source_target_pairs={{0,3},{1,0},{2,1},{3,2},{4,7},{5,4},{6,5},{7,6},{8,11},{9,8},{10,9... | collective-permute-start | bytes 786440 | tf_op jit(solution)/shard_map/ppermute | solution.py:55
  105.2 16.2 %collective-permute-start.20 = (bf16[128,1024]{1,0:T(8,128)(2,1)S(1)}, bf16[128,1024]{1,0:T(8,128)(2,1)S(1)}, u32[]{:S(2)}, u32[]{:S(2)}) collective-permute-start(bf16[128,1024]{1,0:T(8,128)(2,1)S(1)} %get-tuple-element.66), channel_id=1, source_target_pairs={{0,2},{1,3},{2,0},{3,1},{4,6},{5,7},{6,4},{7,5},{8,10},{9,11},{10,... | collective-permute-start | bytes 786440 | tf_op jit(solution)/shard_map/ppermute | solution.py:55
  107.3 18.1 %collective-permute-start.21 = (bf16[128,1024]{1,0:T(8,128)(2,1)S(1)}, bf16[128,1024]{1,0:T(8,128)(2,1)S(1)}, u32[]{:S(2)}, u32[]{:S(2)}) collective-permute-start(bf16[128,1024]{1,0:T(8,128)(2,1)S(1)} %get-tuple-element.67), channel_id=1, source_target_pairs={{0,1},{1,2},{2,3},{3,0},{4,5},{5,6},{6,7},{7,4},{8,9},{9,10},{10,1... | collective-permute-start | bytes 786440 | tf_op jit(solution)/shard_map/ppermute | solution.py:55
  115.7 12.2 %collective-permute-start.18 = (bf16[128,1024]{1,0:T(8,128)(2,1)S(1)}, bf16[128,1024]{1,0:T(8,128)(2,1)S(1)}, u32[]{:S(2)}, u32[]{:S(2)}) collective-permute-start(bf16[128,1024]{1,0:T(8,128)(2,1)S(1)} %memory_sum.1), channel_id=1, source_target_pairs={{0,4},{1,5},{2,6},{3,7},{4,0},{5,1},{6,2},{7,3},{8,12},{9,13},{10,... | collective-permute-start | bytes 786440 | tf_op jit(solution)/shard_map/ppermute | solution.py:55
  (14 other events, 95.8 us)

commit v4 on v3

--- a/solution.py
+++ b/solution.py
@@ -61,22 +61,23 @@
     )
 
 
-def pack_memory_kernel(place, mk_ref, mv_ref, near_ref, far_ref):
-    for out, half in ((near_ref, place[1]), (far_ref, 1 - place[1])):
+def pack_memory_kernel(mk_ref, mv_ref, near_ref, far_ref):
+    yl = lax.axis_index("member") // 4
+    for out, half in ((near_ref, yl), (far_ref, 1 - yl)):
         cols = pl.ds(pl.multiple_of(half * HALF, HALF), HALF)
         out[0:MEM, :] = mk_ref[:, cols]
         out[MEM:, :] = mv_ref[:, cols]
 
 
-def pack_memory(place, mk, mv):
+def pack_memory(mk, mv):
     return pl.pallas_call(
         pack_memory_kernel,
-        in_specs=[SMEM, VMEM, VMEM],
+        in_specs=[VMEM, VMEM],
         out_specs=[VMEM] * 2,
         out_shape=[jax.ShapeDtypeStruct((2 * MEM, HALF), LOW)] * 2,
         cost_estimate=pl.CostEstimate(flops=0, bytes_accessed=1 << 20, transcendentals=0),
         name="pack_memory",
-    )(place, mk, mv)
+    )(mk, mv)
 
 
 def pack_queries_kernel(place, q_ref, g_ref, k_ref, v_ref, *rest):
@@ -155,10 +156,11 @@
     key_at = lax.broadcasted_iota(jnp.int32, (ROWS, ROWS), 0)
     query_at = lax.broadcasted_iota(jnp.int32, (ROWS, ROWS), 1)
     visible = key_at <= query_at
-    for head in range(2):
-        cols = slice(head * HEAD_DIM, (head + 1) * HEAD_DIM)
+    def one_head(head):
+        cols = pl.ds(pl.multiple_of(head * HEAD_DIM, HEAD_DIM), HEAD_DIM)
+        mine_cols = pl.ds(pl.multiple_of(place[1] * HALF + head * HEAD_DIM, HEAD_DIM), HEAD_DIM)
         q, g, k, v = [
-            [ref[:, cols], far_ref[n * ROWS : (n + 1) * ROWS, cols]]
+            [ref[:, mine_cols], far_ref[n * ROWS : (n + 1) * ROWS, cols]]
             for n, ref in enumerate((q_ref, g_ref, k_ref, v_ref))
         ]
         mk = jnp.concatenate([ref[n, 0:MEM, cols] for n in range(2) for ref in memory], axis=0)
@@ -209,25 +211,23 @@
             term_refs[n][0:MEM, cols] = dk[rows, :]
             term_refs[n][MEM:, cols] = dv[rows, :]
 
+    def two_heads(step, carry):
+        one_head(2 * step)
+        one_head(2 * step + 1)
+        return carry
+
+    lax.fori_loop(0, 4, two_heads, 0)
+
 
 def attention(place, q, g, k, v, far, memory):
-    def rows(count):
-        return pl.BlockSpec((count, PAIR), lambda h, s: (0, h))
-
-    mine = pl.BlockSpec((ROWS, PAIR), lambda h, s: (0, 4 * s[1] + h))
-    whole = pl.BlockSpec((2, 2 * MEM, PAIR), lambda h, s: (0, 0, h))
     shapes = [(2 * ROWS, HALF), (2 * ROWS, HALF), (ROWS, HALF), (2 * ROWS, HALF)]
     shapes += [(2 * MEM, HALF)] * 8
     return pl.pallas_call(
         attention_kernel,
-        grid_spec=pltpu.PrefetchScalarGridSpec(
-            num_scalar_prefetch=1,
-            grid=(4,),
-            in_specs=[mine] * 4 + [rows(4 * ROWS)] + [whole] * 4,
-            out_specs=[rows(shape[0]) for shape in shapes],
-        ),
+        in_specs=[SMEM] + [VMEM] * 9,
+        out_specs=[VMEM] * 12,
         out_shape=[jax.ShapeDtypeStruct(shape, LOW) for shape in shapes],
-        compiler_params=pltpu.CompilerParams(vmem_limit_bytes=24 << 20),
+        compiler_params=pltpu.CompilerParams(vmem_limit_bytes=28 << 20),
         cost_estimate=pl.CostEstimate(
             flops=int(8e9), bytes_accessed=5 << 20, transcendentals=2 << 20
         ),
@@ -411,7 +411,7 @@
     member = lax.axis_index("member")
     place = jnp.stack((core, member // 4, member, lax.rem(member, 4))).astype(jnp.int32)
 
-    own_memory, give_memory = pack_memory(place, memory_keys, memory_values)
+    own_memory, give_memory = pack_memory(memory_keys, memory_values)
     other_memory = shift(give_memory, "yl", 2, 1)
     give_queries = pack_queries(
         place, queries, grad_output, local_keys, local_values, [own_memory]

time: 131 us -> 129 us (0.985)
  waiting for transfers between devices: 56.5 us -> 54.8 us
  starting transfers between devices: 46 us -> 47.6 us
  Pallas kernels: 25.9 us -> 24.5 us
    ppermute x23, waiting for transfers between devices: 56.5 us -> 54.8 us  [shift(): return lax.ppermute(array, AXES, pairs(key, size, step))]
    ppermute x23, starting transfers between devices: 35.1 us -> 36.7 us  [shift(): return lax.ppermute(array, AXES, pairs(key, size, step))]
    pallas_call x2, Pallas kernels: 11.9 us -> 10.5 us  [the longest x1 8.66 us: attention(): pl.pallas_call(attention_kernel, in_specs=[SMEM] + [VMEM] * 9, out_specs=...]
where the time goes in v4:
time: 129 us
  waiting for transfers between devices  54.8 us (42%)
  starting transfers between devices  47.6 us (37%)
  Pallas kernels  24.5 us (19%)
    ppermute x23, waiting for transfers between devices, shift(): return lax.ppermute(array, AXES, pairs(key, size, step))  54.8 us
    ppermute x23, starting transfers between devices, shift(): return lax.ppermute(array, AXES, pairs(key, size, step))  36.7 us
    all_to_all x1, starting transfers between devices, local(): lax.all_to_all(both.reshape(32, 16, HALF), AXES, 0, 0, axis_index_groups=...  10.9 us
    pallas_call x1, Pallas kernels, attention(): pl.pallas_call(attention_kernel, in_specs=[SMEM] + [VMEM] * 9, out_specs=...  8.66 us
    pallas_call x1, Pallas kernels, hidden_pieces(): pl.pallas_call(hidden_kernel, in_specs=[SMEM, VMEM] + [ANY] * len(after),...  3.12 us
    pallas_call x1, Pallas kernels, pack_queries(): pl.pallas_call(pack_queries_kernel, grid_spec=pltpu.PrefetchScalarGridSpe...  3.04 us
  transfers between devices with their start and end apart: 24, of which 13 were waited for; matrix products, arithmetic and copies ran while one was open for 0% of the time, Pallas kernels for 15%

profile of v4, /device:TPU:1, one launch (start us, length us, event | category | flops | bytes accessed | tf_op | source)
XLA Modules:
  0.0 129.2 jit_solution(15684710676969133932)
XLA Ops:
  0.6 1.9 %pack_memory.1 = (bf16[128,1024]{1,0:T(8,128)(2,1)}, bf16[128,1024]{1,0:T(8,128)(2,1)}) custom-call(bf16[64,2048]{1,0:T(8,128)(2,1)} %mk_ref.1, bf16[64,2048]{1,0:T(8,128)(2,1)} %mv_ref.1), custom_call_target="tpu_custom_call" | custom-call | bytes 1048576 | tf_op jit(solution)/shard_map/pack_memory/pallas_call | solution.py:73
  2.5 2.1 %collective-permute-start = (bf16[128,1024]{1,0:T(8,128)(2,1)}, bf16[128,1024]{1,0:T(8,128)(2,1)S(1)}, u32[]{:S(2)}, u32[]{:S(2)}) collective-permute-start(bf16[128,1024]{1,0:T(8,128)(2,1)} %get-tuple-element.41), channel_id=1, source_target_pairs={{0,4},{1,5},{2,6},{3,7},{4,0},{5,1},{6,2},{7,3},{8,12},{9,13},{10,... | collective-permute-start | bytes 786440 | tf_op jit(solution)/shard_map/ppermute | solution.py:55
  5.2 3.0 %pack_queries.1.refs_0_ = bf16[512,1024]{1,0:T(8,128)(2,1)} custom-call(s32[4]{0:T(128)} %pad_add_fusion.place, bf16[128,2048]{1,0:T(8,128)(2,1)} %q_ref.3, bf16[128,2048]{1,0:T(8,128)(2,1)} %g_ref.3, bf16[128,2048]{1,0:T(8,128)(2,1)} %k_ref.3, bf16[128,2048]{1,0:T(8,128)(2,1)} %v_ref.3, bf16[128,1024]{1,0:T(8,128)(2,1)} %get-tuple-element.40.rest_0_.a_ref), custom_call_target="tpu_custom_call" | custom-call | bytes 2097152 | tf_op jit(solution)/shard_map/pack_queries/pallas_call | solution.py:91
  9.8 2.2 %collective-permute-start.1 = (bf16[512,1024]{1,0:T(8,128)(2,1)S(1)}, bf16[512,1024]{1,0:T(8,128)(2,1)S(1)}, u32[]{:S(2)}, u32[]{:S(2)}) collective-permute-start(bf16[512,1024]{1,0:T(8,128)(2,1)S(1)} %gate.2.refs_0_), channel_id=1, source_target_pairs={{0,4},{1,5},{2,6},{3,7},{4,0},{5,1},{6,2},{7,3},{8,12},{9,13},{10,... | collective-permute-start | bytes 3145736 | tf_op jit(solution)/shard_map/ppermute | solution.py:55
  12.0 2.7 %collective-permute-start.4 = (bf16[2,128,1024]{2,1,0:T(8,128)(2,1)S(1)}, bf16[2,128,1024]{2,1,0:T(8,128)(2,1)S(1)}, u32[]{:S(2)}, u32[]{:S(2)}) collective-permute-start(bf16[2,128,1024]{2,1,0:T(8,128)(2,1)S(1)} %join_memory.1.refs_1_.refs_0_), channel_id=1, source_target_pairs={{0,3},{1,0},{2,1},{3,2},{4,7},{5,4},{6,5},{7,6},{8,11},{9,8},{10,9... | collective-permute-start | bytes 1572872 | tf_op jit(solution)/shard_map/ppermute | solution.py:55
  15.8 3.1 %pack_hidden.1 = (bf16[2,512,128]{2,1,0:T(8,128)(2,1)S(1)}, bf16[2,512,128]{2,1,0:T(8,128)(2,1)S(1)}, bf16[2,512,128]{2,1,0:T(8,128)(2,1)S(1)}, bf16[2,512,128]{2,1,0:T(8,128)(2,1)S(1)}) custom-call(s32[4]{0:T(128)S(1)} %copy-done.11, bf16[128,4096]{1,0:T(8,128)(2,1)S(1)} %copy-done.12, bf16[512,1024]{1,0:T(8,128)(2,1)S(1)} %gate.2.refs_0_, ...), custom_call_target="tpu_custom_call" | custom-call | flops 1073741824 | bytes 2097152 | tf_op jit(solution)/shard_map/pack_hidden/pallas_call | solution.py:122
  18.9 6.3 %collective-permute-done.4.refs_3_.refs_5_ = bf16[2,128,1024]{2,1,0:T(8,128)(2,1)S(1)} collective-permute-done((bf16[2,128,1024]{2,1,0:T(8,128)(2,1)S(1)}, bf16[2,128,1024]{2,1,0:T(8,128)(2,1)S(1)}, u32[]{:S(2)}, u32[]{:S(2)}) %collective-permute-start.4) | collective-permute-done | bytes 524320 | tf_op jit(solution)/shard_map/ppermute | solution.py:55
  25.2 2.3 %collective-permute-done.3.refs_2_.refs_4_ = bf16[2,128,1024]{2,1,0:T(8,128)(2,1)S(1)} collective-permute-done((bf16[2,128,1024]{2,1,0:T(8,128)(2,1)S(1)}, bf16[2,128,1024]{2,1,0:T(8,128)(2,1)S(1)}, u32[]{:S(2)}, u32[]{:S(2)}) %collective-permute-start.3) | collective-permute-done | bytes 524320 | tf_op jit(solution)/shard_map/ppermute | solution.py:55
  27.6 9.7 %collective-permute-start.7 = (bf16[2,512,128]{2,1,0:T(8,128)(2,1)S(1)}, bf16[2,512,128]{2,1,0:T(8,128)(2,1)S(1)}, u32[]{:S(2)}, u32[]{:S(2)}) collective-permute-start(bf16[2,512,128]{2,1,0:T(8,128)(2,1)S(1)} %get-tuple-element.52), channel_id=1, source_target_pairs={{0,1},{1,2},{2,3},{3,0},{4,5},{5,6},{6,7},{7,4},{8,9},{9,10},{10,1... | collective-permute-start | bytes 786440 | tf_op jit(solution)/shard_map/ppermute | solution.py:55
  41.4 8.7 %attention_backward.1 = (bf16[256,1024]{1,0:T(8,128)(2,1)S(1)}, bf16[256,1024]{1,0:T(8,128)(2,1)S(1)}, bf16[128,1024]{1,0:T(8,128)(2,1)S(1)}, bf16[256,1024]{1,0...) custom-call(s32[4]{0:T(128)S(1)} %copy-done.11, ...), custom_call_target="tpu_custom_call" | custom-call | flops 8000000000 | bytes 5242880 | tf_op jit(solution)/shard_map/attention_backward/pallas_call | solution.py:225
  54.4 18.9 %collective-permute-done.5.refs_16_.first_ref = bf16[128,1024]{1,0:T(8,128)(2,1)S(1)} collective-permute-done((bf16[128,1024]{1,0:T(8,128)(2,1)S(1)}, bf16[128,1024]{1,0:T(8,128)(2,1)S(1)}, u32[]{:S(2)}, u32[]{:S(2)}) %collective-permute-start.5) | collective-permute-done | bytes 262176 | tf_op jit(solution)/shard_map/ppermute | solution.py:55
  73.3 5.6 %collective-permute-done.12.refs_7_ = bf16[256,1024]{1,0:T(8,128)(2,1)S(1)} collective-permute-done((bf16[256,1024]{1,0:T(8,128)(2,1)S(1)}, bf16[256,1024]{1,0:T(8,128)(2,1)S(1)}, u32[]{:S(2)}, u32[]{:S(2)}) %collective-permute-start.12) | collective-permute-done | bytes 524320 | tf_op jit(solution)/shard_map/ppermute | solution.py:55
  78.9 1.8 %product_give.1 = (bf16[512,1024]{1,0:T(8,128)(2,1)S(1)}, bf16[128,1024]{1,0:T(8,128)(2,1)S(1)}, bf16[128,1024]{1,0:T(8,128)(2,1)S(1)}, bf16[128,1024]{1,0:T(8,1...) custom-call(s32[4]{0:T(128)S(1)} %copy-done.11, ...), custom_call_target="tpu_custom_call", output_to_operand_aliasing={{1}: (11, {}), {2}: (12, {}), {3}: (13, {}), {4}: (14, {}),... | custom-call | flops 1000000000 | bytes 4194304 | tf_op jit(solution)/shard_map/product_give/pallas_call | solution.py:261
  81.3 1.8 %product_keep.1.a_ref = bf16[512,1024]{1,0:T(8,128)(2,1)S(1)} custom-call(s32[4]{0:T(128)S(1)} %copy-done.11, bf16[2,512,128]{2,1,0:T(8,128)(2,1)S(1)} %get-tuple-element.51.refs_0_, bf16[2,512,128]{2,1,0:T(8,128)(2,1)S(1)} %collective-permute-done.7.refs_0_.refs_1_, bf16[2,512,128]{2,1,0:T(8,128)(2,1)S(1)} %collective-permute-done.8.refs_1_.refs_2_, ...), custom_call_target="tpu_custom_call" | custom-call | flops 2000000000 | bytes 4194304 | tf_op jit(solution)/shard_map/product_keep/pallas_call | solution.py:275
  84.8 10.9 %all-to-all-start = ((bf16[32,16,1024]{2,1,0:T(8,128)(2,1)}), bf16[32,16,1024]{2,1,0:T(8,128)(2,1)S(1)}, u32[]{:S(2)}, u32[]{:S(2)}) async-start(bf16[32,16,1024]{2,1,0:T(8,128)(2,1)} %bitcast.4), calls=%async_computation | async-start | bytes 2097152 | tf_op jit(solution)/shard_map/all_to_all | solution.py:441
  99.0 2.1 %collective-permute-start.19 = (bf16[128,1024]{1,0:T(8,128)(2,1)S(1)}, bf16[128,1024]{1,0:T(8,128)(2,1)S(1)}, u32[]{:S(2)}, u32[]{:S(2)}) collective-permute-start(bf16[128,1024]{1,0:T(8,128)(2,1)S(1)} %get-tuple-element.65), channel_id=1, source_target_pairs={{0,3},{1,0},{2,1},{3,2},{4,7},{5,4},{6,5},{7,6},{8,11},{9,8},{10,9... | collective-permute-start | bytes 786440 | tf_op jit(solution)/shard_map/ppermute | solution.py:55
  101.2 2.0 %collective-permute-done.15.refs_1_ = bf16[128,1024]{1,0:T(8,128)(2,1)S(1)} collective-permute-done((bf16[128,1024]{1,0:T(8,128)(2,1)}, bf16[128,1024]{1,0:T(8,128)(2,1)S(1)}, u32[]{:S(2)}, u32[]{:S(2)}) %collective-permute-start.15) | collective-permute-done | bytes 262176 | tf_op jit(solution)/shard_map/ppermute | solution.py:55
  105.3 4.1 %collective-permute-start.21 = (bf16[128,1024]{1,0:T(8,128)(2,1)S(1)}, bf16[128,1024]{1,0:T(8,128)(2,1)S(1)}, u32[]{:S(2)}, u32[]{:S(2)}) collective-permute-start(bf16[128,1024]{1,0:T(8,128)(2,1)S(1)} %get-tuple-element.67), channel_id=1, source_target_pairs={{0,1},{1,2},{2,3},{3,0},{4,5},{5,6},{6,7},{7,4},{8,9},{9,10},{10,1... | collective-permute-start | bytes 786440 | tf_op jit(solution)/shard_map/ppermute | solution.py:55
  109.4 4.2 %collective-permute-done.17.refs_3_ = bf16[128,1024]{1,0:T(8,128)(2,1)S(1)} collective-permute-done((bf16[128,1024]{1,0:T(8,128)(2,1)}, bf16[128,1024]{1,0:T(8,128)(2,1)S(1)}, u32[]{:S(2)}, u32[]{:S(2)}) %collective-permute-start.17) | collective-permute-done | bytes 262176 | tf_op jit(solution)/shard_map/ppermute | solution.py:55
  113.7 1.6 %collective-permute-start.18 = (bf16[128,1024]{1,0:T(8,128)(2,1)S(1)}, bf16[128,1024]{1,0:T(8,128)(2,1)S(1)}, u32[]{:S(2)}, u32[]{:S(2)}) collective-permute-start(bf16[128,1024]{1,0:T(8,128)(2,1)S(1)} %memory_sum.1), channel_id=1, source_target_pairs={{0,4},{1,5},{2,6},{3,7},{4,0},{5,1},{6,2},{7,3},{8,12},{9,13},{10,... | collective-permute-start | bytes 786440 | tf_op jit(solution)/shard_map/ppermute | solution.py:55
  115.3 4.7 %collective-permute-done.6.back_ref = bf16[256,1024]{1,0:T(8,128)(2,1)S(1)} collective-permute-done((bf16[256,1024]{1,0:T(8,128)(2,1)}, bf16[256,1024]{1,0:T(8,128)(2,1)S(1)}, u32[]{:S(2)}, u32[]{:S(2)}) %collective-permute-start.6) | collective-permute-done | bytes 524320 | tf_op jit(solution)/shard_map/ppermute | solution.py:55
  120.0 3.3 %collective-permute-done.21.refs_3_ = bf16[128,1024]{1,0:T(8,128)(2,1)S(1)} collective-permute-done((bf16[128,1024]{1,0:T(8,128)(2,1)S(1)}, bf16[128,1024]{1,0:T(8,128)(2,1)S(1)}, u32[]{:S(2)}, u32[]{:S(2)}) %collective-permute-start.21) | collective-permute-done | bytes 262176 | tf_op jit(solution)/shard_map/ppermute | solution.py:55
  123.4 3.0 %collective-permute-done.18.got_ref = bf16[128,1024]{1,0:T(8,128)(2,1)S(1)} collective-permute-done((bf16[128,1024]{1,0:T(8,128)(2,1)S(1)}, bf16[128,1024]{1,0:T(8,128)(2,1)S(1)}, u32[]{:S(2)}, u32[]{:S(2)}) %collective-permute-start.18) | collective-permute-done | bytes 262176 | tf_op jit(solution)/shard_map/ppermute | solution.py:55
  126.3 2.0 %unpack_heads.1 = (bf16[128,2048]{1,0:T(8,128)(2,1)}, bf16[128,2048]{1,0:T(8,128)(2,1)}, bf16[128,2048]{1,0:T(8,128)(2,1)}, bf16[64,2048]{1,0:T(8,128)(2,1)}, bf16[64,2048]{1,0:T(8,128)(2,1)}) custom-call(s32[4]{0:T(128)S(1)} %copy-done.11, bf16[256,1024]{1,0:T(8,128)(2,1)S(1)} %get-tuple-element.42.refs_3_.refs_6_.gq_ref, ...), custom_call_target="tpu_custom_call" | custom-call | bytes 4194304 | tf_op jit(solution)/shard_map/unpack_heads/pallas_call | solution.py:375
  (67 shorter events, 20.3 us)
Async XLA Ops:
  2.5 7.2 %collective-permute-start = (bf16[128,1024]{1,0:T(8,128)(2,1)}, bf16[128,1024]{1,0:T(8,128)(2,1)S(1)}, u32[]{:S(2)}, u32[]{:S(2)}) collective-permute-start(bf16[128,1024]{1,0:T(8,128)(2,1)} %get-tuple-element.41), channel_id=1, source_target_pairs={{0,4},{1,5},{2,6},{3,7},{4,0},{5,1},{6,2},{7,3},{8,12},{9,13},{10,... | collective-permute-start | bytes 786440 | tf_op jit(solution)/shard_map/ppermute | solution.py:55
  9.8 31.6 %collective-permute-start.1 = (bf16[512,1024]{1,0:T(8,128)(2,1)S(1)}, bf16[512,1024]{1,0:T(8,128)(2,1)S(1)}, u32[]{:S(2)}, u32[]{:S(2)}) collective-permute-start(bf16[512,1024]{1,0:T(8,128)(2,1)S(1)} %gate.2.refs_0_), channel_id=1, source_target_pairs={{0,4},{1,5},{2,6},{3,7},{4,0},{5,1},{6,2},{7,3},{8,12},{9,13},{10,... | collective-permute-start | bytes 3145736 | tf_op jit(solution)/shard_map/ppermute | solution.py:55
  12.0 13.2 %collective-permute-start.4 = (bf16[2,128,1024]{2,1,0:T(8,128)(2,1)S(1)}, bf16[2,128,1024]{2,1,0:T(8,128)(2,1)S(1)}, u32[]{:S(2)}, u32[]{:S(2)}) collective-permute-start(bf16[2,128,1024]{2,1,0:T(8,128)(2,1)S(1)} %join_memory.1.refs_1_.refs_0_), channel_id=1, source_target_pairs={{0,3},{1,0},{2,1},{3,2},{4,7},{5,4},{6,5},{7,6},{8,11},{9,8},{10,9... | collective-permute-start | bytes 1572872 | tf_op jit(solution)/shard_map/ppermute | solution.py:55
  14.6 12.9 %collective-permute-start.3 = (bf16[2,128,1024]{2,1,0:T(8,128)(2,1)S(1)}, bf16[2,128,1024]{2,1,0:T(8,128)(2,1)S(1)}, u32[]{:S(2)}, u32[]{:S(2)}) collective-permute-start(bf16[2,128,1024]{2,1,0:T(8,128)(2,1)S(1)} %join_memory.1.refs_1_.refs_0_), channel_id=1, source_target_pairs={{0,2},{1,3},{2,0},{3,1},{4,6},{5,7},{6,4},{7,5},{8,10},{9,11},{10,... | collective-permute-start | bytes 1572872 | tf_op jit(solution)/shard_map/ppermute | solution.py:55
  15.2 26.1 %collective-permute-start.2 = (bf16[2,128,1024]{2,1,0:T(8,128)(2,1)S(1)}, bf16[2,128,1024]{2,1,0:T(8,128)(2,1)S(1)}, u32[]{:S(2)}, u32[]{:S(2)}) collective-permute-start(bf16[2,128,1024]{2,1,0:T(8,128)(2,1)S(1)} %join_memory.1.refs_1_.refs_0_), channel_id=1, source_target_pairs={{0,1},{1,2},{2,3},{3,0},{4,5},{5,6},{6,7},{7,4},{8,9},{9,10},{10,1... | collective-permute-start | bytes 1572872 | tf_op jit(solution)/shard_map/ppermute | solution.py:55
  27.6 22.6 %collective-permute-start.7 = (bf16[2,512,128]{2,1,0:T(8,128)(2,1)S(1)}, bf16[2,512,128]{2,1,0:T(8,128)(2,1)S(1)}, u32[]{:S(2)}, u32[]{:S(2)}) collective-permute-start(bf16[2,512,128]{2,1,0:T(8,128)(2,1)S(1)} %get-tuple-element.52), channel_id=1, source_target_pairs={{0,1},{1,2},{2,3},{3,0},{4,5},{5,6},{6,7},{7,4},{8,9},{9,10},{10,1... | collective-permute-start | bytes 786440 | tf_op jit(solution)/shard_map/ppermute | solution.py:55
  37.2 12.9 %collective-permute-start.8 = (bf16[2,512,128]{2,1,0:T(8,128)(2,1)S(1)}, bf16[2,512,128]{2,1,0:T(8,128)(2,1)S(1)}, u32[]{:S(2)}, u32[]{:S(2)}) collective-permute-start(bf16[2,512,128]{2,1,0:T(8,128)(2,1)S(1)} %get-tuple-element.53), channel_id=1, source_target_pairs={{0,2},{1,3},{2,0},{3,1},{4,6},{5,7},{6,4},{7,5},{8,10},{9,11},{10,... | collective-permute-start | bytes 786440 | tf_op jit(solution)/shard_map/ppermute | solution.py:55
  38.3 11.8 %collective-permute-start.9 = (bf16[2,512,128]{2,1,0:T(8,128)(2,1)S(1)}, bf16[2,512,128]{2,1,0:T(8,128)(2,1)S(1)}, u32[]{:S(2)}, u32[]{:S(2)}) collective-permute-start(bf16[2,512,128]{2,1,0:T(8,128)(2,1)S(1)} %get-tuple-element.54), channel_id=1, source_target_pairs={{0,3},{1,0},{2,1},{3,2},{4,7},{5,4},{6,5},{7,6},{8,11},{9,8},{10,9... | collective-permute-start | bytes 786440 | tf_op jit(solution)/shard_map/ppermute | solution.py:55
  41.2 8.9 %collective-permute-start.10 = (bf16[2,512,128]{2,1,0:T(8,128)(2,1)S(1)}, bf16[2,512,128]{2,1,0:T(8,128)(2,1)S(1)}, u32[]{:S(2)}, u32[]{:S(2)}) collective-permute-start(bf16[2,512,128]{2,1,0:T(8,128)(2,1)S(1)} %get-tuple-element.51.refs_0_), channel_id=1, source_target_pairs={{0,4},{1,5},{2,6},{3,7},{4,0},{5,1},{6,2},{7,3},{8,12},{9,13},{10,... | collective-permute-start | bytes 786440 | tf_op jit(solution)/shard_map/ppermute | solution.py:55
  51.0 27.9 %collective-permute-start.11 = (bf16[3,2,512,128]{3,2,1,0:T(8,128)(2,1)S(1)}, bf16[3,2,512,128]{3,2,1,0:T(8,128)(2,1)S(1)}, u32[]{:S(2)}, u32[]{:S(2)}) collective-permute-start(bf16[3,2,512,128]{3,2,1,0:T(8,128)(2,1)S(1)} %stack_hidden.1), channel_id=1, source_target_pairs={{0,4},{1,5},{2,6},{3,7},{4,0},{5,1},{6,2},{7,3},{8,12},{9,13},{10,... | collective-permute-start | bytes 2359304 | tf_op jit(solution)/shard_map/ppermute | solution.py:55
  52.3 21.0 %collective-permute-start.14 = (bf16[256,1024]{1,0:T(8,128)(2,1)S(1)}, bf16[256,1024]{1,0:T(8,128)(2,1)S(1)}, u32[]{:S(2)}, u32[]{:S(2)}) collective-permute-start(bf16[256,1024]{1,0:T(8,128)(2,1)S(1)} %get-tuple-element.42.refs_3_.refs_6_.gq_ref), channel_id=1, source_target_pairs={{0,3},{1,0},{2,1},{3,2},{4,7},{5,4},{6,5},{7,6},{8,11},{9,8},{10,9... | collective-permute-start | bytes 1572872 | tf_op jit(solution)/shard_map/ppermute | solution.py:55
  52.3 21.0 %collective-permute-start.13 = (bf16[256,1024]{1,0:T(8,128)(2,1)S(1)}, bf16[256,1024]{1,0:T(8,128)(2,1)S(1)}, u32[]{:S(2)}, u32[]{:S(2)}) collective-permute-start(bf16[256,1024]{1,0:T(8,128)(2,1)S(1)} %get-tuple-element.42.refs_3_.refs_6_.gq_ref), channel_id=1, source_target_pairs={{0,2},{1,3},{2,0},{3,1},{4,6},{5,7},{6,4},{7,5},{8,10},{9,11},{10,... | collective-permute-start | bytes 1572872 | tf_op jit(solution)/shard_map/ppermute | solution.py:55
  53.1 25.7 %collective-permute-start.12 = (bf16[256,1024]{1,0:T(8,128)(2,1)S(1)}, bf16[256,1024]{1,0:T(8,128)(2,1)S(1)}, u32[]{:S(2)}, u32[]{:S(2)}) collective-permute-start(bf16[256,1024]{1,0:T(8,128)(2,1)S(1)} %get-tuple-element.42.refs_3_.refs_6_.gq_ref), channel_id=1, source_target_pairs={{0,1},{1,2},{2,3},{3,0},{4,5},{5,6},{6,7},{7,4},{8,9},{9,10},{10,1... | collective-permute-start | bytes 1572872 | tf_op jit(solution)/shard_map/ppermute | solution.py:55
  53.7 19.5 %collective-permute-start.5 = (bf16[128,1024]{1,0:T(8,128)(2,1)S(1)}, bf16[128,1024]{1,0:T(8,128)(2,1)S(1)}, u32[]{:S(2)}, u32[]{:S(2)}) collective-permute-start(bf16[128,1024]{1,0:T(8,128)(2,1)S(1)} %get-tuple-element.44), channel_id=1, source_target_pairs={{0,4},{1,5},{2,6},{3,7},{4,0},{5,1},{6,2},{7,3},{8,12},{9,13},{10,... | collective-permute-start | bytes 786440 | tf_op jit(solution)/shard_map/ppermute | solution.py:55
  80.7 2.9 %collective-permute-start.22 = (bf16[512,1024]{1,0:T(8,128)(2,1)S(1)}, bf16[512,1024]{1,0:T(8,128)(2,1)S(1)}, u32[]{:S(2)}, u32[]{:S(2)}) collective-permute-start(bf16[512,1024]{1,0:T(8,128)(2,1)S(1)} %get-tuple-element.73.refs_10_), channel_id=1, source_target_pairs={{0,8},{1,9},{2,10},{3,11},{4,12},{5,13},{6,14},{7,15},{8,0},{9,1},... | collective-permute-start | bytes 3145736 | tf_op jit(solution)/shard_map/ppermute | solution.py:55
  84.8 43.6 %all-to-all-start = ((bf16[32,16,1024]{2,1,0:T(8,128)(2,1)}), bf16[32,16,1024]{2,1,0:T(8,128)(2,1)S(1)}, u32[]{:S(2)}, u32[]{:S(2)}) async-start(bf16[32,16,1024]{2,1,0:T(8,128)(2,1)} %bitcast.4), calls=%async_computation | async-start | bytes 2097152 | tf_op jit(solution)/shard_map/all_to_all | solution.py:441
  95.7 7.5 %collective-permute-start.15 = (bf16[128,1024]{1,0:T(8,128)(2,1)}, bf16[128,1024]{1,0:T(8,128)(2,1)S(1)}, u32[]{:S(2)}, u32[]{:S(2)}) collective-permute-start(bf16[128,1024]{1,0:T(8,128)(2,1)} %copy-done.6), channel_id=1, source_target_pairs={{0,3},{1,0},{2,1},{3,2},{4,7},{5,4},{6,5},{7,6},{8,11},{9,8},{10,9... | collective-permute-start | bytes 786440 | tf_op jit(solution)/shard_map/ppermute | solution.py:55
  96.7 8.6 %collective-permute-start.16 = (bf16[128,1024]{1,0:T(8,128)(2,1)}, bf16[128,1024]{1,0:T(8,128)(2,1)S(1)}, u32[]{:S(2)}, u32[]{:S(2)}) collective-permute-start(bf16[128,1024]{1,0:T(8,128)(2,1)} %copy-done.7), channel_id=1, source_target_pairs={{0,2},{1,3},{2,0},{3,1},{4,6},{5,7},{6,4},{7,5},{8,10},{9,11},{10,... | collective-permute-start | bytes 786440 | tf_op jit(solution)/shard_map/ppermute | solution.py:55
  97.2 16.3 %collective-permute-start.17 = (bf16[128,1024]{1,0:T(8,128)(2,1)}, bf16[128,1024]{1,0:T(8,128)(2,1)S(1)}, u32[]{:S(2)}, u32[]{:S(2)}) collective-permute-start(bf16[128,1024]{1,0:T(8,128)(2,1)} %copy-done.8), channel_id=1, source_target_pairs={{0,1},{1,2},{2,3},{3,0},{4,5},{5,6},{6,7},{7,4},{8,9},{9,10},{10,1... | collective-permute-start | bytes 786440 | tf_op jit(solution)/shard_map/ppermute | solution.py:55
  97.8 22.2 %collective-permute-start.6 = (bf16[256,1024]{1,0:T(8,128)(2,1)}, bf16[256,1024]{1,0:T(8,128)(2,1)S(1)}, u32[]{:S(2)}, u32[]{:S(2)}) collective-permute-start(bf16[256,1024]{1,0:T(8,128)(2,1)} %copy-done.13), channel_id=1, source_target_pairs={{0,4},{1,5},{2,6},{3,7},{4,0},{5,1},{6,2},{7,3},{8,12},{9,13},{10,... | collective-permute-start | bytes 1572872 | tf_op jit(solution)/shard_map/ppermute | solution.py:55
  99.0 21.0 %collective-permute-start.19 = (bf16[128,1024]{1,0:T(8,128)(2,1)S(1)}, bf16[128,1024]{1,0:T(8,128)(2,1)S(1)}, u32[]{:S(2)}, u32[]{:S(2)}) collective-permute-start(bf16[128,1024]{1,0:T(8,128)(2,1)S(1)} %get-tuple-element.65), channel_id=1, source_target_pairs={{0,3},{1,0},{2,1},{3,2},{4,7},{5,4},{6,5},{7,6},{8,11},{9,8},{10,9... | collective-permute-start | bytes 786440 | tf_op jit(solution)/shard_map/ppermute | solution.py:55
  103.2 16.8 %collective-permute-start.20 = (bf16[128,1024]{1,0:T(8,128)(2,1)S(1)}, bf16[128,1024]{1,0:T(8,128)(2,1)S(1)}, u32[]{:S(2)}, u32[]{:S(2)}) collective-permute-start(bf16[128,1024]{1,0:T(8,128)(2,1)S(1)} %get-tuple-element.66), channel_id=1, source_target_pairs={{0,2},{1,3},{2,0},{3,1},{4,6},{5,7},{6,4},{7,5},{8,10},{9,11},{10,... | collective-permute-start | bytes 786440 | tf_op jit(solution)/shard_map/ppermute | solution.py:55
  105.3 18.1 %collective-permute-start.21 = (bf16[128,1024]{1,0:T(8,128)(2,1)S(1)}, bf16[128,1024]{1,0:T(8,128)(2,1)S(1)}, u32[]{:S(2)}, u32[]{:S(2)}) collective-permute-start(bf16[128,1024]{1,0:T(8,128)(2,1)S(1)} %get-tuple-element.67), channel_id=1, source_target_pairs={{0,1},{1,2},{2,3},{3,0},{4,5},{5,6},{6,7},{7,4},{8,9},{9,10},{10,1... | collective-permute-start | bytes 786440 | tf_op jit(solution)/shard_map/ppermute | solution.py:55
  113.7 12.7 %collective-permute-start.18 = (bf16[128,1024]{1,0:T(8,128)(2,1)S(1)}, bf16[128,1024]{1,0:T(8,128)(2,1)S(1)}, u32[]{:S(2)}, u32[]{:S(2)}) collective-permute-start(bf16[128,1024]{1,0:T(8,128)(2,1)S(1)} %memory_sum.1), channel_id=1, source_target_pairs={{0,4},{1,5},{2,6},{3,7},{4,0},{5,1},{6,2},{7,3},{8,12},{9,13},{10,... | collective-permute-start | bytes 786440 | tf_op jit(solution)/shard_map/ppermute | solution.py:55
  (14 other events, 95.1 us)

commit v5 on v4

--- a/solution.py
+++ b/solution.py
@@ -211,12 +211,12 @@
             term_refs[n][0:MEM, cols] = dk[rows, :]
             term_refs[n][MEM:, cols] = dv[rows, :]
 
-    def two_heads(step, carry):
-        one_head(2 * step)
-        one_head(2 * step + 1)
+    def four_heads(step, carry):
+        for n in range(4):
+            one_head(4 * step + n)
         return carry
 
-    lax.fori_loop(0, 4, two_heads, 0)
+    lax.fori_loop(0, 2, four_heads, 0)
 
 
 def attention(place, q, g, k, v, far, memory):

time: 129 us -> 129 us (level)
  starting transfers between devices: 47.6 us -> 49.3 us
  waiting for transfers between devices: 54.8 us -> 53.2 us
    ppermute x23, starting transfers between devices: 36.7 us -> 38.4 us  [shift(): return lax.ppermute(array, AXES, pairs(key, size, step))]
    ppermute x23, waiting for transfers between devices: 54.8 us -> 53.2 us  [shift(): return lax.ppermute(array, AXES, pairs(key, size, step))]
  transfers between devices with their start and end apart: 24 -> 24, of which waited for: 13 -> 13; matrix products, arithmetic and copies ran while one was open for 0% -> 0% of each run, Pallas kernels for 15% -> 14%
where the time goes in v5:
time: 129 us
  waiting for transfers between devices  53.2 us (41%)
  starting transfers between devices  49.3 us (38%)
  Pallas kernels  24.2 us (19%)
    ppermute x23, waiting for transfers between devices, shift(): return lax.ppermute(array, AXES, pairs(key, size, step))  53.2 us
    ppermute x23, starting transfers between devices, shift(): return lax.ppermute(array, AXES, pairs(key, size, step))  38.4 us
    all_to_all x1, starting transfers between devices, local(): lax.all_to_all(both.reshape(32, 16, HALF), AXES, 0, 0, axis_index_groups=...  10.9 us
    pallas_call x1, Pallas kernels, attention(): pl.pallas_call(attention_kernel, in_specs=[SMEM] + [VMEM] * 9, out_specs=...  8.34 us
    pallas_call x1, Pallas kernels, hidden_pieces(): pl.pallas_call(hidden_kernel, in_specs=[SMEM, VMEM] + [ANY] * len(after),...  3.12 us
    pallas_call x1, Pallas kernels, pack_queries(): pl.pallas_call(pack_queries_kernel, grid_spec=pltpu.PrefetchScalarGridSpe...  3.04 us
  transfers between devices with their start and end apart: 24, of which 13 were waited for; matrix products, arithmetic and copies ran while one was open for 0% of the time, Pallas kernels for 14%

profile of v5, /device:TPU:1, one launch (start us, length us, event | category | flops | bytes accessed | tf_op | source)
XLA Modules:
  0.0 128.9 jit_solution(16350006089634377771)
XLA Ops:
  0.6 1.9 %pack_memory.1 = (bf16[128,1024]{1,0:T(8,128)(2,1)}, bf16[128,1024]{1,0:T(8,128)(2,1)}) custom-call(bf16[64,2048]{1,0:T(8,128)(2,1)} %mk_ref.1, bf16[64,2048]{1,0:T(8,128)(2,1)} %mv_ref.1), custom_call_target="tpu_custom_call" | custom-call | bytes 1048576 | tf_op jit(solution)/shard_map/pack_memory/pallas_call | solution.py:73
  2.5 2.1 %collective-permute-start = (bf16[128,1024]{1,0:T(8,128)(2,1)}, bf16[128,1024]{1,0:T(8,128)(2,1)S(1)}, u32[]{:S(2)}, u32[]{:S(2)}) collective-permute-start(bf16[128,1024]{1,0:T(8,128)(2,1)} %get-tuple-element.41), channel_id=1, source_target_pairs={{0,4},{1,5},{2,6},{3,7},{4,0},{5,1},{6,2},{7,3},{8,12},{9,13},{10,... | collective-permute-start | bytes 786440 | tf_op jit(solution)/shard_map/ppermute | solution.py:55
  5.2 3.0 %pack_queries.1.refs_0_ = bf16[512,1024]{1,0:T(8,128)(2,1)} custom-call(s32[4]{0:T(128)} %pad_add_fusion.place, bf16[128,2048]{1,0:T(8,128)(2,1)} %q_ref.3, bf16[128,2048]{1,0:T(8,128)(2,1)} %g_ref.3, bf16[128,2048]{1,0:T(8,128)(2,1)} %k_ref.3, bf16[128,2048]{1,0:T(8,128)(2,1)} %v_ref.3, bf16[128,1024]{1,0:T(8,128)(2,1)} %get-tuple-element.40.rest_0_.a_ref), custom_call_target="tpu_custom_call" | custom-call | bytes 2097152 | tf_op jit(solution)/shard_map/pack_queries/pallas_call | solution.py:91
  9.8 2.2 %collective-permute-start.1 = (bf16[512,1024]{1,0:T(8,128)(2,1)S(1)}, bf16[512,1024]{1,0:T(8,128)(2,1)S(1)}, u32[]{:S(2)}, u32[]{:S(2)}) collective-permute-start(bf16[512,1024]{1,0:T(8,128)(2,1)S(1)} %gate.2.refs_0_), channel_id=1, source_target_pairs={{0,4},{1,5},{2,6},{3,7},{4,0},{5,1},{6,2},{7,3},{8,12},{9,13},{10,... | collective-permute-start | bytes 3145736 | tf_op jit(solution)/shard_map/ppermute | solution.py:55
  12.0 2.7 %collective-permute-start.4 = (bf16[2,128,1024]{2,1,0:T(8,128)(2,1)S(1)}, bf16[2,128,1024]{2,1,0:T(8,128)(2,1)S(1)}, u32[]{:S(2)}, u32[]{:S(2)}) collective-permute-start(bf16[2,128,1024]{2,1,0:T(8,128)(2,1)S(1)} %join_memory.1.refs_1_.refs_0_), channel_id=1, source_target_pairs={{0,3},{1,0},{2,1},{3,2},{4,7},{5,4},{6,5},{7,6},{8,11},{9,8},{10,9... | collective-permute-start | bytes 1572872 | tf_op jit(solution)/shard_map/ppermute | solution.py:55
  15.8 3.1 %pack_hidden.1 = (bf16[2,512,128]{2,1,0:T(8,128)(2,1)S(1)}, bf16[2,512,128]{2,1,0:T(8,128)(2,1)S(1)}, bf16[2,512,128]{2,1,0:T(8,128)(2,1)S(1)}, bf16[2,512,128]{2,1,0:T(8,128)(2,1)S(1)}) custom-call(s32[4]{0:T(128)S(1)} %copy-done.11, bf16[128,4096]{1,0:T(8,128)(2,1)S(1)} %copy-done.12, bf16[512,1024]{1,0:T(8,128)(2,1)S(1)} %gate.2.refs_0_, ...), custom_call_target="tpu_custom_call" | custom-call | flops 1073741824 | bytes 2097152 | tf_op jit(solution)/shard_map/pack_hidden/pallas_call | solution.py:122
  18.9 6.3 %collective-permute-done.4.refs_3_.refs_5_ = bf16[2,128,1024]{2,1,0:T(8,128)(2,1)S(1)} collective-permute-done((bf16[2,128,1024]{2,1,0:T(8,128)(2,1)S(1)}, bf16[2,128,1024]{2,1,0:T(8,128)(2,1)S(1)}, u32[]{:S(2)}, u32[]{:S(2)}) %collective-permute-start.4) | collective-permute-done | bytes 524320 | tf_op jit(solution)/shard_map/ppermute | solution.py:55
  25.2 2.3 %collective-permute-done.3.refs_2_.refs_4_ = bf16[2,128,1024]{2,1,0:T(8,128)(2,1)S(1)} collective-permute-done((bf16[2,128,1024]{2,1,0:T(8,128)(2,1)S(1)}, bf16[2,128,1024]{2,1,0:T(8,128)(2,1)S(1)}, u32[]{:S(2)}, u32[]{:S(2)}) %collective-permute-start.3) | collective-permute-done | bytes 524320 | tf_op jit(solution)/shard_map/ppermute | solution.py:55
  27.6 9.7 %collective-permute-start.7 = (bf16[2,512,128]{2,1,0:T(8,128)(2,1)S(1)}, bf16[2,512,128]{2,1,0:T(8,128)(2,1)S(1)}, u32[]{:S(2)}, u32[]{:S(2)}) collective-permute-start(bf16[2,512,128]{2,1,0:T(8,128)(2,1)S(1)} %get-tuple-element.52), channel_id=1, source_target_pairs={{0,1},{1,2},{2,3},{3,0},{4,5},{5,6},{6,7},{7,4},{8,9},{9,10},{10,1... | collective-permute-start | bytes 786440 | tf_op jit(solution)/shard_map/ppermute | solution.py:55
  41.4 8.3 %attention_backward.1 = (bf16[256,1024]{1,0:T(8,128)(2,1)S(1)}, bf16[256,1024]{1,0:T(8,128)(2,1)S(1)}, bf16[128,1024]{1,0:T(8,128)(2,1)S(1)}, bf16[256,1024]{1,0...) custom-call(s32[4]{0:T(128)S(1)} %copy-done.11, ...), custom_call_target="tpu_custom_call" | custom-call | flops 8000000000 | bytes 5242880 | tf_op jit(solution)/shard_map/attention_backward/pallas_call | solution.py:225
  54.6 18.0 %collective-permute-done.5.refs_16_.first_ref = bf16[128,1024]{1,0:T(8,128)(2,1)S(1)} collective-permute-done((bf16[128,1024]{1,0:T(8,128)(2,1)S(1)}, bf16[128,1024]{1,0:T(8,128)(2,1)S(1)}, u32[]{:S(2)}, u32[]{:S(2)}) %collective-permute-start.5) | collective-permute-done | bytes 262176 | tf_op jit(solution)/shard_map/ppermute | solution.py:55
  72.6 5.9 %collective-permute-done.12.refs_7_ = bf16[256,1024]{1,0:T(8,128)(2,1)S(1)} collective-permute-done((bf16[256,1024]{1,0:T(8,128)(2,1)S(1)}, bf16[256,1024]{1,0:T(8,128)(2,1)S(1)}, u32[]{:S(2)}, u32[]{:S(2)}) %collective-permute-start.12) | collective-permute-done | bytes 524320 | tf_op jit(solution)/shard_map/ppermute | solution.py:55
  78.5 1.8 %product_give.1 = (bf16[512,1024]{1,0:T(8,128)(2,1)S(1)}, bf16[128,1024]{1,0:T(8,128)(2,1)S(1)}, bf16[128,1024]{1,0:T(8,128)(2,1)S(1)}, bf16[128,1024]{1,0:T(8,1...) custom-call(s32[4]{0:T(128)S(1)} %copy-done.11, ...), custom_call_target="tpu_custom_call", output_to_operand_aliasing={{1}: (11, {}), {2}: (12, {}), {3}: (13, {}), {4}: (14, {}),... | custom-call | flops 1000000000 | bytes 4194304 | tf_op jit(solution)/shard_map/product_give/pallas_call | solution.py:261
  81.0 1.8 %product_keep.1.a_ref = bf16[512,1024]{1,0:T(8,128)(2,1)S(1)} custom-call(s32[4]{0:T(128)S(1)} %copy-done.11, bf16[2,512,128]{2,1,0:T(8,128)(2,1)S(1)} %get-tuple-element.51.refs_0_, bf16[2,512,128]{2,1,0:T(8,128)(2,1)S(1)} %collective-permute-done.7.refs_0_.refs_1_, bf16[2,512,128]{2,1,0:T(8,128)(2,1)S(1)} %collective-permute-done.8.refs_1_.refs_2_, ...), custom_call_target="tpu_custom_call" | custom-call | flops 2000000000 | bytes 4194304 | tf_op jit(solution)/shard_map/product_keep/pallas_call | solution.py:275
  84.5 10.9 %all-to-all-start = ((bf16[32,16,1024]{2,1,0:T(8,128)(2,1)}), bf16[32,16,1024]{2,1,0:T(8,128)(2,1)S(1)}, u32[]{:S(2)}, u32[]{:S(2)}) async-start(bf16[32,16,1024]{2,1,0:T(8,128)(2,1)} %bitcast.4), calls=%async_computation | async-start | bytes 2097152 | tf_op jit(solution)/shard_map/all_to_all | solution.py:441
  99.0 2.3 %collective-permute-start.19 = (bf16[128,1024]{1,0:T(8,128)(2,1)S(1)}, bf16[128,1024]{1,0:T(8,128)(2,1)S(1)}, u32[]{:S(2)}, u32[]{:S(2)}) collective-permute-start(bf16[128,1024]{1,0:T(8,128)(2,1)S(1)} %get-tuple-element.65), channel_id=1, source_target_pairs={{0,3},{1,0},{2,1},{3,2},{4,7},{5,4},{6,5},{7,6},{8,11},{9,8},{10,9... | collective-permute-start | bytes 786440 | tf_op jit(solution)/shard_map/ppermute | solution.py:55
  101.3 1.5 %collective-permute-done.15.refs_1_ = bf16[128,1024]{1,0:T(8,128)(2,1)S(1)} collective-permute-done((bf16[128,1024]{1,0:T(8,128)(2,1)}, bf16[128,1024]{1,0:T(8,128)(2,1)S(1)}, u32[]{:S(2)}, u32[]{:S(2)}) %collective-permute-start.15) | collective-permute-done | bytes 262176 | tf_op jit(solution)/shard_map/ppermute | solution.py:55
  105.0 4.4 %collective-permute-start.21 = (bf16[128,1024]{1,0:T(8,128)(2,1)S(1)}, bf16[128,1024]{1,0:T(8,128)(2,1)S(1)}, u32[]{:S(2)}, u32[]{:S(2)}) collective-permute-start(bf16[128,1024]{1,0:T(8,128)(2,1)S(1)} %get-tuple-element.67), channel_id=1, source_target_pairs={{0,1},{1,2},{2,3},{3,0},{4,5},{5,6},{6,7},{7,4},{8,9},{9,10},{10,1... | collective-permute-start | bytes 786440 | tf_op jit(solution)/shard_map/ppermute | solution.py:55
  109.4 3.8 %collective-permute-done.17.refs_3_ = bf16[128,1024]{1,0:T(8,128)(2,1)S(1)} collective-permute-done((bf16[128,1024]{1,0:T(8,128)(2,1)}, bf16[128,1024]{1,0:T(8,128)(2,1)S(1)}, u32[]{:S(2)}, u32[]{:S(2)}) %collective-permute-start.17) | collective-permute-done | bytes 262176 | tf_op jit(solution)/shard_map/ppermute | solution.py:55
  113.4 1.6 %collective-permute-start.18 = (bf16[128,1024]{1,0:T(8,128)(2,1)S(1)}, bf16[128,1024]{1,0:T(8,128)(2,1)S(1)}, u32[]{:S(2)}, u32[]{:S(2)}) collective-permute-start(bf16[128,1024]{1,0:T(8,128)(2,1)S(1)} %memory_sum.1), channel_id=1, source_target_pairs={{0,4},{1,5},{2,6},{3,7},{4,0},{5,1},{6,2},{7,3},{8,12},{9,13},{10,... | collective-permute-start | bytes 786440 | tf_op jit(solution)/shard_map/ppermute | solution.py:55
  115.0 4.9 %collective-permute-done.6.back_ref = bf16[256,1024]{1,0:T(8,128)(2,1)S(1)} collective-permute-done((bf16[256,1024]{1,0:T(8,128)(2,1)}, bf16[256,1024]{1,0:T(8,128)(2,1)S(1)}, u32[]{:S(2)}, u32[]{:S(2)}) %collective-permute-start.6) | collective-permute-done | bytes 524320 | tf_op jit(solution)/shard_map/ppermute | solution.py:55
  119.8 3.2 %collective-permute-done.21.refs_3_ = bf16[128,1024]{1,0:T(8,128)(2,1)S(1)} collective-permute-done((bf16[128,1024]{1,0:T(8,128)(2,1)S(1)}, bf16[128,1024]{1,0:T(8,128)(2,1)S(1)}, u32[]{:S(2)}, u32[]{:S(2)}) %collective-permute-start.21) | collective-permute-done | bytes 262176 | tf_op jit(solution)/shard_map/ppermute | solution.py:55
  123.0 3.1 %collective-permute-done.18.got_ref = bf16[128,1024]{1,0:T(8,128)(2,1)S(1)} collective-permute-done((bf16[128,1024]{1,0:T(8,128)(2,1)S(1)}, bf16[128,1024]{1,0:T(8,128)(2,1)S(1)}, u32[]{:S(2)}, u32[]{:S(2)}) %collective-permute-start.18) | collective-permute-done | bytes 262176 | tf_op jit(solution)/shard_map/ppermute | solution.py:55
  126.1 2.0 %unpack_heads.1 = (bf16[128,2048]{1,0:T(8,128)(2,1)}, bf16[128,2048]{1,0:T(8,128)(2,1)}, bf16[128,2048]{1,0:T(8,128)(2,1)}, bf16[64,2048]{1,0:T(8,128)(2,1)}, bf16[64,2048]{1,0:T(8,128)(2,1)}) custom-call(s32[4]{0:T(128)S(1)} %copy-done.11, bf16[256,1024]{1,0:T(8,128)(2,1)S(1)} %get-tuple-element.42.refs_3_.refs_6_.gq_ref, ...), custom_call_target="tpu_custom_call" | custom-call | bytes 4194304 | tf_op jit(solution)/shard_map/unpack_heads/pallas_call | solution.py:375
  (67 shorter events, 21.2 us)
Async XLA Ops:
  2.5 7.2 %collective-permute-start = (bf16[128,1024]{1,0:T(8,128)(2,1)}, bf16[128,1024]{1,0:T(8,128)(2,1)S(1)}, u32[]{:S(2)}, u32[]{:S(2)}) collective-permute-start(bf16[128,1024]{1,0:T(8,128)(2,1)} %get-tuple-element.41), channel_id=1, source_target_pairs={{0,4},{1,5},{2,6},{3,7},{4,0},{5,1},{6,2},{7,3},{8,12},{9,13},{10,... | collective-permute-start | bytes 786440 | tf_op jit(solution)/shard_map/ppermute | solution.py:55
  9.8 31.6 %collective-permute-start.1 = (bf16[512,1024]{1,0:T(8,128)(2,1)S(1)}, bf16[512,1024]{1,0:T(8,128)(2,1)S(1)}, u32[]{:S(2)}, u32[]{:S(2)}) collective-permute-start(bf16[512,1024]{1,0:T(8,128)(2,1)S(1)} %gate.2.refs_0_), channel_id=1, source_target_pairs={{0,4},{1,5},{2,6},{3,7},{4,0},{5,1},{6,2},{7,3},{8,12},{9,13},{10,... | collective-permute-start | bytes 3145736 | tf_op jit(solution)/shard_map/ppermute | solution.py:55
  12.0 13.2 %collective-permute-start.4 = (bf16[2,128,1024]{2,1,0:T(8,128)(2,1)S(1)}, bf16[2,128,1024]{2,1,0:T(8,128)(2,1)S(1)}, u32[]{:S(2)}, u32[]{:S(2)}) collective-permute-start(bf16[2,128,1024]{2,1,0:T(8,128)(2,1)S(1)} %join_memory.1.refs_1_.refs_0_), channel_id=1, source_target_pairs={{0,3},{1,0},{2,1},{3,2},{4,7},{5,4},{6,5},{7,6},{8,11},{9,8},{10,9... | collective-permute-start | bytes 1572872 | tf_op jit(solution)/shard_map/ppermute | solution.py:55
  14.6 12.9 %collective-permute-start.3 = (bf16[2,128,1024]{2,1,0:T(8,128)(2,1)S(1)}, bf16[2,128,1024]{2,1,0:T(8,128)(2,1)S(1)}, u32[]{:S(2)}, u32[]{:S(2)}) collective-permute-start(bf16[2,128,1024]{2,1,0:T(8,128)(2,1)S(1)} %join_memory.1.refs_1_.refs_0_), channel_id=1, source_target_pairs={{0,2},{1,3},{2,0},{3,1},{4,6},{5,7},{6,4},{7,5},{8,10},{9,11},{10,... | collective-permute-start | bytes 1572872 | tf_op jit(solution)/shard_map/ppermute | solution.py:55
  15.2 26.1 %collective-permute-start.2 = (bf16[2,128,1024]{2,1,0:T(8,128)(2,1)S(1)}, bf16[2,128,1024]{2,1,0:T(8,128)(2,1)S(1)}, u32[]{:S(2)}, u32[]{:S(2)}) collective-permute-start(bf16[2,128,1024]{2,1,0:T(8,128)(2,1)S(1)} %join_memory.1.refs_1_.refs_0_), channel_id=1, source_target_pairs={{0,1},{1,2},{2,3},{3,0},{4,5},{5,6},{6,7},{7,4},{8,9},{9,10},{10,1... | collective-permute-start | bytes 1572872 | tf_op jit(solution)/shard_map/ppermute | solution.py:55
  27.6 22.2 %collective-permute-start.7 = (bf16[2,512,128]{2,1,0:T(8,128)(2,1)S(1)}, bf16[2,512,128]{2,1,0:T(8,128)(2,1)S(1)}, u32[]{:S(2)}, u32[]{:S(2)}) collective-permute-start(bf16[2,512,128]{2,1,0:T(8,128)(2,1)S(1)} %get-tuple-element.52), channel_id=1, source_target_pairs={{0,1},{1,2},{2,3},{3,0},{4,5},{5,6},{6,7},{7,4},{8,9},{9,10},{10,1... | collective-permute-start | bytes 786440 | tf_op jit(solution)/shard_map/ppermute | solution.py:55
  37.2 12.6 %collective-permute-start.8 = (bf16[2,512,128]{2,1,0:T(8,128)(2,1)S(1)}, bf16[2,512,128]{2,1,0:T(8,128)(2,1)S(1)}, u32[]{:S(2)}, u32[]{:S(2)}) collective-permute-start(bf16[2,512,128]{2,1,0:T(8,128)(2,1)S(1)} %get-tuple-element.53), channel_id=1, source_target_pairs={{0,2},{1,3},{2,0},{3,1},{4,6},{5,7},{6,4},{7,5},{8,10},{9,11},{10,... | collective-permute-start | bytes 786440 | tf_op jit(solution)/shard_map/ppermute | solution.py:55
  38.3 11.5 %collective-permute-start.9 = (bf16[2,512,128]{2,1,0:T(8,128)(2,1)S(1)}, bf16[2,512,128]{2,1,0:T(8,128)(2,1)S(1)}, u32[]{:S(2)}, u32[]{:S(2)}) collective-permute-start(bf16[2,512,128]{2,1,0:T(8,128)(2,1)S(1)} %get-tuple-element.54), channel_id=1, source_target_pairs={{0,3},{1,0},{2,1},{3,2},{4,7},{5,4},{6,5},{7,6},{8,11},{9,8},{10,9... | collective-permute-start | bytes 786440 | tf_op jit(solution)/shard_map/ppermute | solution.py:55
  41.2 8.6 %collective-permute-start.10 = (bf16[2,512,128]{2,1,0:T(8,128)(2,1)S(1)}, bf16[2,512,128]{2,1,0:T(8,128)(2,1)S(1)}, u32[]{:S(2)}, u32[]{:S(2)}) collective-permute-start(bf16[2,512,128]{2,1,0:T(8,128)(2,1)S(1)} %get-tuple-element.51.refs_0_), channel_id=1, source_target_pairs={{0,4},{1,5},{2,6},{3,7},{4,0},{5,1},{6,2},{7,3},{8,12},{9,13},{10,... | collective-permute-start | bytes 786440 | tf_op jit(solution)/shard_map/ppermute | solution.py:55
  50.7 27.9 %collective-permute-start.11 = (bf16[3,2,512,128]{3,2,1,0:T(8,128)(2,1)S(1)}, bf16[3,2,512,128]{3,2,1,0:T(8,128)(2,1)S(1)}, u32[]{:S(2)}, u32[]{:S(2)}) collective-permute-start(bf16[3,2,512,128]{3,2,1,0:T(8,128)(2,1)S(1)} %stack_hidden.1), channel_id=1, source_target_pairs={{0,4},{1,5},{2,6},{3,7},{4,0},{5,1},{6,2},{7,3},{8,12},{9,13},{10,... | collective-permute-start | bytes 2359304 | tf_op jit(solution)/shard_map/ppermute | solution.py:55
  51.9 20.7 %collective-permute-start.14 = (bf16[256,1024]{1,0:T(8,128)(2,1)S(1)}, bf16[256,1024]{1,0:T(8,128)(2,1)S(1)}, u32[]{:S(2)}, u32[]{:S(2)}) collective-permute-start(bf16[256,1024]{1,0:T(8,128)(2,1)S(1)} %get-tuple-element.42.refs_3_.refs_6_.gq_ref), channel_id=1, source_target_pairs={{0,3},{1,0},{2,1},{3,2},{4,7},{5,4},{6,5},{7,6},{8,11},{9,8},{10,9... | collective-permute-start | bytes 1572872 | tf_op jit(solution)/shard_map/ppermute | solution.py:55
  51.9 20.7 %collective-permute-start.13 = (bf16[256,1024]{1,0:T(8,128)(2,1)S(1)}, bf16[256,1024]{1,0:T(8,128)(2,1)S(1)}, u32[]{:S(2)}, u32[]{:S(2)}) collective-permute-start(bf16[256,1024]{1,0:T(8,128)(2,1)S(1)} %get-tuple-element.42.refs_3_.refs_6_.gq_ref), channel_id=1, source_target_pairs={{0,2},{1,3},{2,0},{3,1},{4,6},{5,7},{6,4},{7,5},{8,10},{9,11},{10,... | collective-permute-start | bytes 1572872 | tf_op jit(solution)/shard_map/ppermute | solution.py:55
  53.3 25.2 %collective-permute-start.12 = (bf16[256,1024]{1,0:T(8,128)(2,1)S(1)}, bf16[256,1024]{1,0:T(8,128)(2,1)S(1)}, u32[]{:S(2)}, u32[]{:S(2)}) collective-permute-start(bf16[256,1024]{1,0:T(8,128)(2,1)S(1)} %get-tuple-element.42.refs_3_.refs_6_.gq_ref), channel_id=1, source_target_pairs={{0,1},{1,2},{2,3},{3,0},{4,5},{5,6},{6,7},{7,4},{8,9},{9,10},{10,1... | collective-permute-start | bytes 1572872 | tf_op jit(solution)/shard_map/ppermute | solution.py:55
  53.4 19.2 %collective-permute-start.5 = (bf16[128,1024]{1,0:T(8,128)(2,1)S(1)}, bf16[128,1024]{1,0:T(8,128)(2,1)S(1)}, u32[]{:S(2)}, u32[]{:S(2)}) collective-permute-start(bf16[128,1024]{1,0:T(8,128)(2,1)S(1)} %get-tuple-element.44), channel_id=1, source_target_pairs={{0,4},{1,5},{2,6},{3,7},{4,0},{5,1},{6,2},{7,3},{8,12},{9,13},{10,... | collective-permute-start | bytes 786440 | tf_op jit(solution)/shard_map/ppermute | solution.py:55
  80.4 2.9 %collective-permute-start.22 = (bf16[512,1024]{1,0:T(8,128)(2,1)S(1)}, bf16[512,1024]{1,0:T(8,128)(2,1)S(1)}, u32[]{:S(2)}, u32[]{:S(2)}) collective-permute-start(bf16[512,1024]{1,0:T(8,128)(2,1)S(1)} %get-tuple-element.73.refs_10_), channel_id=1, source_target_pairs={{0,8},{1,9},{2,10},{3,11},{4,12},{5,13},{6,14},{7,15},{8,0},{9,1},... | collective-permute-start | bytes 3145736 | tf_op jit(solution)/shard_map/ppermute | solution.py:55
  84.5 43.7 %all-to-all-start = ((bf16[32,16,1024]{2,1,0:T(8,128)(2,1)}), bf16[32,16,1024]{2,1,0:T(8,128)(2,1)S(1)}, u32[]{:S(2)}, u32[]{:S(2)}) async-start(bf16[32,16,1024]{2,1,0:T(8,128)(2,1)} %bitcast.4), calls=%async_computation | async-start | bytes 2097152 | tf_op jit(solution)/shard_map/all_to_all | solution.py:441
  95.4 7.5 %collective-permute-start.15 = (bf16[128,1024]{1,0:T(8,128)(2,1)}, bf16[128,1024]{1,0:T(8,128)(2,1)S(1)}, u32[]{:S(2)}, u32[]{:S(2)}) collective-permute-start(bf16[128,1024]{1,0:T(8,128)(2,1)} %copy-done.6), channel_id=1, source_target_pairs={{0,3},{1,0},{2,1},{3,2},{4,7},{5,4},{6,5},{7,6},{8,11},{9,8},{10,9... | collective-permute-start | bytes 786440 | tf_op jit(solution)/shard_map/ppermute | solution.py:55
  96.4 8.6 %collective-permute-start.16 = (bf16[128,1024]{1,0:T(8,128)(2,1)}, bf16[128,1024]{1,0:T(8,128)(2,1)S(1)}, u32[]{:S(2)}, u32[]{:S(2)}) collective-permute-start(bf16[128,1024]{1,0:T(8,128)(2,1)} %copy-done.7), channel_id=1, source_target_pairs={{0,2},{1,3},{2,0},{3,1},{4,6},{5,7},{6,4},{7,5},{8,10},{9,11},{10,... | collective-permute-start | bytes 786440 | tf_op jit(solution)/shard_map/ppermute | solution.py:55
  97.4 15.8 %collective-permute-start.17 = (bf16[128,1024]{1,0:T(8,128)(2,1)}, bf16[128,1024]{1,0:T(8,128)(2,1)S(1)}, u32[]{:S(2)}, u32[]{:S(2)}) collective-permute-start(bf16[128,1024]{1,0:T(8,128)(2,1)} %copy-done.8), channel_id=1, source_target_pairs={{0,1},{1,2},{2,3},{3,0},{4,5},{5,6},{6,7},{7,4},{8,9},{9,10},{10,1... | collective-permute-start | bytes 786440 | tf_op jit(solution)/shard_map/ppermute | solution.py:55
  97.8 22.0 %collective-permute-start.6 = (bf16[256,1024]{1,0:T(8,128)(2,1)}, bf16[256,1024]{1,0:T(8,128)(2,1)S(1)}, u32[]{:S(2)}, u32[]{:S(2)}) collective-permute-start(bf16[256,1024]{1,0:T(8,128)(2,1)} %copy-done.13), channel_id=1, source_target_pairs={{0,4},{1,5},{2,6},{3,7},{4,0},{5,1},{6,2},{7,3},{8,12},{9,13},{10,... | collective-permute-start | bytes 1572872 | tf_op jit(solution)/shard_map/ppermute | solution.py:55
  99.0 20.8 %collective-permute-start.19 = (bf16[128,1024]{1,0:T(8,128)(2,1)S(1)}, bf16[128,1024]{1,0:T(8,128)(2,1)S(1)}, u32[]{:S(2)}, u32[]{:S(2)}) collective-permute-start(bf16[128,1024]{1,0:T(8,128)(2,1)S(1)} %get-tuple-element.65), channel_id=1, source_target_pairs={{0,3},{1,0},{2,1},{3,2},{4,7},{5,4},{6,5},{7,6},{8,11},{9,8},{10,9... | collective-permute-start | bytes 786440 | tf_op jit(solution)/shard_map/ppermute | solution.py:55
  102.9 17.0 %collective-permute-start.20 = (bf16[128,1024]{1,0:T(8,128)(2,1)S(1)}, bf16[128,1024]{1,0:T(8,128)(2,1)S(1)}, u32[]{:S(2)}, u32[]{:S(2)}) collective-permute-start(bf16[128,1024]{1,0:T(8,128)(2,1)S(1)} %get-tuple-element.66), channel_id=1, source_target_pairs={{0,2},{1,3},{2,0},{3,1},{4,6},{5,7},{6,4},{7,5},{8,10},{9,11},{10,... | collective-permute-start | bytes 786440 | tf_op jit(solution)/shard_map/ppermute | solution.py:55
  105.0 18.1 %collective-permute-start.21 = (bf16[128,1024]{1,0:T(8,128)(2,1)S(1)}, bf16[128,1024]{1,0:T(8,128)(2,1)S(1)}, u32[]{:S(2)}, u32[]{:S(2)}) collective-permute-start(bf16[128,1024]{1,0:T(8,128)(2,1)S(1)} %get-tuple-element.67), channel_id=1, source_target_pairs={{0,1},{1,2},{2,3},{3,0},{4,5},{5,6},{6,7},{7,4},{8,9},{9,10},{10,1... | collective-permute-start | bytes 786440 | tf_op jit(solution)/shard_map/ppermute | solution.py:55
  113.4 12.8 %collective-permute-start.18 = (bf16[128,1024]{1,0:T(8,128)(2,1)S(1)}, bf16[128,1024]{1,0:T(8,128)(2,1)S(1)}, u32[]{:S(2)}, u32[]{:S(2)}) collective-permute-start(bf16[128,1024]{1,0:T(8,128)(2,1)S(1)} %memory_sum.1), channel_id=1, source_target_pairs={{0,4},{1,5},{2,6},{3,7},{4,0},{5,1},{6,2},{7,3},{8,12},{9,13},{10,... | collective-permute-start | bytes 786440 | tf_op jit(solution)/shard_map/ppermute | solution.py:55
  (14 other events, 95.2 us)
